TPU v7x, 32 devices: a whole 2x2x4 slice. The times are simulated.
32 devices in a mesh: groups: 2 (over x), replica: 2 (over core), tensor: 8 (over z, y).
Axes of the slice: x: 2, y: 2, z: 4, core: 2. Of those that a mesh axis runs over, the one named last changes fastest.
Arguments:
- activations: bfloat16 [2048, 8192], P(('groups', 'replica'), 'tensor'), parts along dimension 0, may hold values from -800 to 800
- input_norm_scale: float32 [8192], replicated, may hold values from 0.1 to 1.9
- query_weight: bfloat16 [8192, 8192], P(None, 'tensor'), may hold values from -2 to 2
- key_value_weight: bfloat16 [8192, 2048], P('tensor'), may hold values from -1 to 1
- adapter_down_weight: bfloat16 [8192, 4096], P('tensor'), may hold values from -0.0625 to 0.0625
- adapter_up_weight: bfloat16 [4096, 8192], P(None, 'tensor'), may hold values from -1.5 to 1.5
- adapter_index_pairs: int32 [2048, 2], P(('groups', 'replica')), parts along dimension 0, may hold values from 0 to 255, all different within a row
- adapter_mix_weights: float32 [2048, 2], P(('groups', 'replica')), parts along dimension 0, may hold values from 0.25 to 1
- prompt_live_length: int32 [8], P(('groups', 'replica')), parts along dimension 0, may hold values from 64 to 256, as said below
Outputs:
- context: bfloat16 [2048, 8192], P(('groups', 'replica'), 'tensor'), parts along dimension 0
There are 2 independent parts, one for each index of `groups`. A program takes and returns all parts, laid end to end along the dimension named above; an argument that names none is the same for every part. Nothing has to cross between parts.
Inputs may be any that keep to these rules, and one draw needn't show every extreme that they name: `adapter_index_pairs`: the two adapters of a token differ. `prompt_live_length`: some prompt of every draw is live in all 256 positions.
All inputs are finite; a program needn't handle non-finite values.
Results may differ from a plain program's by a relative error of at most 0.0089.
Values may be sent and summed in bfloat16 or wider, within the bound.
No kernel may reach another device: no remote copies, remote signals or barrier semaphores. Data moves between devices by JAX's collectives and lax.ppermute only.
A program may use at most 192 MiB of HBM per device.

v0:
```python
import math

import jax
import jax.numpy as jnp
from jax import lax
from jax.sharding import PartitionSpec as P

QUERY_HEADS = 64
KV_HEADS = 8
HEAD_WIDTH = 128
ADAPTER_COUNT = 256
ADAPTER_RANK = 16
SLOT = 256


EPS = 1e-05
ROPE_BASE = 500000.0


def rotate_pairs(values, positions, freq_index, active):
    row_count = values.shape[0]
    pairs = values.reshape(row_count, -1, 2)
    inverse = jnp.power(jnp.float32(ROPE_BASE), -2.0 * freq_index.astype(jnp.float32) / HEAD_WIDTH)
    angles = positions.astype(jnp.float32)[:, None] * inverse[None, :]
    cosine = jnp.where(active[None, :], jnp.cos(angles), 1.0)
    sines = jnp.where(active[None, :], jnp.sin(angles), 0.0)
    first = pairs[:, :, 0]
    second = pairs[:, :, 1]
    turned = jnp.stack([first * cosine - second * sines, first * sines + second * cosine], axis=2)
    return turned.reshape(row_count, -1)


def attend(queries, keyvals, lengths):
    seqs = lengths.shape[0]
    query_blocks = queries.reshape(seqs, SLOT, -1, HEAD_WIDTH)
    keyval_blocks = keyvals.reshape(seqs, SLOT, 2, HEAD_WIDTH)
    key_rows = keyval_blocks[:, :, 0, :]
    value_rows = keyval_blocks[:, :, 1, :]
    scores = jnp.einsum(
        "pshd,pud->phsu", query_blocks, key_rows, preferred_element_type=jnp.float32
    ) / math.sqrt(HEAD_WIDTH)
    row_index = jnp.arange(SLOT)[:, None]
    col_index = jnp.arange(SLOT)[None, :]
    allowed = (col_index <= row_index)[None, None, :, :] & (
        col_index[None, None, :, :] < lengths[:, None, None, None]
    )
    masked = jnp.where(allowed, scores, -1e30)
    row_top = jnp.max(masked, axis=3, keepdims=True)
    weights = jnp.where(allowed, jnp.exp(masked - row_top), 0.0)
    totals = jnp.sum(weights, axis=3, keepdims=True)
    mixed = jnp.einsum(
        "phsu,pud->pshd",
        weights.astype(jnp.bfloat16),
        value_rows,
        preferred_element_type=jnp.float32,
    )
    mixed = mixed / jnp.transpose(totals, (0, 2, 1, 3))
    live_rows = (jnp.arange(SLOT)[None, :] < lengths[:, None])[:, :, None, None]
    return jnp.where(live_rows, mixed, 0.0).astype(jnp.bfloat16).reshape(seqs * SLOT, -1)


def shards(
    activations,
    input_norm_scale,
    query_weight,
    key_value_weight,
    adapter_down_weight,
    adapter_up_weight,
    adapter_index_pairs,
    adapter_mix_weights,
    prompt_live_length,
):
    token_count = activations.shape[0]
    local_width = activations.shape[1]
    shard_index = lax.axis_index("tensor")
    gathered = lax.all_gather(activations, "tensor", axis=1, tiled=True)
    gathered32 = gathered.astype(jnp.float32)
    inverse = lax.rsqrt(jnp.mean(gathered32 * gathered32, axis=1, keepdims=True) + EPS)
    normalized_input = (gathered32 * inverse * input_norm_scale[None, :]).astype(jnp.bfloat16)
    normalized_local_input = lax.dynamic_slice_in_dim(
        normalized_input, shard_index * local_width, local_width, 1
    )
    q_base = jnp.dot(normalized_input, query_weight, preferred_element_type=jnp.float32)
    kv_part = jnp.dot(normalized_local_input, key_value_weight, preferred_element_type=jnp.float32)
    reduced_rank_rows = jnp.dot(
        normalized_local_input, adapter_down_weight, preferred_element_type=jnp.float32
    ).reshape(token_count, ADAPTER_COUNT, ADAPTER_RANK)
    onehot = (
        adapter_index_pairs[:, :, None] == jnp.arange(ADAPTER_COUNT, dtype=jnp.int32)[None, None, :]
    ).astype(jnp.float32)
    low_part = jnp.einsum(
        "tka,tar->tkr", onehot, reduced_rank_rows, precision=lax.Precision.HIGHEST
    )
    heads_local = query_weight.shape[1] // HEAD_WIDTH
    kv_group = shard_index * heads_local // (QUERY_HEADS // KV_HEADS)
    kv_raw, low = lax.psum((kv_part, low_part), "tensor")
    selected = lax.dynamic_slice_in_dim(kv_raw, kv_group * 2 * HEAD_WIDTH, 2 * HEAD_WIDTH, 1)
    weighted = low * adapter_mix_weights[:, :, None]
    mixing_factors = jnp.einsum("tka,tkr->tar", onehot, weighted, precision=lax.Precision.HIGHEST)
    mixing_factors = mixing_factors.reshape(token_count, ADAPTER_COUNT * ADAPTER_RANK).astype(
        jnp.bfloat16
    )
    query_update = jnp.dot(mixing_factors, adapter_up_weight, preferred_element_type=jnp.float32)
    positions = jnp.arange(token_count) % SLOT
    query_pairs = jnp.arange(query_weight.shape[1] // 2)
    queries = rotate_pairs(
        q_base + query_update, positions, 2 * query_pairs % HEAD_WIDTH // 2, query_pairs >= 0
    ).astype(jnp.bfloat16)
    in_head = 2 * jnp.arange(HEAD_WIDTH)
    keyvals = rotate_pairs(
        selected, positions, in_head % HEAD_WIDTH // 2, in_head < HEAD_WIDTH
    ).astype(jnp.bfloat16)
    return attend(queries, keyvals, prompt_live_length)


def solution(mesh):
    placed = (
        P(("groups", "replica"), "tensor"),
        P(),
        P(None, "tensor"),
        P("tensor", None),
        P("tensor", None),
        P(None, "tensor"),
        P(("groups", "replica"), None),
        P(("groups", "replica"), None),
        P(("groups", "replica")),
    )
    return jax.shard_map(
        shards,
        mesh=mesh,
        in_specs=placed,
        out_specs=P(("groups", "replica"), "tensor"),
        check_vma=False,
    )
```

profile of v0, /device:TPU:0, one launch (start us, length us, event | category | flops | bytes accessed | tf_op | source)
XLA Modules:
  0.0 433.8 jit_solution(16041056426872827651)
XLA Ops:
  7.3 0.8 copy.28
  8.2 129.0 %all-gather.2.cloned.1.call-done = bf16[512,8192]{1,0:T(8,128)(2,1)} async-done(((bf16[512,1024]{1,0:T(8,128)(2,1)}), bf16[512,8192]{1,0:T(8,128)(2,1)}) %all-gather.2.cloned.1.call-update) | async-done | bytes 8388624 | tf_op jit(solution)/shard_map/all_gather | solution.py:76
  137.2 5.1 %fusion.1 = f32[512]{0:T(512)S(1)} fusion(bf16[512,8192]{1,0:T(8,128)(2,1)} %all-gather.2.cloned.1.call-done), kind=kLoop, calls=%fused_computation.3 | loop fusion | flops 12582400 | bytes 8390656 | tf_op jit(solution)/shard_map/reduce_sum | solution.py:78
  142.3 9.8 %fusion.3 = bf16[512,8192]{1,0:T(8,128)(2,1)} fusion(bf16[512,8192]{1,0:T(8,128)(2,1)} %all-gather.2.cloned.1.call-done, f32[8192]{0:T(1024)S(1)} %copy-done.1, f32[512]{0:T(512)S(1)} %add_rsqrt_fusion), kind=kLoop, calls=%fused_computation.5 | loop fusion | flops 16777216 | bytes 16812032 | tf_op jit(solution)/shard_map/convert_element_type | solution.py:79
  152.2 11.5 %fusion.25 = f32[512,4096]{0,1:T(8,128)} fusion(bf16[1024,4096]{1,0:T(8,128)(2,1)} %param.13, bf16[512,8192]{1,0:T(8,128)(2,1)} %fusion.3, s32[]{:T(128)S(6)} %select_n.140), kind=kOutput, calls=%fused_computation.35 | convolution fusion | flops 4294967296 | bytes 17825796 | tf_op jit(solution)/shard_map/dot_general | solution.py:85
  163.7 10.4 %copy.30 = f32[512,256,16]{1,2,0:T(8,128)} copy(f32[512,256,16]{0,2,1:T(8,128)} %bitcast.57) | data formatting | bytes 16777216 | tf_op jit(solution)/shard_map/reshape | solution.py:87
  174.1 6.9 %fusion.27 = f32[512,2048]{1,0:T(8,128)} fusion(bf16[1024,2048]{1,0:T(8,128)(2,1)} %param.12, bf16[512,8192]{1,0:T(8,128)(2,1)} %fusion.3, s32[]{:T(128)S(6)} %select_n.140), kind=kOutput, calls=%fused_computation.37 | convolution fusion | flops 2147483648 | bytes 9437188 | tf_op jit(solution)/shard_map/dot_general | solution.py:84
  181.0 5.3 %fusion.24 = f32[512,2,16]{2,1,0:T(2,128)} fusion(f32[512,256,16]{1,2,0:T(8,128)S(1)} %copy-done, s32[512,2]{1,0:T(8,128)S(1)} %copy.28), kind=kOutput, calls=%fused_computation.34 | convolution fusion | flops 50593792 | bytes 8458240 | tf_op jit(solution)/shard_map/tka,tar->tkr/dot_general | solution.py:91
  187.5 167.2 %all-reduce.3.cloned.1.call-done = (f32[512,2,16]{2,1,0:T(2,128)}, f32[512,2048]{1,0:T(8,128)}) async-done(((f32[512,2,16]{2,1,0:T(2,128)}, f32[512,2048]{1,0:T(8,128)}), (f32[512,2,16]{2,1,0:T(2,128)}, f32[512,2048]{1,0:T(8,128)})) %all-reduce.3.cloned.1.call-update) | async-done | bytes 4259856 | tf_op jit(solution)/shard_map/psum | solution.py:96
  354.7 1.1 constant_dynamic-slice_fusion
  356.3 8.9 %subtract_convert_fusion = (bf16[512,128,1]{0,2,1:T(2,128)(2,1)S(1)}, bf16[512,128,1]{0,2,1:T(2,128)(2,1)S(1)}) fusion(f32[512,128,2]{0,2,1:T(2,128)S(1)} %reshape.421, f32[128]{0:T(128)S(1)} %multiply_power_fusion, f32[512]{0:T(512)S(1)} %fusion.34, pred[128]{0:T(512)(128)(4,1)S(1)} %fusion.45), kind=kLoop, calls=%fused_computation.50 | loop fusion | flops 720896 | bytes 789120 | tf_op jit(solution)/shard_map/convert.2
  366.4 7.3 %convolution_convert_fusion = bf16[512,256,16]{1,2,0:T(8,128)(2,1)} fusion(f32[512,2,16]{2,1,0:T(2,128)S(1)} %copy-done.3, s32[512,2]{1,0:T(8,128)S(1)} %copy.28, f32[512,2]{1,0:T(8,128)S(1)} %copy.31), kind=kOutput, calls=%fused_computation.9 | convolution fusion | flops 52707328 | bytes 4268032 | tf_op jit(solution)/shard_map/tka,tkr->tar/dot_general | solution.py:99
  373.7 8.6 %copy.32 = bf16[512,256,16]{0,2,1:T(8,128)(2,1)} copy(bf16[512,256,16]{1,2,0:T(8,128)(2,1)} %convolution_convert_fusion) | data formatting | bytes 8388608 | tf_op jit(solution)/shard_map/convert_element_type | solution.py:100
  382.3 8.2 %fusion.53 = f32[512,1024]{1,0:T(8,128)S(1)} fusion(bf16[512,4096]{0,1:T(8,128)(2,1)} %bitcast.58, bf16[4096,1024]{1,0:T(8,128)(2,1)} %param.14), kind=kOutput, calls=%fused_computation.95 | convolution fusion | flops 4294967296 | bytes 14680064 | tf_op jit(solution)/shard_map/dot_general | solution.py:103
  390.5 14.7 %convolution_add_fusion = f32[512,1024]{1,0:T(8,128)S(1)} fusion(f32[512,1024]{1,0:T(8,128)S(1)} %fusion.53, bf16[512,8192]{1,0:T(8,128)(2,1)} %fusion.3, bf16[8192,1024]{1,0:T(8,128)(2,1)} %param.11), kind=kOutput, calls=%fused_computation.18 | convolution fusion | flops 8590458880 | bytes 29360128 | tf_op jit(solution)/shard_map/dot_general | solution.py:83
  405.2 1.9 copy.33
  407.1 2.5 reshape.423
  409.6 2.6 fusion.50
  412.2 2.3 copy.46
  414.5 1.3 copy.47
  415.8 4.6 %fusion.19 = (bf16[512,512,1]{1,0,2:T(8,128)(2,1)S(1)}, bf16[512,512,1]{1,0,2:T(8,128)(2,1)S(1)}) fusion(f32[512,512,1]{1,0,2:T(8,128)S(1)} %copy.47, f32[512,512,1]{1,0,2:T(8,128)S(1)} %copy.46, f32[512]{0:T(512)S(1)} %fusion.39, f32[512]{0:T(512)S(1)} %fusion.34), kind=kLoop, calls=%fused_computation.26 | loop fusion | flops 2359296 | bytes 3149824 | tf_op jit(solution)/shard_map/convert
  420.6 1.0 copy.36
  423.0 1.5 fusion.52
  425.8 1.2 copy.54
  (34 shorter events, 6.2 us)
Async XLA Ops:
  6.5 130.7 %all-gather.2.cloned.1.call-start = ((), (), s32[]{:S(2)}) async-start(), calls=%async_computation | async-start | bytes 9437184 | tf_op jit(solution)/shard_map/all_gather | solution.py:76
  7.3 347.4 %all-reduce.3.cloned.1.call-start = ((), (), s32[]{:S(2)}) async-start(), calls=%async_computation.1 | async-start | bytes 9437184 | tf_op jit(solution)/shard_map/psum | solution.py:96
  8.1 134.2 %copy-start.1 = (f32[8192]{0:T(1024)S(1)}, f32[8192]{0:T(1024)}, u32[]{:S(2)}) copy-start(f32[8192]{0:T(1024)} %param.10) | copy-start | bytes 98308
  174.1 6.9 %copy-start = (f32[512,256,16]{1,2,0:T(8,128)S(1)}, f32[512,256,16]{1,2,0:T(8,128)}, u32[]{:S(2)}) copy-start(f32[512,256,16]{1,2,0:T(8,128)} %copy.30) | copy-start | bytes 25165828
  186.3 0.7 copy-start.2
  186.3 0.9 copy-start.4
  354.7 11.7 %copy-start.3 = (f32[512,2,16]{2,1,0:T(2,128)S(1)}, f32[512,2,16]{2,1,0:T(2,128)}, u32[]{:S(2)}) copy-start(f32[512,2,16]{2,1,0:T(2,128)} %get-tuple-element.5) | copy-start | bytes 196612
Sparse Core Ops, SparseCore 0:
  9.5 127.6 all-gather.1
  186.5 168.1 all-reduce.2
where the time goes:
time: 435 us; the launch traced here: 434 us
  waiting for transfers between devices  297 us (68%)
  matrix products  55.1 us (13%)
  local copies, waits for them, and re-layouts  37.1 us (9%)
  other arithmetic  31 us (7%)
  between operations  13.7 us (3%)
    psum x1, waiting for transfers between devices, shards(): kv_raw, low = lax.psum((kv_part, low_part), 'tensor')  167 us
    all_gather x1, waiting for transfers between devices, shards(): gathered = lax.all_gather(activations, 'tensor', axis=1, tiled=True)  129 us
    dot_general x1, matrix products, shards(): jnp.dot(normalized_input, query_weight, preferred_element_type=jnp.float32)  14.7 us
    another operation x2, other arithmetic  13.5 us
    dot_general x1, matrix products, shards(): jnp.dot(normalized_local_input, adapter_down_weight, preferred_element_ty...  11.5 us
    reshape x1, local copies, waits for them, and re-layouts, shards(): reduced_rank_rows = jnp.dot(normalized_local_input, adapter_down_weight,...  10.4 us
    convert_element_type x1, other arithmetic, shards(): (gathered32 * inverse * input_norm_scale[None, :]).astype(jnp.bfloat16)  9.85 us
  transfers between devices with their start and end apart: 2, of which 2 were waited for; matrix products, arithmetic and copies ran while one was open for 0% of the time, Pallas kernels for 0%

commit v1 on v0

v1 whole, which is shorter than its diff:
```python
import functools
import math

import jax
import jax.numpy as jnp
import numpy as np
from jax import lax
from jax.experimental import pallas as pl
from jax.experimental.pallas import tpu as pltpu
from jax.sharding import PartitionSpec as P

QUERY_HEADS = 64
KV_HEADS = 8
HEAD_WIDTH = 128
ADAPTER_RANK = 16
SLOT = 256
LANES = 128
LOW_ROWS = 40

EPS = 1e-05
ROPE_BASE = 500000.0

SIDE_SQUARES = 0
SIDE_MIX = 1
SIDE_INDEX = 3

VMEM_LIMIT = 56 * 1024 * 1024
F32 = jnp.float32
BF16 = jnp.bfloat16


def call(kernel, out_shape, flops, moved, **kwargs):
    return pl.pallas_call(
        kernel,
        out_shape=out_shape,
        compiler_params=pltpu.CompilerParams(vmem_limit_bytes=VMEM_LIMIT),
        cost_estimate=pl.CostEstimate(flops=flops, bytes_accessed=moved, transcendentals=0),
        **kwargs,
    )


def whole(shape):
    return pl.BlockSpec(shape, lambda *_: (0,) * len(shape))


def shape_of(shape, dtype):
    return jax.ShapeDtypeStruct(shape, dtype)


def scale_kernel(pack_ref, x_ref, scale_ref, xs_ref):
    start = pl.multiple_of(pack_ref[0], 16)
    xs_ref[...] = (x_ref[...].astype(F32) * scale_ref[...]).astype(BF16)
    second = (x_ref[SLOT:, :].astype(F32) * scale_ref[...]).astype(BF16)
    xs_ref[pl.ds(start, SLOT), :] = second


def scale_rows(pack, x, scale):
    rows, width = x.shape
    return call(
        scale_kernel,
        shape_of((rows, width), BF16),
        2 * rows * width,
        4 * rows * width,
        grid_spec=pltpu.PrefetchScalarGridSpec(
            num_scalar_prefetch=1,
            grid=(1,),
            in_specs=[whole((rows, width)), whole((1, width))],
            out_specs=whole((rows, width)),
        ),
    )(pack, x, scale)


def side_kernel(pack_ref, x_ref, index_ref, mix_ref, side_ref):
    start = pl.multiple_of(pack_ref[0], 16)
    rows = x_ref.shape[0]
    x = x_ref[...].astype(F32)
    squares = jnp.sum(x * x, axis=1, keepdims=True)
    lane = lax.broadcasted_iota(jnp.int32, (rows, LANES), 1)
    side = jnp.where(lane == SIDE_SQUARES, squares, 0.0)
    for k in range(2):
        side = jnp.where(lane == SIDE_MIX + k, mix_ref[:, k : k + 1], side)
        side = jnp.where(lane == SIDE_INDEX + k, index_ref[:, k : k + 1].astype(F32), side)
    side_ref[...] = side
    side_ref[pl.ds(start, SLOT), :] = side[SLOT:]


def side_rows(pack, x, index, mix):
    rows, width = x.shape
    return call(
        side_kernel,
        shape_of((rows, LANES), F32),
        2 * rows * width,
        2 * rows * width,
        grid_spec=pltpu.PrefetchScalarGridSpec(
            num_scalar_prefetch=1,
            grid=(1,),
            in_specs=[whole((rows, width)), whole((rows, 2)), whole((rows, 2))],
            out_specs=whole((rows, LANES)),
        ),
    )(pack, x, index, mix)


def kv_kernel(xs_ref, w_ref, out_ref):
    out_ref[0] = jnp.dot(xs_ref[...], w_ref[...], preferred_element_type=F32).astype(BF16)


def kv_partials(xs, weight, rows):
    width = xs.shape[1]
    return call(
        kv_kernel,
        shape_of((KV_HEADS, rows, 2 * HEAD_WIDTH), BF16),
        2 * rows * width * weight.shape[1],
        2 * width * weight.shape[1] + 2 * rows * (width + weight.shape[1]),
        grid=(KV_HEADS,),
        in_specs=[
            whole((rows, width)),
            pl.BlockSpec((width, 2 * HEAD_WIDTH), lambda g: (0, g)),
        ],
        out_specs=pl.BlockSpec((1, rows, 2 * HEAD_WIDTH), lambda g: (g, 0, 0)),
    )(xs, weight)


def adapter_of(first, rows):
    lane = lax.broadcasted_iota(jnp.int32, (rows, LANES), 1)
    return ((first + lane) // ADAPTER_RANK).astype(F32)


def low_kernel(rows, xs_ref, w_ref, side_ref, out_ref, acc_ref):
    step = pl.program_id(0)
    tile = w_ref.shape[1]

    @pl.when(step == 0)
    def _():
        acc_ref[...] = jnp.zeros_like(acc_ref)

    product = jnp.dot(xs_ref[...], w_ref[...], preferred_element_type=F32)
    for k in range(2):
        wanted = side_ref[:rows, SIDE_INDEX + k : SIDE_INDEX + k + 1]
        total = acc_ref[k, :rows, :]
        for s in range(tile // LANES):
            adapter = adapter_of(step * tile + s * LANES, 8)[:1]
            total += jnp.where(adapter == wanted, product[:, s * LANES : (s + 1) * LANES], 0.0)
        acc_ref[k, :rows, :] = total

    @pl.when(step == pl.num_programs(0) - 1)
    def _():
        lane = lax.broadcasted_iota(jnp.int32, acc_ref.shape[1:], 1)
        folded = []
        for k in range(2):
            value = acc_ref[k]
            shift = ADAPTER_RANK
            while shift < LANES:
                value = value + pltpu.roll(value, shift, 1)
                shift *= 2
            folded.append(value)
        packed = jnp.where(lane < ADAPTER_RANK, folded[0], folded[1])
        packed = jnp.where(lane < 2 * ADAPTER_RANK, packed, 0.0)
        squares = side_ref[:, SIDE_SQUARES : SIDE_SQUARES + 1]
        packed = jnp.where(lane == 2 * ADAPTER_RANK, squares, packed)
        out_ref[...] = packed.T[:LOW_ROWS]


def low_partials(xs, weight, side, rows):
    width, columns = weight.shape
    tile = min(512, columns)
    tokens = side.shape[0]
    return call(
        functools.partial(low_kernel, rows),
        shape_of((LOW_ROWS, tokens), F32),
        2 * rows * width * columns,
        2 * width * columns,
        grid=(columns // tile,),
        in_specs=[
            whole((rows, width)),
            pl.BlockSpec((width, tile), lambda j: (0, j)),
            whole((tokens, LANES)),
        ],
        out_specs=whole((LOW_ROWS, tokens)),
        scratch_shapes=[pltpu.VMEM((2, tokens, LANES), F32)],
    )(xs, weight, side)


def delta_kernel(rows, model_width, low_ref, side_ref, w_ref, out_ref, inv_ref, co_ref):
    step = pl.program_id(0)
    tile = w_ref.shape[0]

    @pl.when(step == 0)
    def _():
        tokens = low_ref.shape[1]
        padding = jnp.zeros((LANES - LOW_ROWS, tokens), F32)
        low = jnp.concatenate([low_ref[...], padding], axis=0).T
        lane = lax.broadcasted_iota(jnp.int32, (tokens, LANES), 1)
        squares = low[:, 2 * ADAPTER_RANK : 2 * ADAPTER_RANK + 1]
        inverse = lax.rsqrt(squares * (1.0 / model_width) + EPS)
        inv_ref[...] = jnp.broadcast_to(inverse, (tokens, LANES))
        for k in range(2):
            value = jnp.where(lane // ADAPTER_RANK == k, low, 0.0)
            shift = ADAPTER_RANK
            while shift < LANES:
                value = value + pltpu.roll(value, shift, 1)
                shift *= 2
            co_ref[k] = value * inverse * side_ref[:, SIDE_MIX + k : SIDE_MIX + k + 1]
        out_ref[...] = jnp.zeros_like(out_ref)

    wanted = [side_ref[:rows, SIDE_INDEX + k : SIDE_INDEX + k + 1] for k in range(2)]
    pieces = []
    for s in range(tile // LANES):
        adapter = adapter_of(step * tile + s * LANES, 8)[:1]
        piece = jnp.where(adapter == wanted[1], co_ref[1, :rows, :], 0.0)
        piece = jnp.where(adapter == wanted[0], co_ref[0, :rows, :], piece)
        pieces.append(piece.astype(BF16))
    coefficients = jnp.concatenate(pieces, axis=1)
    out_ref[...] += jnp.dot(coefficients, w_ref[...], preferred_element_type=F32)


def query_delta(low, side, weight, rows, model_width):
    depth, columns = weight.shape
    tile = min(512, depth)
    tokens = side.shape[0]
    return call(
        functools.partial(delta_kernel, rows, model_width),
        (shape_of((rows, columns), F32), shape_of((tokens, LANES), F32)),
        2 * rows * depth * columns,
        2 * depth * columns + 4 * rows * columns,
        grid=(depth // tile,),
        in_specs=[
            whole((LOW_ROWS, tokens)),
            whole((tokens, LANES)),
            pl.BlockSpec((tile, columns), lambda j: (j, 0)),
        ],
        out_specs=(whole((rows, columns)), whole((tokens, LANES))),
        scratch_shapes=[pltpu.VMEM((2, tokens, LANES), F32)],
    )(low, side, weight)


def query_kernel(counts, has_total, info_ref, *refs):
    refs = list(refs)
    out_ref = refs.pop()
    total_ref = refs.pop(0) if has_total else None
    weights = refs[-len(counts) :]
    blocks = refs[: -len(counts)]
    start = 0
    for piece in range(counts[0]):
        rows = blocks[piece].shape[0]
        value = total_ref[start : start + rows, :] if has_total else None
        for source, w_ref in enumerate(weights):
            block = blocks[source * counts[0] + piece]
            product = jnp.dot(block[...], w_ref[...], preferred_element_type=F32)
            value = product if value is None else value + product
        out_ref[start : start + rows, :] = value
        start += rows


def query_step(info, total, sources, weight, rows):
    width = weight.shape[0] // info.shape[1]
    columns = weight.shape[1]
    tile = min(512, columns)
    slots = [slot for slot, _ in sources]
    blocks = [block for _, pieces in sources for block in pieces]
    counts = [len(pieces) for _, pieces in sources]
    piece_rows = [rows // counts[0]] * counts[0]
    in_specs = []
    operands = []
    aliases = {}
    if total is not None:
        in_specs.append(pl.BlockSpec((rows, tile), lambda j, _: (0, j)))
        operands.append(total)
        aliases = {1: 0}
    for i, block in enumerate(blocks):
        in_specs.append(whole((piece_rows[i % counts[0]], width)))
        operands.append(block)
    for slot in slots:
        in_specs.append(pl.BlockSpec((width, tile), lambda j, info, slot=slot: (info[0, slot], j)))
        operands.append(weight)
    return call(
        functools.partial(query_kernel, counts, total is not None),
        shape_of((rows, columns), F32),
        2 * rows * width * columns * len(slots),
        2 * width * (columns + rows) * len(slots) + 8 * rows * columns,
        grid_spec=pltpu.PrefetchScalarGridSpec(
            num_scalar_prefetch=1,
            grid=(columns // tile,),
            in_specs=in_specs,
            out_specs=pl.BlockSpec((rows, tile), lambda j, _: (0, j)),
        ),
        input_output_aliases=aliases,
    )(info, *operands)


def rotate(values, cosines, sines):
    lane = lax.broadcasted_iota(jnp.int32, values.shape, 1)
    after = pltpu.roll(values, LANES - 1, 1)
    before = pltpu.roll(values, 1, 1)
    other = jnp.where(lane % 2 == 0, after, before)
    return values * cosines + other * sines


def attention_kernel(
    rows, info_ref, pack_ref, total_ref, delta_ref, inv_ref, first_ref, second_ref, w_ref,
    own_ref, cw_ref, ccw_ref, cos_ref, sin_ref, out_ref, query_s, kv_s, key_s, value_s,
):
    half = rows // 2
    starts = [0, pl.multiple_of(pack_ref[0], 16)]
    lengths = [pack_ref[1], pack_ref[2]]
    inverse = inv_ref[:rows, 0:1]
    row = lax.broadcasted_iota(jnp.int32, (SLOT, SLOT), 0)
    col = lax.broadcasted_iota(jnp.int32, (SLOT, SLOT), 1)
    row_narrow = lax.broadcasted_iota(jnp.int32, (SLOT, HEAD_WIDTH), 0)

    @pl.when(pl.program_id(0) == 0)
    def _():
        raw = own_ref[0].astype(F32) + cw_ref[...].astype(F32) + ccw_ref[...].astype(F32)
        kv_s[:rows, :] = raw * inverse
        kv_s[rows:, :] = jnp.zeros((SLOT, 2 * HEAD_WIDTH), F32)
        query_s[rows:, :] = jnp.zeros((SLOT, query_s.shape[1]), F32)
        for i in range(2):
            pair = kv_s[pl.ds(starts[i], SLOT), :]
            key_s[i] = rotate(pair[:, :HEAD_WIDTH], cos_ref[...], sin_ref[...]).astype(BF16)
            value = jnp.where(row_narrow < lengths[i], pair[:, HEAD_WIDTH:], 0.0)
            value_s[i] = value.astype(BF16)

    for piece, ref in enumerate((first_ref, second_ref)):
        span = slice(piece * half, (piece + 1) * half)
        product = jnp.dot(ref[...], w_ref[...], preferred_element_type=F32)
        query_s[span, :] = (total_ref[span, :] + product) * inverse[span] + delta_ref[span, :]

    for i in range(2):
        allowed = (col <= row) & (col < lengths[i])
        for head in range(w_ref.shape[1] // HEAD_WIDTH):
            span = slice(head * HEAD_WIDTH, (head + 1) * HEAD_WIDTH)
            query = query_s[pl.ds(starts[i], SLOT), span]
            query = rotate(query, cos_ref[...], sin_ref[...]).astype(BF16)
            scores = lax.dot_general(
                query, key_s[i], (((1,), (1,)), ((), ())), preferred_element_type=F32
            ) * (1.0 / math.sqrt(HEAD_WIDTH))
            scores = jnp.where(allowed, scores, -1e30)
            top = jnp.max(scores, axis=1, keepdims=True)
            weights = jnp.where(allowed, jnp.exp(scores - top), 0.0)
            totals = jnp.sum(weights, axis=1, keepdims=True)
            mixed = jnp.dot(weights.astype(BF16), value_s[i], preferred_element_type=F32)
            mixed = jnp.where(row_narrow < lengths[i], mixed / totals, 0.0)
            out_ref[i * SLOT : (i + 1) * SLOT, span] = mixed.astype(BF16)


def attention(info, pack, total, delta, inv, last, last_slot, weight, kv, tables, rows, group_slot):
    width = weight.shape[0] // info.shape[1]
    columns = weight.shape[1]
    tile = min(2 * HEAD_WIDTH, columns)
    own, cw, ccw = kv
    tokens = inv.shape[0]
    pair = 2 * HEAD_WIDTH
    return call(
        functools.partial(attention_kernel, rows),
        shape_of((tokens, columns), BF16),
        2 * rows * width * columns + 4 * tokens * SLOT * columns,
        2 * width * (columns + rows) + 8 * rows * columns + 2 * tokens * columns,
        grid_spec=pltpu.PrefetchScalarGridSpec(
            num_scalar_prefetch=2,
            grid=(columns // tile,),
            in_specs=[
                pl.BlockSpec((rows, tile), lambda j, *_: (0, j)),
                pl.BlockSpec((rows, tile), lambda j, *_: (0, j)),
                whole((tokens, LANES)),
                whole((rows // 2, width)),
                whole((rows // 2, width)),
                pl.BlockSpec((width, tile), lambda j, info, _: (info[0, last_slot], j)),
                pl.BlockSpec((1, rows, pair), lambda j, info, _: (info[1, group_slot], 0, 0)),
                whole((rows, pair)),
                whole((rows, pair)),
                whole((SLOT, HEAD_WIDTH)),
                whole((SLOT, HEAD_WIDTH)),
            ],
            out_specs=pl.BlockSpec((tokens, tile), lambda j, *_: (0, j)),
            scratch_shapes=[
                pltpu.VMEM((rows + SLOT, tile), F32),
                pltpu.VMEM((rows + SLOT, pair), F32),
                pltpu.VMEM((2, SLOT, HEAD_WIDTH), BF16),
                pltpu.VMEM((2, SLOT, HEAD_WIDTH), BF16),
            ],
        ),
    )(info, pack, total, delta, inv, *last, weight, own, cw, ccw, *tables)


def rotation_tables():
    lane = jnp.arange(HEAD_WIDTH)
    inverse = jnp.power(F32(ROPE_BASE), -2.0 * (lane // 2).astype(F32) / HEAD_WIDTH)
    angles = jnp.arange(SLOT).astype(F32)[:, None] * inverse[None, :]
    sines = jnp.sin(angles)
    return jnp.cos(angles), jnp.where(lane[None, :] % 2 == 0, -sines, sines)


def ring_order(count):
    if count > 8:
        return list(range(count))
    return list(range(0, count, 2)) + list(range(1, count, 2))[::-1]


def program(count, rows, pack, info, x, scale, wq, wkv, wdown, wup, index, mix):
    order = ring_order(count)
    half = rows // 2
    reach = count // 2
    cw = [(order[i], order[(i + 1) % count]) for i in range(count)]
    ccw = [(b, a) for a, b in cw]
    send_cw = functools.partial(lax.ppermute, axis_name="tensor", perm=cw)
    send_ccw = functools.partial(lax.ppermute, axis_name="tensor", perm=ccw)
    model_width = wq.shape[0]

    xs = scale_rows(pack, x, scale)
    pieces = [xs[:half], xs[half:rows]]
    side = side_rows(pack, x, index, mix)
    partials = kv_partials(xs, wkv, rows)
    low = low_partials(xs, wdown, side, rows)

    went_cw, went_ccw = list(pieces), list(pieces)
    arrived = []
    for step in range(1, reach):
        for i in range(2):
            went_cw[i] = send_cw(went_cw[i])
            went_ccw[i] = send_ccw(went_ccw[i])
        arrived.append((list(went_cw), list(went_ccw)))
    last = (send_cw(went_cw[0]), send_ccw(went_ccw[1]))

    def block(row):
        return lax.dynamic_index_in_dim(partials, row, 0, keepdims=False)

    def add(a, b):
        return (a.astype(F32) + b.astype(F32)).astype(BF16)

    sums_cw = sums_ccw = None
    for step in range(1, reach + 1):
        own = block(info[1, reach + 1 - step])
        sums_cw = send_cw(own if sums_cw is None else add(sums_cw, own))
        if step < reach:
            own = block(info[1, count - reach + step])
            sums_ccw = send_ccw(own if sums_ccw is None else add(sums_ccw, own))
    if sums_ccw is None:
        sums_ccw = jnp.zeros_like(sums_cw)

    bit = 1
    while bit < count:
        low = low + lax.ppermute(low, "tensor", [(i, i ^ bit) for i in range(count)])
        bit *= 2

    total = query_step(info, None, [(0, [xs])], wq, rows)
    for step in range(1, reach):
        from_cw, from_ccw = arrived[step - 1]
        total = query_step(info, total, [(count - step, from_cw), (step, from_ccw)], wq, rows)
    delta, inv = query_delta(low, side, wup, rows, model_width)
    return attention(
        info, pack, total, delta, inv, last, reach, wq, (partials, sums_cw, sums_ccw),
        rotation_tables(), rows, 0,
    )


def shards(count, x, scale, wq, wkv, wdown, wup, index, mix, lengths):
    width = x.shape[1]
    shard = lax.axis_index("tensor")
    order = ring_order(count)
    group = (wq.shape[1] // HEAD_WIDTH, QUERY_HEADS // KV_HEADS)
    table = np.zeros((count, 2, count), np.int32)
    for place, device in enumerate(order):
        for away in range(count):
            other = order[(place + away) % count]
            table[device, 0, away] = other
            table[device, 1, away] = other * group[0] // group[1]
    info = lax.dynamic_index_in_dim(jnp.asarray(table), shard, 0, keepdims=False)
    scale = lax.dynamic_slice_in_dim(scale, shard * width, width, 0).reshape(1, width)
    live = (lengths + 15) // 16 * 16
    pack = jnp.concatenate([live[:1], lengths])
    rows = x.shape[0]
    return program(count, rows, pack, info, x, scale, wq, wkv, wdown, wup, index, mix)


def solution(mesh):
    placed = (
        P(("groups", "replica"), "tensor"),
        P(),
        P(None, "tensor"),
        P("tensor", None),
        P("tensor", None),
        P(None, "tensor"),
        P(("groups", "replica"), None),
        P(("groups", "replica"), None),
        P(("groups", "replica")),
    )
    return jax.shard_map(
        functools.partial(shards, mesh.shape["tensor"]),
        mesh=mesh,
        in_specs=placed,
        out_specs=P(("groups", "replica"), "tensor"),
        check_vma=False,
    )
```

time: 435 us -> 170 us (0.39)
  waiting for transfers between devices: 297 us -> 29.5 us
  Pallas kernels: 0 us -> 73.2 us
  matrix products: 55.1 us -> 0 us
  starting transfers between devices: 0.04 us -> 31.2 us
  local copies, waits for them, and re-layouts: 37.1 us -> 11.2 us
  other arithmetic: 31 us -> 8.64 us
    psum x1 -> x0, waiting for transfers between devices: 167 us -> none  [shards(): kv_raw, low = lax.psum((kv_part, low_part), 'tensor')]
    all_gather x1 -> x0, waiting for transfers between devices: 129 us -> none  [shards(): gathered = lax.all_gather(activations, 'tensor', axis=1, tiled=True)]
    pallas_call x0 -> x10, Pallas kernels: none -> 73.2 us  [the longest x4 26 us: query_step(): call(functools.partial(query_kernel, counts, total is not None), shape_of...]
    dot_general x8 -> x0, matrix products: 55.1 us -> none  [the longest x1 14.7 us: shards(): jnp.dot(normalized_input, query_weight, preferred_element_type=jnp.float32)]
    ppermute x0 -> x24, starting transfers between devices: none -> 31.2 us  [the longest x6 10.2 us: program(): went_ccw[i] = send_ccw(went_ccw[i])]
    ppermute x0 -> x24, waiting for transfers between devices: none -> 29.5 us  [the longest x3 24 us: program(): lax.ppermute(low, 'tensor', [(i, i ^ bit) for i in range(count)])]
    another operation x4 -> x0, other arithmetic: 14.2 us -> none
    reshape x3 -> x0, local copies, waits for them, and re-layouts: 13.2 us -> none  [the longest x1 10.4 us: shards(): reduced_rank_rows = jnp.dot(normalized_local_input, adapter_down_weight,...]
  transfers between devices with their start and end apart: 2 -> 24, of which waited for: 2 -> 6; matrix products, arithmetic and copies ran while one was open for 0% -> 7% of each run, Pallas kernels for 0% -> 27%
where the time goes in v1:
time: 170 us; the launch traced here: 167 us
  Pallas kernels  73.2 us (43%)
  starting transfers between devices  31.2 us (18%)
  waiting for transfers between devices  29.5 us (17%)
  between operations  13.7 us (8%)
  local copies, waits for them, and re-layouts  11.2 us (7%)
  other arithmetic  8.64 us (5%)
    pallas_call x4, Pallas kernels, query_step(): call(functools.partial(query_kernel, counts, total is not None), shape_of...  26 us
    ppermute x3, waiting for transfers between devices, program(): lax.ppermute(low, 'tensor', [(i, i ^ bit) for i in range(count)])  24 us
    pallas_call x1, Pallas kernels, query_delta(): call(functools.partial(delta_kernel, rows, model_width), (shape_of((rows,...  11.6 us
    pallas_call x1, Pallas kernels, low_partials(): call(functools.partial(low_kernel, rows), shape_of((LOW_ROWS, tokens), F3...  10.7 us
    pallas_call x1, Pallas kernels, attention(): call(functools.partial(attention_kernel, rows), shape_of((tokens, columns...  10.4 us
    ppermute x6, starting transfers between devices, program(): went_ccw[i] = send_ccw(went_ccw[i])  10.2 us
    pallas_call x1, Pallas kernels, kv_partials(): call(kv_kernel, shape_of((KV_HEADS, rows, 2 * HEAD_WIDTH), BF16), 2 * row...  8.12 us
    ppermute x3, starting transfers between devices, program(): lax.ppermute(low, 'tensor', [(i, i ^ bit) for i in range(count)])  7.54 us
  transfers between devices with their start and end apart: 24, of which 6 were waited for; matrix products, arithmetic and copies ran while one was open for 7% of the time, Pallas kernels for 27%

profile of v1, /device:TPU:0, one launch (start us, length us, event | category | flops | bytes accessed | tf_op | source)
XLA Modules:
  0.0 167.4 jit_solution(6379732784817852393)
XLA Ops:
  6.4 3.1 %shard_map.100.refs_0_.xs_ref = bf16[512,1024]{1,0:T(8,128)(2,1)} custom-call(s32[3]{0:T(128)} %pad_add_fusion.pack_ref, bf16[512,1024]{1,0:T(8,128)(2,1)} %x_ref.3, f32[1,1024]{1,0:T(1,128)} %bitcast.30), custom_call_target="tpu_custom_call" | custom-call | flops 1048576 | bytes 2097152 | tf_op jit(solution)/shard_map/pallas_call | solution.py:59
  9.5 3.3 %shard_map.105.side_ref = f32[512,128]{1,0:T(8,128)} custom-call(s32[3]{0:T(128)} %pad_add_fusion.pack_ref, bf16[512,1024]{1,0:T(8,128)(2,1)} %x_ref.3, s32[512,2]{1,0:T(8,128)} %copy.14.index_ref, f32[512,2]{1,0:T(8,128)} %copy.15.mix_ref), custom_call_target="tpu_custom_call" | custom-call | flops 1048576 | bytes 1048576 | tf_op jit(solution)/shard_map/pallas_call | solution.py:89
  12.8 10.7 %shard_map.106 = f32[40,512]{1,0:T(8,128)} custom-call(bf16[512,1024]{1,0:T(8,128)(2,1)} %shard_map.100.refs_0_.xs_ref, bf16[1024,4096]{1,0:T(8,128)(2,1)} %w_ref.4, f32[512,128]{1,0:T(8,128)} %shard_map.105.side_ref), custom_call_target="tpu_custom_call" | custom-call | flops 4294967296 | bytes 8388608 | tf_op jit(solution)/shard_map/pallas_call | solution.py:167
  23.5 3.0 %collective-permute-start.12 = (f32[40,512]{1,0:T(8,128)}, f32[40,512]{1,0:T(8,128)S(1)}, u32[]{:S(2)}, u32[]{:S(2)}) collective-permute-start(f32[40,512]{1,0:T(8,128)} %shard_map.106), channel_id=1, source_target_pairs={{0,1},{1,0},{2,3},{3,2},{4,5},{5,4},{6,7},{7,6},{8,9},{9,8},{10,11... | collective-permute-start | bytes 245768 | tf_op jit(solution)/shard_map/ppermute | solution.py:441
  30.5 8.1 %shard_map.108.own_ref = bf16[8,512,256]{2,1,0:T(8,128)(2,1)} custom-call(bf16[512,1024]{1,0:T(8,128)(2,1)} %shard_map.100.refs_0_.xs_ref, bf16[1024,2048]{1,0:T(8,128)(2,1)} %w_ref.6), custom_call_target="tpu_custom_call" | custom-call | flops 2147483648 | bytes 7340032 | tf_op jit(solution)/shard_map/pallas_call | solution.py:109
  42.0 2.0 %collective-permute-start.17 = (bf16[512,256]{1,0:T(8,128)(2,1)}, bf16[512,256]{1,0:T(8,128)(2,1)}, u32[]{:S(2)}, u32[]{:S(2)}) collective-permute-start(bf16[512,256]{1,0:T(8,128)(2,1)} %get-tuple-element.14), channel_id=1, source_target_pairs={{0,2},{2,4},{4,6},{6,7},{7,5},{5,3},{3,1},{1,0},{8,10},{10,12},{12... | collective-permute-start | bytes 786440 | tf_op jit(solution)/shard_map/ppermute | solution.py:432
  51.6 2.0 %collective-permute-start.13 = (f32[40,512]{1,0:T(8,128)S(1)}, f32[40,512]{1,0:T(8,128)S(1)}, u32[]{:S(2)}, u32[]{:S(2)}) collective-permute-start(f32[40,512]{1,0:T(8,128)S(1)} %add.76), channel_id=1, source_target_pairs={{0,2},{1,3},{2,0},{3,1},{4,6},{5,7},{6,4},{7,5},{8,10},{9,11},{10,... | collective-permute-start | bytes 245768 | tf_op jit(solution)/shard_map/ppermute | solution.py:441
  55.4 18.1 %collective-permute-done.13 = f32[40,512]{1,0:T(8,128)S(1)} collective-permute-done((f32[40,512]{1,0:T(8,128)S(1)}, f32[40,512]{1,0:T(8,128)S(1)}, u32[]{:S(2)}, u32[]{:S(2)}) %collective-permute-start.13) | collective-permute-done | bytes 81952 | tf_op jit(solution)/shard_map/ppermute | solution.py:441
  73.5 2.5 %collective-permute-start.2 = (bf16[256,1024]{1,0:T(8,128)(2,1)}, bf16[256,1024]{1,0:T(8,128)(2,1)}, u32[]{:S(2)}, u32[]{:S(2)}) collective-permute-start(bf16[256,1024]{1,0:T(8,128)(2,1)} %get-tuple-element.16), channel_id=1, source_target_pairs={{2,0},{4,2},{6,4},{7,6},{5,7},{3,5},{1,3},{0,1},{10,8},{12,10},{14... | collective-permute-start | bytes 1572872 | tf_op jit(solution)/shard_map/ppermute | solution.py:419
  79.6 2.6 %collective-permute-start.14 = (f32[40,512]{1,0:T(8,128)S(1)}, f32[40,512]{1,0:T(8,128)S(1)}, u32[]{:S(2)}, u32[]{:S(2)}) collective-permute-start(f32[40,512]{1,0:T(8,128)S(1)} %add.77), channel_id=1, source_target_pairs={{0,4},{1,5},{2,6},{3,7},{4,0},{5,1},{6,2},{7,3},{8,12},{9,13},{10,... | collective-permute-start | bytes 245768 | tf_op jit(solution)/shard_map/ppermute | solution.py:441
  82.3 2.0 %collective-permute-start.4 = (bf16[256,1024]{1,0:T(8,128)(2,1)}, bf16[256,1024]{1,0:T(8,128)(2,1)}, u32[]{:S(2)}, u32[]{:S(2)}) collective-permute-start(bf16[256,1024]{1,0:T(8,128)(2,1)} %collective-permute-done.refs_1_), channel_id=1, source_target_pairs={{0,2},{2,4},{4,6},{6,7},{7,5},{5,3},{3,1},{1,0},{8,10},{10,12},{12... | collective-permute-start | bytes 1572872 | tf_op jit(solution)/shard_map/ppermute | solution.py:418
  84.4 2.0 %collective-permute-start.7 = (bf16[256,1024]{1,0:T(8,128)(2,1)S(1)}, bf16[256,1024]{1,0:T(8,128)(2,1)}, u32[]{:S(2)}, u32[]{:S(2)}) collective-permute-start(bf16[256,1024]{1,0:T(8,128)(2,1)S(1)} %collective-permute-done.3.refs_4_), channel_id=1, source_target_pairs={{2,0},{4,2},{6,4},{7,6},{5,7},{3,5},{1,3},{0,1},{10,8},{12,10},{14... | collective-permute-start | bytes 1572872 | tf_op jit(solution)/shard_map/ppermute | solution.py:419
  88.2 5.8 %collective-permute-done.14 = f32[40,512]{1,0:T(8,128)S(1)} collective-permute-done((f32[40,512]{1,0:T(8,128)S(1)}, f32[40,512]{1,0:T(8,128)S(1)}, u32[]{:S(2)}, u32[]{:S(2)}) %collective-permute-start.14) | collective-permute-done | bytes 81952 | tf_op jit(solution)/shard_map/ppermute | solution.py:441
  100.9 4.8 %shard_map.101.refs_0_ = f32[512,1024]{1,0:T(8,128)} custom-call(s32[2,8]{1,0:T(2,128)} %copy-done.12, bf16[512,1024]{1,0:T(8,128)(2,1)} %shard_map.100.refs_0_.xs_ref, bf16[8192,1024]{1,0:T(8,128)(2,1)} %w_ref.7), custom_call_target="tpu_custom_call" | custom-call | flops 1073741824 | bytes 7340032 | tf_op jit(solution)/shard_map/pallas_call | solution.py:275
  107.7 3.8 %collective-permute-start.19 = (bf16[512,256]{1,0:T(8,128)(2,1)S(1)}, bf16[512,256]{1,0:T(8,128)(2,1)S(1)}, u32[]{:S(2)}, u32[]{:S(2)}) collective-permute-start(bf16[512,256]{1,0:T(8,128)(2,1)S(1)} %get-tuple-element.12), channel_id=1, source_target_pairs={{0,2},{2,4},{4,6},{6,7},{7,5},{5,3},{3,1},{1,0},{8,10},{10,12},{12... | collective-permute-start | bytes 786440 | tf_op jit(solution)/shard_map/ppermute | solution.py:432
  111.6 2.0 %collective-permute-start.11 = (bf16[256,1024]{1,0:T(8,128)(2,1)}, bf16[256,1024]{1,0:T(8,128)(2,1)S(1)}, u32[]{:S(2)}, u32[]{:S(2)}) collective-permute-start(bf16[256,1024]{1,0:T(8,128)(2,1)} %collective-permute-done.7.refs_4_), channel_id=1, source_target_pairs={{2,0},{4,2},{6,4},{7,6},{5,7},{3,5},{1,3},{0,1},{10,8},{12,10},{14... | collective-permute-start | bytes 1572872 | tf_op jit(solution)/shard_map/ppermute | solution.py:419
  113.6 11.6 %shard_map.107 = (f32[512,1024]{1,0:T(8,128)}, f32[512,128]{1,0:T(8,128)}) custom-call(f32[40,512]{1,0:T(8,128)} %add.78.low_ref, f32[512,128]{1,0:T(8,128)} %shard_map.105.side_ref, bf16[4096,1024]{1,0:T(8,128)(2,1)} %w_ref.5), custom_call_target="tpu_custom_call" | custom-call | flops 4294967296 | bytes 10485760 | tf_op jit(solution)/shard_map/pallas_call | solution.py:220
  125.2 2.0 %collective-permute-start.10 = (bf16[256,1024]{1,0:T(8,128)(2,1)}, bf16[256,1024]{1,0:T(8,128)(2,1)S(1)}, u32[]{:S(2)}, u32[]{:S(2)}) collective-permute-start(bf16[256,1024]{1,0:T(8,128)(2,1)} %collective-permute-done.6.refs_3_), channel_id=1, source_target_pairs={{2,0},{4,2},{6,4},{7,6},{5,7},{3,5},{1,3},{0,1},{10,8},{12,10},{14... | collective-permute-start | bytes 1572872 | tf_op jit(solution)/shard_map/ppermute | solution.py:419
  127.2 7.0 %shard_map.102.refs_0_ = f32[512,1024]{1,0:T(8,128)} custom-call(s32[2,8]{1,0:T(2,128)} %copy-done.12, f32[512,1024]{1,0:T(8,128)} %shard_map.101.refs_0_, bf16[256,1024]{1,0:T(8,128)(2,1)} %collective-permute-done.refs_1_, bf16[256,1024]{1,0:T(8,128)(2,1)} %copy-done.2, ...), custom_call_target="tpu_custom_call", output_to_operand_aliasing={{}: (1, {})} | custom-call | flops 2147483648 | bytes 10485760 | tf_op jit(solution)/shard_map/pallas_call | solution.py:275
  134.3 2.0 %collective-permute-start.16 = (bf16[256,1024]{1,0:T(8,128)(2,1)S(1)}, bf16[256,1024]{1,0:T(8,128)(2,1)S(1)}, u32[]{:S(2)}, u32[]{:S(2)}) collective-permute-start(bf16[256,1024]{1,0:T(8,128)(2,1)S(1)} %collective-permute-done.11.refs_4_), channel_id=1, source_target_pairs={{2,0},{4,2},{6,4},{7,6},{5,7},{3,5},{1,3},{0,1},{10,8},{12,10},{14... | collective-permute-start | bytes 1572872 | tf_op jit(solution)/shard_map/ppermute | solution.py:421
  137.5 3.3 %collective-permute-done.9.refs_2_ = bf16[256,1024]{1,0:T(8,128)(2,1)S(1)} collective-permute-done((bf16[256,1024]{1,0:T(8,128)(2,1)}, bf16[256,1024]{1,0:T(8,128)(2,1)S(1)}, u32[]{:S(2)}, u32[]{:S(2)}) %collective-permute-start.9) | collective-permute-done | bytes 524320 | tf_op jit(solution)/shard_map/ppermute | solution.py:418
  140.9 7.0 %shard_map.103.refs_0_ = f32[512,1024]{1,0:T(8,128)} custom-call(s32[2,8]{1,0:T(2,128)} %copy-done.12, f32[512,1024]{1,0:T(8,128)} %shard_map.102.refs_0_, bf16[256,1024]{1,0:T(8,128)(2,1)} %collective-permute-done.4.refs_1_, bf16[256,1024]{1,0:T(8,128)(2,1)} %collective-permute-done.5.refs_2_, ...), custom_call_target="tpu_custom_call", output_to_operand_aliasing={{}: (1, {})} | custom-call | flops 2147483648 | bytes 10485760 | tf_op jit(solution)/shard_map/pallas_call | solution.py:275
  148.7 7.0 %shard_map.104.total_ref = f32[512,1024]{1,0:T(8,128)} custom-call(s32[2,8]{1,0:T(2,128)} %copy-done.12, f32[512,1024]{1,0:T(8,128)} %shard_map.103.refs_0_, bf16[256,1024]{1,0:T(8,128)(2,1)} %copy-done.4, bf16[256,1024]{1,0:T(8,128)(2,1)} %copy-done.6, bf16[256,1024]{1,0:T(8,128)(2,1)} %copy-done.7, ...), custom_call_target="tpu_custom_call", output_to_operand_aliasing={{}: (1, {})} | custom-call | flops 2147483648 | bytes 10485760 | tf_op jit(solution)/shard_map/pallas_call | solution.py:275
  156.9 10.4 %shard_map.109 = bf16[512,1024]{1,0:T(8,128)(2,1)} custom-call(s32[2,8]{1,0:T(2,128)} %copy-done.12, s32[3]{0:T(128)} %pad_add_fusion.pack_ref, f32[512,1024]{1,0:T(8,128)} %shard_map.104.total_ref, f32[512,1024]{1,0:T(8,128)} %get-tuple-element.7.delta_ref, f32[512,128]{1,0:T(8,128)} %get-tuple-element.8.inv_ref, bf16[256,1024]{1,0:T(8,128)(2,1)} %copy-done.8, ...), custom_call_target="tpu_custom_call" | custom-call | flops 1610612736 | bytes 8388608 | tf_op jit(solution)/shard_map/pallas_call | solution.py:352
  (85 shorter events, 27.4 us)
Async XLA Ops:
  23.5 25.7 %collective-permute-start.12 = (f32[40,512]{1,0:T(8,128)}, f32[40,512]{1,0:T(8,128)S(1)}, u32[]{:S(2)}, u32[]{:S(2)}) collective-permute-start(f32[40,512]{1,0:T(8,128)} %shard_map.106), channel_id=1, source_target_pairs={{0,1},{1,0},{2,3},{3,2},{4,5},{5,4},{6,7},{7,6},{8,9},{9,8},{10,11... | collective-permute-start | bytes 245768 | tf_op jit(solution)/shard_map/ppermute | solution.py:441
  42.0 34.0 %collective-permute-start.21 = (bf16[512,256]{1,0:T(8,128)(2,1)}, bf16[512,256]{1,0:T(8,128)(2,1)}, u32[]{:S(2)}, u32[]{:S(2)}) collective-permute-start(bf16[512,256]{1,0:T(8,128)(2,1)} %get-tuple-element.13), channel_id=1, source_target_pairs={{2,0},{4,2},{6,4},{7,6},{5,7},{3,5},{1,3},{0,1},{10,8},{12,10},{14... | collective-permute-start | bytes 786440 | tf_op jit(solution)/shard_map/ppermute | solution.py:435
  42.0 9.6 %collective-permute-start.17 = (bf16[512,256]{1,0:T(8,128)(2,1)}, bf16[512,256]{1,0:T(8,128)(2,1)}, u32[]{:S(2)}, u32[]{:S(2)}) collective-permute-start(bf16[512,256]{1,0:T(8,128)(2,1)} %get-tuple-element.14), channel_id=1, source_target_pairs={{0,2},{2,4},{4,6},{6,7},{7,5},{5,3},{3,1},{1,0},{8,10},{10,12},{12... | collective-permute-start | bytes 786440 | tf_op jit(solution)/shard_map/ppermute | solution.py:432
  45.1 37.1 %collective-permute-start.1 = (bf16[256,1024]{1,0:T(8,128)(2,1)}, bf16[256,1024]{1,0:T(8,128)(2,1)S(1)}, u32[]{:S(2)}, u32[]{:S(2)}) collective-permute-start(bf16[256,1024]{1,0:T(8,128)(2,1)} %get-tuple-element.15), channel_id=1, source_target_pairs={{0,2},{2,4},{4,6},{6,7},{7,5},{5,3},{3,1},{1,0},{8,10},{10,12},{12... | collective-permute-start | bytes 1572872 | tf_op jit(solution)/shard_map/ppermute | solution.py:418
  46.7 37.6 %collective-permute-start.3 = (bf16[256,1024]{1,0:T(8,128)(2,1)}, bf16[256,1024]{1,0:T(8,128)(2,1)S(1)}, u32[]{:S(2)}, u32[]{:S(2)}) collective-permute-start(bf16[256,1024]{1,0:T(8,128)(2,1)} %get-tuple-element.15), channel_id=1, source_target_pairs={{2,0},{4,2},{6,4},{7,6},{5,7},{3,5},{1,3},{0,1},{10,8},{12,10},{14... | collective-permute-start | bytes 1572872 | tf_op jit(solution)/shard_map/ppermute | solution.py:419
  49.2 30.4 %collective-permute-start = (bf16[256,1024]{1,0:T(8,128)(2,1)}, bf16[256,1024]{1,0:T(8,128)(2,1)}, u32[]{:S(2)}, u32[]{:S(2)}) collective-permute-start(bf16[256,1024]{1,0:T(8,128)(2,1)} %get-tuple-element.16), channel_id=1, source_target_pairs={{0,2},{2,4},{4,6},{6,7},{7,5},{5,3},{3,1},{1,0},{8,10},{10,12},{12... | collective-permute-start | bytes 1572872 | tf_op jit(solution)/shard_map/ppermute | solution.py:418
  51.6 21.9 %collective-permute-start.13 = (f32[40,512]{1,0:T(8,128)S(1)}, f32[40,512]{1,0:T(8,128)S(1)}, u32[]{:S(2)}, u32[]{:S(2)}) collective-permute-start(f32[40,512]{1,0:T(8,128)S(1)} %add.76), channel_id=1, source_target_pairs={{0,2},{1,3},{2,0},{3,1},{4,6},{5,7},{6,4},{7,5},{8,10},{9,11},{10,... | collective-permute-start | bytes 245768 | tf_op jit(solution)/shard_map/ppermute | solution.py:441
  73.5 21.1 %collective-permute-start.2 = (bf16[256,1024]{1,0:T(8,128)(2,1)}, bf16[256,1024]{1,0:T(8,128)(2,1)}, u32[]{:S(2)}, u32[]{:S(2)}) collective-permute-start(bf16[256,1024]{1,0:T(8,128)(2,1)} %get-tuple-element.16), channel_id=1, source_target_pairs={{2,0},{4,2},{6,4},{7,6},{5,7},{3,5},{1,3},{0,1},{10,8},{12,10},{14... | collective-permute-start | bytes 1572872 | tf_op jit(solution)/shard_map/ppermute | solution.py:419
  76.0 8.3 %collective-permute-start.18 = (bf16[512,256]{1,0:T(8,128)(2,1)}, bf16[512,256]{1,0:T(8,128)(2,1)}, u32[]{:S(2)}, u32[]{:S(2)}) collective-permute-start(bf16[512,256]{1,0:T(8,128)(2,1)} %fusion.4), channel_id=1, source_target_pairs={{0,2},{2,4},{4,6},{6,7},{7,5},{5,3},{3,1},{1,0},{8,10},{10,12},{12... | collective-permute-start | bytes 786440 | tf_op jit(solution)/shard_map/ppermute | solution.py:432
  79.6 14.3 %collective-permute-start.14 = (f32[40,512]{1,0:T(8,128)S(1)}, f32[40,512]{1,0:T(8,128)S(1)}, u32[]{:S(2)}, u32[]{:S(2)}) collective-permute-start(f32[40,512]{1,0:T(8,128)S(1)} %add.77), channel_id=1, source_target_pairs={{0,4},{1,5},{2,6},{3,7},{4,0},{5,1},{6,2},{7,3},{8,12},{9,13},{10,... | collective-permute-start | bytes 245768 | tf_op jit(solution)/shard_map/ppermute | solution.py:441
  82.3 29.3 %collective-permute-start.4 = (bf16[256,1024]{1,0:T(8,128)(2,1)}, bf16[256,1024]{1,0:T(8,128)(2,1)}, u32[]{:S(2)}, u32[]{:S(2)}) collective-permute-start(bf16[256,1024]{1,0:T(8,128)(2,1)} %collective-permute-done.refs_1_), channel_id=1, source_target_pairs={{0,2},{2,4},{4,6},{6,7},{7,5},{5,3},{3,1},{1,0},{8,10},{10,12},{12... | collective-permute-start | bytes 1572872 | tf_op jit(solution)/shard_map/ppermute | solution.py:418
  84.3 27.3 %collective-permute-start.5 = (bf16[256,1024]{1,0:T(8,128)(2,1)S(1)}, bf16[256,1024]{1,0:T(8,128)(2,1)}, u32[]{:S(2)}, u32[]{:S(2)}) collective-permute-start(bf16[256,1024]{1,0:T(8,128)(2,1)S(1)} %collective-permute-done.1.refs_2_), channel_id=1, source_target_pairs={{0,2},{2,4},{4,6},{6,7},{7,5},{5,3},{3,1},{1,0},{8,10},{10,12},{12... | collective-permute-start | bytes 1572872 | tf_op jit(solution)/shard_map/ppermute | solution.py:418
  84.4 27.2 %collective-permute-start.7 = (bf16[256,1024]{1,0:T(8,128)(2,1)S(1)}, bf16[256,1024]{1,0:T(8,128)(2,1)}, u32[]{:S(2)}, u32[]{:S(2)}) collective-permute-start(bf16[256,1024]{1,0:T(8,128)(2,1)S(1)} %collective-permute-done.3.refs_4_), channel_id=1, source_target_pairs={{2,0},{4,2},{6,4},{7,6},{5,7},{3,5},{1,3},{0,1},{10,8},{12,10},{14... | collective-permute-start | bytes 1572872 | tf_op jit(solution)/shard_map/ppermute | solution.py:419
  94.6 13.1 %collective-permute-start.22 = (bf16[512,256]{1,0:T(8,128)(2,1)}, bf16[512,256]{1,0:T(8,128)(2,1)}, u32[]{:S(2)}, u32[]{:S(2)}) collective-permute-start(bf16[512,256]{1,0:T(8,128)(2,1)} %get-tuple-element.11), channel_id=1, source_target_pairs={{2,0},{4,2},{6,4},{7,6},{5,7},{3,5},{1,3},{0,1},{10,8},{12,10},{14... | collective-permute-start | bytes 786440 | tf_op jit(solution)/shard_map/ppermute | solution.py:435
  94.6 30.6 %collective-permute-start.6 = (bf16[256,1024]{1,0:T(8,128)(2,1)}, bf16[256,1024]{1,0:T(8,128)(2,1)}, u32[]{:S(2)}, u32[]{:S(2)}) collective-permute-start(bf16[256,1024]{1,0:T(8,128)(2,1)} %collective-permute-done.2.refs_3_), channel_id=1, source_target_pairs={{2,0},{4,2},{6,4},{7,6},{5,7},{3,5},{1,3},{0,1},{10,8},{12,10},{14... | collective-permute-start | bytes 1572872 | tf_op jit(solution)/shard_map/ppermute | solution.py:419
  107.7 28.6 %collective-permute-start.19 = (bf16[512,256]{1,0:T(8,128)(2,1)S(1)}, bf16[512,256]{1,0:T(8,128)(2,1)S(1)}, u32[]{:S(2)}, u32[]{:S(2)}) collective-permute-start(bf16[512,256]{1,0:T(8,128)(2,1)S(1)} %get-tuple-element.12), channel_id=1, source_target_pairs={{0,2},{2,4},{4,6},{6,7},{7,5},{5,3},{3,1},{1,0},{8,10},{10,12},{12... | collective-permute-start | bytes 786440 | tf_op jit(solution)/shard_map/ppermute | solution.py:432
  111.5 22.7 %collective-permute-start.8 = (bf16[256,1024]{1,0:T(8,128)(2,1)}, bf16[256,1024]{1,0:T(8,128)(2,1)S(1)}, u32[]{:S(2)}, u32[]{:S(2)}) collective-permute-start(bf16[256,1024]{1,0:T(8,128)(2,1)} %collective-permute-done.4.refs_1_), channel_id=1, source_target_pairs={{0,2},{2,4},{4,6},{6,7},{7,5},{5,3},{3,1},{1,0},{8,10},{10,12},{12... | collective-permute-start | bytes 1572872 | tf_op jit(solution)/shard_map/ppermute | solution.py:418
  111.6 29.3 %collective-permute-start.9 = (bf16[256,1024]{1,0:T(8,128)(2,1)}, bf16[256,1024]{1,0:T(8,128)(2,1)S(1)}, u32[]{:S(2)}, u32[]{:S(2)}) collective-permute-start(bf16[256,1024]{1,0:T(8,128)(2,1)} %collective-permute-done.5.refs_2_), channel_id=1, source_target_pairs={{0,2},{2,4},{4,6},{6,7},{7,5},{5,3},{3,1},{1,0},{8,10},{10,12},{12... | collective-permute-start | bytes 1572872 | tf_op jit(solution)/shard_map/ppermute | solution.py:418
  111.6 22.7 %collective-permute-start.11 = (bf16[256,1024]{1,0:T(8,128)(2,1)}, bf16[256,1024]{1,0:T(8,128)(2,1)S(1)}, u32[]{:S(2)}, u32[]{:S(2)}) collective-permute-start(bf16[256,1024]{1,0:T(8,128)(2,1)} %collective-permute-done.7.refs_4_), channel_id=1, source_target_pairs={{2,0},{4,2},{6,4},{7,6},{5,7},{3,5},{1,3},{0,1},{10,8},{12,10},{14... | collective-permute-start | bytes 1572872 | tf_op jit(solution)/shard_map/ppermute | solution.py:419
  125.2 22.7 %collective-permute-start.10 = (bf16[256,1024]{1,0:T(8,128)(2,1)}, bf16[256,1024]{1,0:T(8,128)(2,1)S(1)}, u32[]{:S(2)}, u32[]{:S(2)}) collective-permute-start(bf16[256,1024]{1,0:T(8,128)(2,1)} %collective-permute-done.6.refs_3_), channel_id=1, source_target_pairs={{2,0},{4,2},{6,4},{7,6},{5,7},{3,5},{1,3},{0,1},{10,8},{12,10},{14... | collective-permute-start | bytes 1572872 | tf_op jit(solution)/shard_map/ppermute | solution.py:419
  134.2 21.7 %collective-permute-start.15 = (bf16[256,1024]{1,0:T(8,128)(2,1)S(1)}, bf16[256,1024]{1,0:T(8,128)(2,1)S(1)}, u32[]{:S(2)}, u32[]{:S(2)}) collective-permute-start(bf16[256,1024]{1,0:T(8,128)(2,1)S(1)} %collective-permute-done.8.refs_1_), channel_id=1, source_target_pairs={{0,2},{2,4},{4,6},{6,7},{7,5},{5,3},{3,1},{1,0},{8,10},{10,12},{12... | collective-permute-start | bytes 1572872 | tf_op jit(solution)/shard_map/ppermute | solution.py:421
  134.3 21.6 %collective-permute-start.16 = (bf16[256,1024]{1,0:T(8,128)(2,1)S(1)}, bf16[256,1024]{1,0:T(8,128)(2,1)S(1)}, u32[]{:S(2)}, u32[]{:S(2)}) collective-permute-start(bf16[256,1024]{1,0:T(8,128)(2,1)S(1)} %collective-permute-done.11.refs_4_), channel_id=1, source_target_pairs={{2,0},{4,2},{6,4},{7,6},{5,7},{3,5},{1,3},{0,1},{10,8},{12,10},{14... | collective-permute-start | bytes 1572872 | tf_op jit(solution)/shard_map/ppermute | solution.py:421
  137.4 18.4 %collective-permute-start.20 = (bf16[512,256]{1,0:T(8,128)(2,1)S(1)}, bf16[512,256]{1,0:T(8,128)(2,1)S(1)}, u32[]{:S(2)}, u32[]{:S(2)}) collective-permute-start(bf16[512,256]{1,0:T(8,128)(2,1)S(1)} %get-tuple-element.10), channel_id=1, source_target_pairs={{0,2},{2,4},{4,6},{6,7},{7,5},{5,3},{3,1},{1,0},{8,10},{10,12},{12... | collective-permute-start | bytes 786440 | tf_op jit(solution)/shard_map/ppermute | solution.py:432
  140.9 15.0 %collective-permute-start.23 = (bf16[512,256]{1,0:T(8,128)(2,1)S(1)}, bf16[512,256]{1,0:T(8,128)(2,1)S(1)}, u32[]{:S(2)}, u32[]{:S(2)}) collective-permute-start(bf16[512,256]{1,0:T(8,128)(2,1)S(1)} %get-tuple-element.9), channel_id=1, source_target_pairs={{2,0},{4,2},{6,4},{7,6},{5,7},{3,5},{1,3},{0,1},{10,8},{12,10},{14... | collective-permute-start | bytes 786440 | tf_op jit(solution)/shard_map/ppermute | solution.py:435
  (16 other events, 141.2 us)

commit v2 on v0

v2 whole, which is shorter than its diff:
```python
import functools
import math

import jax
import jax.numpy as jnp
import numpy as np
from jax import lax
from jax.experimental import pallas as pl
from jax.experimental.pallas import tpu as pltpu
from jax.sharding import PartitionSpec as P

QUERY_HEADS = 64
KV_HEADS = 8
HEAD_WIDTH = 128
ADAPTER_RANK = 16
SLOT = 256
LANES = 128
LOW_ROWS = 40

EPS = 1e-05
ROPE_BASE = 500000.0

SIDE_SQUARES = 0
SIDE_MIX = 1
SIDE_INDEX = 3

QUERY_WEIGHT = 8.0
VMEM_LIMIT = 62 * 1024 * 1024
F32 = jnp.float32
BF16 = jnp.bfloat16


def call(kernel, out_shape, microseconds=0.0, **kwargs):
    return pl.pallas_call(
        kernel,
        out_shape=out_shape,
        compiler_params=pltpu.CompilerParams(vmem_limit_bytes=VMEM_LIMIT),
        cost_estimate=pl.CostEstimate(
            flops=int(1.15e9 * microseconds), bytes_accessed=1000, transcendentals=0
        ),
        **kwargs,
    )


def whole(shape):
    return pl.BlockSpec(shape, lambda *_: (0,) * len(shape))


def shape_of(shape, dtype):
    return jax.ShapeDtypeStruct(shape, dtype)


def prefetch(count, grid, in_specs, out_specs, scratch_shapes=()):
    return pltpu.PrefetchScalarGridSpec(
        num_scalar_prefetch=count,
        grid=grid,
        in_specs=in_specs,
        out_specs=out_specs,
        scratch_shapes=scratch_shapes,
    )


def second_start(rows, lengths_ref):
    if rows == 2 * SLOT:
        return SLOT
    return pl.multiple_of((lengths_ref[0] + 15) // 16 * 16, 16)


def write_message(message, block, w_ref):
    half, width = block.shape
    message[:half, :width] = block
    product = jnp.dot(block, w_ref[...], preferred_element_type=F32)
    message[:half, width:] = product.astype(BF16)


def scale_kernel(
    rows, lengths_ref, info_ref, x_ref, scale_ref, cw_w_ref, ccw_w_ref, cw_ref, ccw_ref, packed
):
    packed[...] = (x_ref[...].astype(F32) * scale_ref[...]).astype(BF16)
    if rows != 2 * SLOT:
        packed[pl.ds(second_start(rows, lengths_ref), SLOT), :] = packed[SLOT:, :]
    block = packed[: rows // 2, :]
    write_message(cw_ref, block, cw_w_ref)
    write_message(ccw_ref, block, ccw_w_ref)


def scale_rows(lengths, info, x, scale, weight, rows, reach):
    tokens, width = x.shape
    pair = 2 * HEAD_WIDTH
    message = (rows // 2, width + pair)
    column = [
        pl.BlockSpec((width, pair), lambda j, lengths, info, away=away: (0, info[1, away]))
        for away in (reach, reach + 1)
    ]
    return call(
        functools.partial(scale_kernel, rows),
        (shape_of(message, BF16),) * 2 + (shape_of((tokens, width), BF16),),
        grid_spec=prefetch(
            2,
            (1,),
            [
                whole((tokens, width)),
                pl.BlockSpec((1, width), lambda j, lengths, info: (0, info[0, 0])),
                *column,
            ],
            (whole(message),) * 2 + (whole((tokens, width)),),
        ),
    )(lengths, info, x, scale.reshape(1, -1), weight, weight)


def low_places(tokens, full):
    if full >= 2 * tokens + SLOT:
        second = (slice(0, ADAPTER_RANK), slice(tokens, 2 * tokens))
        squares = (0, slice(2 * tokens, 2 * tokens + SLOT))
        extra = ADAPTER_RANK
    else:
        second = (slice(ADAPTER_RANK, 2 * ADAPTER_RANK), slice(0, tokens))
        squares = (2 * ADAPTER_RANK, slice(0, SLOT))
        extra = 3 * ADAPTER_RANK
    return extra, (slice(0, ADAPTER_RANK), slice(0, tokens)), second, squares


def read_low(region):
    tokens = 2 * SLOT
    _, first, second, (row, lanes) = low_places(tokens, region.shape[1])
    squares = jnp.concatenate(
        [region[row + i : row + i + 1, lanes] + region[row + 2 + i : row + 3 + i, lanes] for i in range(2)],
        axis=1,
    )
    return jnp.concatenate(
        [region[first], region[second], squares, jnp.zeros((LOW_ROWS - 33, tokens), F32)], axis=0
    )


def write_low(message, half, low):
    tokens = 2 * SLOT
    extra, first, second, (row, lanes) = low_places(tokens, message.shape[1])
    message[half : half + extra, :] = jnp.zeros((extra, message.shape[1]), BF16)
    squares = low[2 * ADAPTER_RANK : 2 * ADAPTER_RANK + 1, :]
    rounded = squares.astype(BF16)
    rest = (squares - rounded.astype(F32)).astype(BF16)
    for place, value in ((first, low[:ADAPTER_RANK]), (second, low[ADAPTER_RANK : 2 * ADAPTER_RANK])):
        span = slice(half + place[0].start, half + place[0].stop)
        message[span, place[1]] = value.astype(BF16)
    block = jnp.concatenate(
        [rounded[:, :SLOT], rounded[:, SLOT:], rest[:, :SLOT], rest[:, SLOT:]]
        + [jnp.zeros((ADAPTER_RANK - 4, SLOT), BF16)],
        axis=0,
    )
    message[half + row : half + row + ADAPTER_RANK, lanes] = block


def add_kernel(*refs):
    count = len(refs) // 3
    for i in range(count):
        total = refs[i][...].astype(F32) + refs[count + i][0].astype(F32)
        refs[2 * count + i][...] = total.astype(BF16)


def add_terms(messages, terms, rows):
    half = rows // 2
    full = messages[0].shape[1]
    pair = 2 * HEAD_WIDTH
    lanes = pl.BlockSpec((half, pair), lambda j: (0, full // pair - 1))
    own = [pl.BlockSpec((1, half, pair), lambda j, away=away: (away, 0, 0)) for _, away in terms]
    count = len(messages)
    return call(
        add_kernel,
        (shape_of((half, full), BF16),) * count,
        grid=(1,),
        in_specs=[lanes] * count + own,
        out_specs=(lanes,) * count,
        input_output_aliases={i: i for i in range(count)},
    )(*messages, *[array for array, _ in terms])


def add_low_kernel(half, low_ref, *refs):
    count = len(refs) // 3
    pair = 2 * HEAD_WIDTH
    for i in range(count):
        given, term, out = refs[i], refs[count + i], refs[2 * count + i]
        full = given.shape[1]
        out[:half, : full - pair] = given[:half, : full - pair]
        total = given[:half, full - pair :].astype(F32) + term[0].astype(F32)
        out[:half, full - pair :] = total.astype(BF16)
        write_low(out, half, read_low(given[half:, :].astype(F32)) + low_ref[...])


def add_terms_low(messages, terms, low, rows):
    half = rows // 2
    shape = messages[0].shape
    pair = 2 * HEAD_WIDTH
    own = [pl.BlockSpec((1, half, pair), lambda j, away=away: (away, 1, 0)) for _, away in terms]
    count = len(messages)
    return call(
        functools.partial(add_low_kernel, half),
        (shape_of(shape, BF16),) * count,
        grid=(1,),
        in_specs=[whole(low.shape)] + [whole(shape)] * count + own,
        out_specs=(whole(shape),) * count,
    )(low, *messages, *[array for array, _ in terms])


def kv_kernel(info_ref, x_ref, near_w_ref, far_w_ref, near_ref, far_ref):
    for w_ref, out_ref in ((near_w_ref, near_ref), (far_w_ref, far_ref)):
        product = jnp.dot(x_ref[...], w_ref[...], preferred_element_type=F32)
        out_ref[0] = product.astype(BF16)


def kv_partials(info, packed, weight, rows, count):
    width = weight.shape[0]
    pair = 2 * HEAD_WIDTH
    out = shape_of((count // 2, rows, pair), BF16)
    block = pl.BlockSpec((1, rows, pair), lambda i, info: (i, 0, 0))
    return call(
        kv_kernel,
        (out, out),
        grid_spec=prefetch(
            1,
            (count // 2,),
            [
                whole((rows, width)),
                pl.BlockSpec((width, pair), lambda i, info: (0, info[1, i])),
                pl.BlockSpec((width, pair), lambda i, info: (0, info[1, count // 2 + i])),
            ],
            (block, block),
        ),
    )(info, packed, weight, weight)


def adapter_of(first):
    lane = lax.broadcasted_iota(jnp.int32, (1, LANES), 1)
    return ((first + lane) // ADAPTER_RANK).astype(F32)


def fold(value):
    shift = ADAPTER_RANK
    while shift < LANES:
        value = value + pltpu.roll(value, shift, 1)
        shift *= 2
    return value


def low_kernel(
    rows, lengths_ref, info_ref, x_ref, packed_ref, w_ref, index_ref, mix_ref, cw_w_ref, ccw_w_ref,
    out_ref, side_ref, cw_ref, ccw_ref, acc_ref,
):
    step = pl.program_id(0)
    half = rows // 2
    tile = w_ref.shape[1]
    tokens = x_ref.shape[0]

    @pl.when(step == 0)
    def _():
        acc_ref[...] = jnp.zeros_like(acc_ref)
        x = x_ref[...].astype(F32)
        squares = jnp.sum(x * x, axis=1, keepdims=True)
        given = jnp.concatenate(
            [
                jnp.zeros((1, tokens), F32),
                mix_ref[...],
                index_ref[...].astype(F32),
                jnp.zeros((LANES - 5, tokens), F32),
            ],
            axis=0,
        ).T
        lane = lax.broadcasted_iota(jnp.int32, (tokens, LANES), 1)
        side = jnp.where(lane == SIDE_SQUARES, squares, given)
        side_ref[...] = side
        if rows != tokens:
            side_ref[pl.ds(second_start(rows, lengths_ref), SLOT), :] = side[SLOT:]

    product = jnp.dot(packed_ref[...], w_ref[...], preferred_element_type=F32)
    for k in range(2):
        wanted = side_ref[:rows, SIDE_INDEX + k : SIDE_INDEX + k + 1]
        total = acc_ref[k, :rows, :]
        for s in range(tile // LANES):
            adapter = adapter_of(step * tile + s * LANES)
            part = product[:, s * LANES : (s + 1) * LANES]
            total += jnp.where(adapter == wanted, part, 0.0)
        acc_ref[k, :rows, :] = total

    @pl.when(step == pl.num_programs(0) - 1)
    def _():
        lane = lax.broadcasted_iota(jnp.int32, (tokens, LANES), 1)
        packed = jnp.where(lane < ADAPTER_RANK, fold(acc_ref[0]), fold(acc_ref[1]))
        packed = jnp.where(lane < 2 * ADAPTER_RANK, packed, 0.0)
        squares = side_ref[:, SIDE_SQUARES : SIDE_SQUARES + 1]
        packed = jnp.where(lane == 2 * ADAPTER_RANK, squares, packed)
        low = packed.T[:LOW_ROWS]
        out_ref[...] = low
        for message, w_ref in ((cw_ref, cw_w_ref), (ccw_ref, ccw_w_ref)):
            write_message(message, packed_ref[half:, :], w_ref)
            write_low(message, half, low)


def low_partials(lengths, info, x, packed, weight, index, mix, kv_weight, rows, reach):
    width, columns = weight.shape
    tile = min(1024, columns)
    tokens = x.shape[0]
    pair = 2 * HEAD_WIDTH
    message = (rows // 2 + low_places(tokens, width + pair)[0], width + pair)
    column = [
        pl.BlockSpec((width, pair), lambda j, lengths, info, away=away: (0, info[1, away]))
        for away in (reach - 1, reach)
    ]
    return call(
        functools.partial(low_kernel, rows),
        (shape_of((LOW_ROWS, tokens), F32), shape_of((tokens, LANES), F32))
        + (shape_of(message, BF16),) * 2,
        grid_spec=prefetch(
            2,
            (columns // tile,),
            [
                whole((tokens, width)),
                whole((rows, width)),
                pl.BlockSpec((width, tile), lambda j, *_: (0, j)),
                whole((2, tokens)),
                whole((2, tokens)),
                *column,
            ],
            (whole((LOW_ROWS, tokens)), whole((tokens, LANES)), whole(message), whole(message)),
            [pltpu.VMEM((2, tokens, LANES), F32)],
        ),
    )(lengths, info, x, packed, weight, index.T, mix.T, kv_weight, kv_weight)


def delta_kernel(
    rows, model_width, low_ref, opposite_ref, cw_ref, ccw_ref, side_ref, w_ref, out_ref, inv_ref, co_ref
):
    step = pl.program_id(0)
    tile = w_ref.shape[0]

    @pl.when(step == 0)
    def _():
        tokens = low_ref.shape[1]
        padding = jnp.zeros((LANES - LOW_ROWS, tokens), F32)
        total = low_ref[...] + opposite_ref[...]
        for ref in (cw_ref, ccw_ref):
            total = total + read_low(ref[rows // 2 :, :].astype(F32))
        low = jnp.concatenate([total, padding], axis=0).T
        lane = lax.broadcasted_iota(jnp.int32, (tokens, LANES), 1)
        squares = low[:, 2 * ADAPTER_RANK : 2 * ADAPTER_RANK + 1]
        inverse = lax.rsqrt(squares * (1.0 / model_width) + EPS)
        inv_ref[...] = jnp.broadcast_to(inverse, (tokens, LANES))
        for k in range(2):
            value = fold(jnp.where(lane // ADAPTER_RANK == k, low, 0.0))
            co_ref[k] = value * inverse * side_ref[:, SIDE_MIX + k : SIDE_MIX + k + 1]

    wanted = [side_ref[:rows, SIDE_INDEX + k : SIDE_INDEX + k + 1] for k in range(2)]
    pieces = []
    for s in range(tile // LANES):
        adapter = adapter_of(step * tile + s * LANES)
        piece = jnp.where(adapter == wanted[1], co_ref[1, :rows, :], 0.0)
        piece = jnp.where(adapter == wanted[0], co_ref[0, :rows, :], piece)
        pieces.append(piece.astype(BF16))
    coefficients = jnp.concatenate(pieces, axis=1)
    product = jnp.dot(coefficients, w_ref[...], preferred_element_type=F32)

    @pl.when(step == 0)
    def _():
        out_ref[...] = product

    @pl.when(step > 0)
    def _():
        out_ref[...] += product


def query_delta(lows, messages, side, weight, rows, model_width):
    depth, columns = weight.shape
    tile = min(1024, depth)
    tokens = side.shape[0]
    return call(
        functools.partial(delta_kernel, rows, model_width),
        (shape_of((rows, columns), F32), shape_of((tokens, LANES), F32)),
        grid=(depth // tile,),
        in_specs=[
            whole((LOW_ROWS, tokens)),
            whole((LOW_ROWS, tokens)),
            whole(messages[0].shape),
            whole(messages[1].shape),
            whole((tokens, LANES)),
            pl.BlockSpec((tile, columns), lambda j: (j, 0)),
        ],
        out_specs=(whole((rows, columns)), whole((tokens, LANES))),
        scratch_shapes=[pltpu.VMEM((2, tokens, LANES), F32)],
    )(*lows, *messages, side, weight)


def query_kernel(slots, starts, has_total, info_ref, *refs):
    count = len(slots)
    blocks, weight = refs[:count], refs[count]
    out_ref, x_buf, w_buf, sems, total_sem = refs[-5:]
    half, width = x_buf.shape[1:]

    def copies(i):
        first = pl.multiple_of(info_ref[0, slots[i]] * width, width)
        buf = i % 2
        given = blocks[i].at[pl.ds(starts[i], half), pl.ds(0, width)]
        return [
            pltpu.make_async_copy(given, x_buf.at[buf], sems.at[buf, 0]),
            pltpu.make_async_copy(weight.at[pl.ds(first, width)], w_buf.at[buf], sems.at[buf, 1]),
        ]

    for copy in copies(0):
        copy.start()
    if has_total:
        total_copy = pltpu.make_async_copy(refs[count + 1], out_ref, total_sem)
        total_copy.start()
    for i in range(count):
        if i + 1 < count:
            for copy in copies(i + 1):
                copy.start()
        for copy in copies(i):
            copy.wait()
        product = jnp.dot(x_buf[i % 2], w_buf[i % 2], preferred_element_type=F32)
        if i == 0 and has_total:
            total_copy.wait()
        if i > 0 or has_total:
            out_ref[...] += product
        else:
            out_ref[...] = product


def query_step(info, total, sources, weight, rows):
    half = rows // 2
    columns = weight.shape[1]
    width = weight.shape[0] // info.shape[1]
    operands = [block for _, block, _ in sources] + [weight] + ([] if total is None else [total])
    return call(
        functools.partial(
            query_kernel, [slot for slot, _, _ in sources], [start for _, _, start in sources], total is not None
        ),
        shape_of((half, columns), F32),
        QUERY_WEIGHT,
        grid_spec=prefetch(
            1,
            (1,),
            [pl.BlockSpec(memory_space=pl.ANY)] * len(operands),
            whole((half, columns)),
            [
                pltpu.VMEM((2, half, width), BF16),
                pltpu.VMEM((2, width, columns), BF16),
                pltpu.SemaphoreType.DMA((2, 2)),
                pltpu.SemaphoreType.DMA,
            ],
        ),
    )(info, *operands)


def rotate(values, cosines, sines):
    lane = lax.broadcasted_iota(jnp.int32, values.shape, 1)
    after = pltpu.roll(values, LANES - 1, 1)
    before = pltpu.roll(values, 1, 1)
    other = jnp.where(lane % 2 == 0, after, before)
    return values * cosines + other * sines


def attention_kernel(
    rows, kv_count, info_ref, lengths_ref, total_a_ref, total_b_ref, delta_ref, inv_ref, first_ref,
    second_ref, w_ref, cos_ref, sin_ref, *refs,
):
    kv_refs = refs[:kv_count]
    out_ref, last_s, query_s, kv_s, key_s, value_s, bias_s = refs[kv_count:]
    half = rows // 2
    starts = [0, second_start(rows, lengths_ref)]
    lengths = [lengths_ref[0], lengths_ref[1]]
    inverse = inv_ref[:rows, 0:1]
    row_narrow = lax.broadcasted_iota(jnp.int32, (SLOT, HEAD_WIDTH), 0)

    @pl.when(pl.program_id(0) == 0)
    def _():
        last_s[:half, :] = first_ref[...]
        last_s[half:, :] = second_ref[...]
        for piece in range(2):
            span = slice(piece * half, (piece + 1) * half)
            raw = kv_refs[0][0, span, :].astype(F32)
            for ref in kv_refs[1 + 2 * piece : 3 + 2 * piece]:
                raw = raw + ref[...].astype(F32)
            kv_s[span, :] = raw * inverse[span]
        if rows != 2 * SLOT:
            kv_s[rows:, :] = jnp.zeros((SLOT, 2 * HEAD_WIDTH), F32)
            query_s[rows:, :] = jnp.zeros((SLOT, query_s.shape[1]), F32)
        row = lax.broadcasted_iota(jnp.int32, (SLOT, SLOT), 0)
        col = lax.broadcasted_iota(jnp.int32, (SLOT, SLOT), 1)
        for i in range(2):
            pair = kv_s[pl.ds(starts[i], SLOT), :]
            key_s[i] = rotate(pair[:, :HEAD_WIDTH], cos_ref[...], sin_ref[...]).astype(BF16)
            value = jnp.where(row_narrow < lengths[i], pair[:, HEAD_WIDTH:], 0.0)
            value_s[i] = value.astype(BF16)
            bias_s[i] = jnp.where((col <= row) & (col < lengths[i]), 0.0, -1e30)

    product = jnp.dot(last_s[...], w_ref[...], preferred_element_type=F32)
    for piece, total_ref in enumerate((total_a_ref, total_b_ref)):
        span = slice(piece * half, (piece + 1) * half)
        query_s[span, :] = (total_ref[...] + product[span]) * inverse[span] + delta_ref[span, :]

    factor = math.log2(math.e) / math.sqrt(HEAD_WIDTH)
    for i in range(2):
        for head in range(w_ref.shape[1] // HEAD_WIDTH):
            span = slice(head * HEAD_WIDTH, (head + 1) * HEAD_WIDTH)
            query = query_s[pl.ds(starts[i], SLOT), span]
            query = rotate(query, cos_ref[...], sin_ref[...]).astype(BF16)
            scores = lax.dot_general(
                query, key_s[i], (((1,), (1,)), ((), ())), preferred_element_type=F32
            )
            scores = jnp.where(bias_s[i] == 0.0, scores * factor, -1e30)
            top = jnp.max(scores, axis=1, keepdims=True)
            weights = jnp.exp2(scores - top)
            totals = jnp.sum(weights, axis=1, keepdims=True)
            mixed = jnp.dot(weights.astype(BF16), value_s[i], preferred_element_type=F32)
            mixed = jnp.where(row_narrow < lengths[i], mixed / totals, 0.0)
            out_ref[i * SLOT : (i + 1) * SLOT, span] = mixed.astype(BF16)


def attention(info, lengths, totals, delta, inv, last, last_slot, weight, kv, tables, rows):
    half = rows // 2
    width = weight.shape[0] // info.shape[1]
    columns = weight.shape[1]
    tile = min(2 * HEAD_WIDTH, columns)
    tokens = inv.shape[0]
    pair = 2 * HEAD_WIDTH
    spare = 0 if rows == tokens else SLOT
    return call(
        functools.partial(attention_kernel, rows, len(kv)),
        shape_of((tokens, columns), BF16),
        grid_spec=prefetch(
            2,
            (columns // tile,),
            [
                pl.BlockSpec((half, tile), lambda j, *_: (0, j)),
                pl.BlockSpec((half, tile), lambda j, *_: (0, j)),
                pl.BlockSpec((rows, tile), lambda j, *_: (0, j)),
                whole((tokens, LANES)),
                whole((half, width)),
                whole((half, width)),
                pl.BlockSpec((width, tile), lambda j, info, _: (info[0, last_slot], j)),
                whole((SLOT, HEAD_WIDTH)),
                whole((SLOT, HEAD_WIDTH)),
            ]
            + [pl.BlockSpec((1, rows, pair), lambda j, *_: (0, 0, 0))]
            + [pl.BlockSpec((half, pair), lambda j, *_: (0, width // pair))] * (len(kv) - 1),
            pl.BlockSpec((tokens, tile), lambda j, *_: (0, j)),
            [
                pltpu.VMEM((rows, width), BF16),
                pltpu.VMEM((rows + spare, tile), F32),
                pltpu.VMEM((rows + spare, pair), F32),
                pltpu.VMEM((2, SLOT, HEAD_WIDTH), BF16),
                pltpu.VMEM((2, SLOT, HEAD_WIDTH), BF16),
                pltpu.VMEM((2, SLOT, SLOT), F32),
            ],
        ),
    )(info, lengths, *totals, delta, inv, *last, weight, *tables, *kv)


def rotation_tables():
    lane = jnp.arange(HEAD_WIDTH)
    inverse = jnp.power(F32(ROPE_BASE), -2.0 * (lane // 2).astype(F32) / HEAD_WIDTH)
    angles = jnp.arange(SLOT).astype(F32)[:, None] * inverse[None, :]
    sines = jnp.sin(angles)
    return jnp.cos(angles), jnp.where(lane[None, :] % 2 == 0, -sines, sines)


def ring_order(count):
    if count > 8:
        return list(range(count))
    return list(range(0, count, 2)) + list(range(1, count, 2))[::-1]


def after(value, *earlier):
    return lax.optimization_barrier((value, *earlier))[0]


def program(count, rows, lengths, info, x, scale, wq, wkv, wdown, wup, index, mix):
    order = ring_order(count)
    reach = count // 2
    cw = [(order[i], order[(i + 1) % count]) for i in range(count)]
    ccw = [(b, a) for a, b in cw]
    send_cw = functools.partial(lax.ppermute, axis_name="tensor", perm=cw)
    send_ccw = functools.partial(lax.ppermute, axis_name="tensor", perm=ccw)

    opposite = [(order[i], order[(i + reach) % count]) for i in range(count)]

    cw_first, ccw_first, packed = scale_rows(lengths, info, x, scale, wkv, rows, reach)
    from_cw, from_ccw = [send_cw(cw_first), None], [send_ccw(ccw_first), None]
    low, side, cw_second, ccw_second = low_partials(
        lengths, info, x, packed, wdown, index, mix, wkv, rows, reach
    )
    from_cw[1], from_ccw[1] = send_cw(cw_second), send_ccw(ccw_second)
    low_opposite = lax.ppermute(low, "tensor", opposite)
    near, far = kv_partials(info, after(packed, low), wkv, rows, count)
    done = near
    totals = [None, None]
    delta = inv = None

    def term(away):
        return (near, away) if away < reach else (far, away - reach)

    for step in range(1, reach):
        final = step + 1 == reach
        for piece in range(2):
            got_cw, got_ccw, _ = lax.optimization_barrier((from_cw[piece], from_ccw[piece], done))
            ahead = term(reach - step - piece)
            behind = term(count - reach + step + 1 - piece)
            if final and piece == 1:
                late, _ = lax.optimization_barrier((low_opposite, got_cw))
                delta, inv = query_delta(
                    (low, late), (got_cw, got_ccw), side, wup, rows, wq.shape[0]
                )
            if not final:
                if piece == 0:
                    got_cw, got_ccw = add_terms([got_cw, got_ccw], [ahead, behind], rows)
                else:
                    got_cw, got_ccw = add_terms_low([got_cw, got_ccw], [ahead, behind], low, rows)
                from_cw[piece], from_ccw[piece] = send_cw(got_cw), send_ccw(got_ccw)
            elif piece == 0:
                (got_cw,) = add_terms([got_cw], [ahead], rows)
                from_cw[0], from_ccw[0] = send_cw(got_cw), got_ccw
            else:
                (got_ccw,) = add_terms_low([got_ccw], [behind], low, rows)
                from_cw[1], from_ccw[1] = got_cw, send_ccw(got_ccw)
            sources = [(count - step, got_cw, 0), (step, got_ccw, 0)]
            if step == 1:
                sources = [(0, packed, piece * (rows // 2))] + sources
            totals[piece] = query_step(info, totals[piece], sources, wq, rows)
            done = totals[piece]
    kv = (near, from_cw[0], from_ccw[0], from_cw[1], from_ccw[1])
    return attention(
        info, lengths, totals, delta, inv, (from_cw[0], from_ccw[1]), reach, wq, kv,
        rotation_tables(), rows,
    )


def shards(count, x, scale, wq, wkv, wdown, wup, index, mix, lengths):
    shard = lax.axis_index("tensor")
    order = ring_order(count)
    heads = wq.shape[1] // HEAD_WIDTH
    table = np.zeros((count, 2, count), np.int32)
    for place, device in enumerate(order):
        for i in range(count):
            other = order[(place + i) % count]
            table[device, 0, i] = other
            table[device, 1, i] = other * heads // (QUERY_HEADS // KV_HEADS)
    info = lax.dynamic_index_in_dim(jnp.asarray(table), shard, 0, keepdims=False)
    return program(count, x.shape[0], lengths, info, x, scale, wq, wkv, wdown, wup, index, mix)


def solution(mesh):
    placed = (
        P(("groups", "replica"), "tensor"),
        P(),
        P(None, "tensor"),
        P("tensor", None),
        P("tensor", None),
        P(None, "tensor"),
        P(("groups", "replica"), None),
        P(("groups", "replica"), None),
        P(("groups", "replica")),
    )
    return jax.shard_map(
        functools.partial(shards, mesh.shape["tensor"]),
        mesh=mesh,
        in_specs=placed,
        out_specs=P(("groups", "replica"), "tensor"),
        check_vma=False,
    )
```

time: 435 us -> 135 us (0.31)
  waiting for transfers between devices: 297 us -> 14.5 us
  Pallas kernels: 0 us -> 91.4 us
  matrix products: 55.1 us -> 0 us
  local copies, waits for them, and re-layouts: 37.1 us -> 6.19 us
  other arithmetic: 31 us -> 1.29 us
  starting transfers between devices: 0.04 us -> 20.7 us
  between operations: 13.7 us -> 0.14 us
    psum x1 -> x0, waiting for transfers between devices: 167 us -> none  [shards(): kv_raw, low = lax.psum((kv_part, low_part), 'tensor')]
    all_gather x1 -> x0, waiting for transfers between devices: 129 us -> none  [shards(): gathered = lax.all_gather(activations, 'tensor', axis=1, tiled=True)]
    pallas_call x0 -> x17, Pallas kernels: none -> 91.4 us  [the longest x6 33.9 us: query_step(): call(functools.partial(query_kernel, [slot for slot, _, _ in sources], [s...]
    dot_general x8 -> x0, matrix products: 55.1 us -> none  [the longest x1 14.7 us: shards(): jnp.dot(normalized_input, query_weight, preferred_element_type=jnp.float32)]
    ppermute x0 -> x15, starting transfers between devices: none -> 20.7 us  [the longest x8 8.1 us: program(): from_cw[piece], from_ccw[piece] = (send_cw(got_cw), send_ccw(got_ccw))]
    ppermute x0 -> x15, waiting for transfers between devices: none -> 14.5 us  [the longest x8 14.5 us: program(): from_cw[piece], from_ccw[piece] = (send_cw(got_cw), send_ccw(got_ccw))]
    another operation x4 -> x0, other arithmetic: 14.2 us -> none
    reshape x3 -> x0, local copies, waits for them, and re-layouts: 13.2 us -> none  [the longest x1 10.4 us: shards(): reduced_rank_rows = jnp.dot(normalized_local_input, adapter_down_weight,...]
  transfers between devices with their start and end apart: 2 -> 15, of which waited for: 2 -> 7; matrix products, arithmetic and copies ran while one was open for 0% -> 1% of each run, Pallas kernels for 0% -> 56%
where the time goes in v2:
time: 135 us; the launch traced here: 134 us
  Pallas kernels  91.4 us (68%)
  starting transfers between devices  20.7 us (15%)
  waiting for transfers between devices  14.5 us (11%)
  local copies, waits for them, and re-layouts  6.19 us (5%)
    pallas_call x6, Pallas kernels, query_step(): call(functools.partial(query_kernel, [slot for slot, _, _ in sources], [s...  33.9 us
    ppermute x8, waiting for transfers between devices, program(): from_cw[piece], from_ccw[piece] = (send_cw(got_cw), send_ccw(got_ccw))  14.5 us
    pallas_call x1, Pallas kernels, attention(): call(functools.partial(attention_kernel, rows, len(kv)), shape_of((tokens...  12 us
    pallas_call x1, Pallas kernels, low_partials(): call(functools.partial(low_kernel, rows), (shape_of((LOW_ROWS, tokens), F...  11.4 us
    pallas_call x1, Pallas kernels, query_delta(): call(functools.partial(delta_kernel, rows, model_width), (shape_of((rows,...  10.5 us
    ppermute x8, starting transfers between devices, program(): from_cw[piece], from_ccw[piece] = (send_cw(got_cw), send_ccw(got_ccw))  8.1 us
    pallas_call x3, Pallas kernels, add_terms_low(): call(functools.partial(add_low_kernel, half), (shape_of(shape, BF16),) *...  7.29 us
    pallas_call x1, Pallas kernels, kv_partials(): call(kv_kernel, (out, out), grid_spec=prefetch(1, (count // 2,), [whole((...  6.77 us
  transfers between devices with their start and end apart: 15, of which 7 were waited for; matrix products, arithmetic and copies ran while one was open for 1% of the time, Pallas kernels for 56%

profile of v2, /device:TPU:0, one launch (start us, length us, event | category | flops | bytes accessed | tf_op | source)
XLA Modules:
  0.0 134.2 jit_solution(17199344324548185262)
XLA Ops:
  1.3 4.1 %shard_map.100 = (bf16[256,1280]{1,0:T(8,128)(2,1)}, bf16[256,1280]{1,0:T(8,128)(2,1)}, bf16[512,1024]{1,0:T(8,128)(2,1)}) custom-call(s32[2]{0:T(128)} %lengths_ref.5, s32[2,8]{1,0:T(2,128)} %dynamic-slice_bitcast_fusion.info_ref, bf16[512,1024]{1,0:T(8,128)(2,1)} %x_ref.3, f32[1,8192]{1,0:T(1,128)} %bitcast.5, bf16[1024,2048]{1,0:T(8,128)(2,1)} %far_w_ref.1, ...), custom_call_target="tpu_custom_call" | custom-call | bytes 1000 | tf_op jit(solution)/shard_map/pallas_call | solution.py:95
  5.4 3.0 %collective-permute-start = (bf16[256,1280]{1,0:T(8,128)(2,1)}, bf16[256,1280]{1,0:T(8,128)(2,1)}, u32[]{:S(2)}, u32[]{:S(2)}) collective-permute-start(bf16[256,1280]{1,0:T(8,128)(2,1)} %get-tuple-element.38), channel_id=1, source_target_pairs={{0,2},{2,4},{4,6},{6,7},{7,5},{5,3},{3,1},{1,0},{8,10},{10,12},{12... | collective-permute-start | bytes 1966088 | tf_op jit(solution)/shard_map/ppermute | solution.py:585
  8.4 11.4 %shard_map.101 = (f32[40,512]{1,0:T(8,128)}, f32[512,128]{1,0:T(8,128)}, bf16[272,1280]{1,0:T(8,128)(2,1)}, bf16[272,1280]{1,0:T(8,128)(2,1)}) custom-call(s32[2]{0:T(128)} %lengths_ref.5, s32[2,8]{1,0:T(2,128)} %dynamic-slice_bitcast_fusion.info_ref, bf16[512,1024]{1,0:T(8,128)(2,1)} %x_ref.3, bf16[512,1024]{1,0:T(8,128)(2,1)} %get-tuple-element.42.packed_ref.x_ref.refs_0_, ...), custom_call_target="tpu_custom_call" | custom-call | bytes 1000 | tf_op jit(solution)/shard_map/pallas_call | solution.py:307
  19.8 5.0 %collective-permute-start.12 = (f32[40,512]{1,0:T(8,128)}, f32[40,512]{1,0:T(8,128)S(1)}, u32[]{:S(2)}, u32[]{:S(2)}) collective-permute-start(f32[40,512]{1,0:T(8,128)} %get-tuple-element.41.low_ref), channel_id=1, source_target_pairs={{0,7},{2,5},{4,3},{6,1},{7,0},{5,2},{3,4},{1,6},{8,15},{10,13},{12... | collective-permute-start | bytes 245768 | tf_op jit(solution)/shard_map/ppermute | solution.py:590
  24.8 2.0 %collective-permute-start.5 = (bf16[272,1280]{1,0:T(8,128)(2,1)}, bf16[272,1280]{1,0:T(8,128)(2,1)S(1)}, u32[]{:S(2)}, u32[]{:S(2)}) collective-permute-start(bf16[272,1280]{1,0:T(8,128)(2,1)} %get-tuple-element.50), channel_id=1, source_target_pairs={{2,0},{4,2},{6,4},{7,6},{5,7},{3,5},{1,3},{0,1},{10,8},{12,10},{14... | collective-permute-start | bytes 2088968 | tf_op jit(solution)/shard_map/ppermute | solution.py:589
  26.8 6.8 %shard_map.102 = (bf16[4,512,256]{2,1,0:T(8,128)(2,1)}, bf16[4,512,256]{2,1,0:T(8,128)(2,1)}) custom-call(s32[2,8]{1,0:T(2,128)} %dynamic-slice_bitcast_fusion.info_ref, bf16[512,1024]{1,0:T(8,128)(2,1)} %get-tuple-element.42.packed_ref.x_ref.refs_0_, bf16[1024,2048]{1,0:T(8,128)(2,1)} %far_w_ref.1, bf16[1024,2048]{1,0:T(8,128)(2,1)} %far_w_ref.1), custom_call_target="tpu_custom_call" | custom-call | bytes 1000 | tf_op jit(solution)/shard_map/pallas_call | solution.py:215
  34.9 1.9 %shard_map.103 = (bf16[256,1280]{1,0:T(8,128)(2,1)}, bf16[256,1280]{1,0:T(8,128)(2,1)}) custom-call(bf16[256,1280]{1,0:T(8,128)(2,1)} %collective-permute-done.refs_0_, bf16[256,1280]{1,0:T(8,128)(2,1)} %collective-permute-done.1.refs_1_, ...), custom_call_target="tpu_custom_call", output_to_operand_aliasing={{0}: (0, {}), {1}: (1, {})} | custom-call | bytes 1000 | tf_op jit(solution)/shard_map/pallas_call | solution.py:167
  36.8 2.0 %collective-permute-start.3 = (bf16[256,1280]{1,0:T(8,128)(2,1)}, bf16[256,1280]{1,0:T(8,128)(2,1)}, u32[]{:S(2)}, u32[]{:S(2)}) collective-permute-start(bf16[256,1280]{1,0:T(8,128)(2,1)} %get-tuple-element.48.refs_2_), channel_id=1, source_target_pairs={{2,0},{4,2},{6,4},{7,6},{5,7},{3,5},{1,3},{0,1},{10,8},{12,10},{14... | collective-permute-start | bytes 1966088 | tf_op jit(solution)/shard_map/ppermute | solution.py:615
  38.8 6.3 %shard_map.104.refs_3_ = f32[256,1024]{1,0:T(8,128)} custom-call(s32[2,8]{1,0:T(2,128)} %dynamic-slice_bitcast_fusion.info_ref, bf16[512,1024]{1,0:T(8,128)(2,1)} %get-tuple-element.42.packed_ref.x_ref.refs_0_, bf16[256,1280]{1,0:T(8,128)(2,1)} %get-tuple-element.47.refs_1_, bf16[256,1280]{1,0:T(8,128)(2,1)} %get-tuple-element.48.refs_2_, ...), custom_call_target="tpu_custom_call" | custom-call | flops 9200000000 | bytes 1000 | tf_op jit(solution)/shard_map/pallas_call | solution.py:430
  46.9 2.6 %shard_map.105 = (bf16[272,1280]{1,0:T(8,128)(2,1)}, bf16[272,1280]{1,0:T(8,128)(2,1)}) custom-call(f32[40,512]{1,0:T(8,128)} %get-tuple-element.41.low_ref, bf16[272,1280]{1,0:T(8,128)(2,1)} %copy-done.3, bf16[272,1280]{1,0:T(8,128)(2,1)} %copy-done.4, bf16[4,512,256]{2,1,0:T(8,128)(2,1)} %get-tuple-element.43.refs_2_.refs_1_.refs_0_, ...), custom_call_target="tpu_custom_call" | custom-call | bytes 1000 | tf_op jit(solution)/shard_map/pallas_call | solution.py:195
  51.6 6.4 %shard_map.106.refs_3_ = f32[256,1024]{1,0:T(8,128)} custom-call(s32[2,8]{1,0:T(2,128)} %dynamic-slice_bitcast_fusion.info_ref, bf16[512,1024]{1,0:T(8,128)(2,1)} %get-tuple-element.42.packed_ref.x_ref.refs_0_, bf16[272,1280]{1,0:T(8,128)(2,1)} %get-tuple-element.53.refs_1_, bf16[272,1280]{1,0:T(8,128)(2,1)} %get-tuple-element.54.refs_2_, ...), custom_call_target="tpu_custom_call" | custom-call | flops 9200000000 | bytes 1000 | tf_op jit(solution)/shard_map/pallas_call | solution.py:430
  60.3 2.0 %collective-permute-start.6 = (bf16[256,1280]{1,0:T(8,128)(2,1)}, bf16[256,1280]{1,0:T(8,128)(2,1)}, u32[]{:S(2)}, u32[]{:S(2)}) collective-permute-start(bf16[256,1280]{1,0:T(8,128)(2,1)} %get-tuple-element.57.refs_0_), channel_id=1, source_target_pairs={{0,2},{2,4},{4,6},{6,7},{7,5},{5,3},{3,1},{1,0},{8,10},{10,12},{12... | collective-permute-start | bytes 1966088 | tf_op jit(solution)/shard_map/ppermute | solution.py:615
  62.4 5.3 %shard_map.108.refs_3_ = f32[256,1024]{1,0:T(8,128)} custom-call(s32[2,8]{1,0:T(2,128)} %dynamic-slice_bitcast_fusion.info_ref, bf16[256,1280]{1,0:T(8,128)(2,1)} %get-tuple-element.57.refs_0_, bf16[256,1280]{1,0:T(8,128)(2,1)} %get-tuple-element.58.refs_1_, bf16[8192,1024]{1,0:T(8,128)(2,1)} %w_ref.5, f32[256,1024]{1,0:T(8,128)} %shard_map.104.refs_3_), custom_call_target="tpu_custom_call" | custom-call | flops 9200000000 | bytes 1000 | tf_op jit(solution)/shard_map/pallas_call | solution.py:430
  67.6 5.3 %collective-permute-done.8.refs_0_ = bf16[272,1280]{1,0:T(8,128)(2,1)S(1)} collective-permute-done((bf16[272,1280]{1,0:T(8,128)(2,1)}, bf16[272,1280]{1,0:T(8,128)(2,1)S(1)}, u32[]{:S(2)}, u32[]{:S(2)}) %collective-permute-start.8) | collective-permute-done | bytes 696352 | tf_op jit(solution)/shard_map/ppermute | solution.py:615
  74.7 2.6 %shard_map.109 = (bf16[272,1280]{1,0:T(8,128)(2,1)}, bf16[272,1280]{1,0:T(8,128)(2,1)}) custom-call(f32[40,512]{1,0:T(8,128)} %get-tuple-element.41.low_ref, bf16[272,1280]{1,0:T(8,128)(2,1)} %copy-done.5, bf16[272,1280]{1,0:T(8,128)(2,1)} %copy-done.6, bf16[4,512,256]{2,1,0:T(8,128)(2,1)} %get-tuple-element.43.refs_2_.refs_1_.refs_0_, ...), custom_call_target="tpu_custom_call" | custom-call | bytes 1000 | tf_op jit(solution)/shard_map/pallas_call | solution.py:195
  79.3 5.3 %shard_map.110.refs_3_ = f32[256,1024]{1,0:T(8,128)} custom-call(s32[2,8]{1,0:T(2,128)} %dynamic-slice_bitcast_fusion.info_ref, bf16[272,1280]{1,0:T(8,128)(2,1)} %get-tuple-element.61.refs_0_, bf16[272,1280]{1,0:T(8,128)(2,1)} %get-tuple-element.62.refs_1_, bf16[8192,1024]{1,0:T(8,128)(2,1)} %w_ref.5, f32[256,1024]{1,0:T(8,128)} %shard_map.106.refs_3_), custom_call_target="tpu_custom_call" | custom-call | flops 9200000000 | bytes 1000 | tf_op jit(solution)/shard_map/pallas_call | solution.py:430
  84.6 2.5 %collective-permute-done.6.refs_0_ = bf16[256,1280]{1,0:T(8,128)(2,1)} collective-permute-done((bf16[256,1280]{1,0:T(8,128)(2,1)}, bf16[256,1280]{1,0:T(8,128)(2,1)}, u32[]{:S(2)}, u32[]{:S(2)}) %collective-permute-start.6) | collective-permute-done | bytes 655392 | tf_op jit(solution)/shard_map/ppermute | solution.py:615
  89.1 2.0 %collective-permute-start.13 = (bf16[256,1280]{1,0:T(8,128)(2,1)}, bf16[256,1280]{1,0:T(8,128)(2,1)}, u32[]{:S(2)}, u32[]{:S(2)}) collective-permute-start(bf16[256,1280]{1,0:T(8,128)(2,1)} %shard_map.111.refs_0_), channel_id=1, source_target_pairs={{0,2},{2,4},{4,6},{6,7},{7,5},{5,3},{3,1},{1,0},{8,10},{10,12},{12... | collective-permute-start | bytes 1966088 | tf_op jit(solution)/shard_map/ppermute | solution.py:618
  91.1 5.3 %shard_map.112.total_a_ref = f32[256,1024]{1,0:T(8,128)} custom-call(s32[2,8]{1,0:T(2,128)} %dynamic-slice_bitcast_fusion.info_ref, bf16[256,1280]{1,0:T(8,128)(2,1)} %shard_map.111.refs_0_, bf16[256,1280]{1,0:T(8,128)(2,1)} %collective-permute-done.7.refs_1_.refs_2_, bf16[8192,1024]{1,0:T(8,128)(2,1)} %w_ref.5, f32[256,1024]{1,0:T(8,128)} %shard_map.108.refs_3_), custom_call_target="tpu_custom_call" | custom-call | flops 9200000000 | bytes 1000 | tf_op jit(solution)/shard_map/pallas_call | solution.py:430
  96.4 5.5 %collective-permute-done.10.refs_0_.cw_ref.refs_3_ = bf16[272,1280]{1,0:T(8,128)(2,1)S(1)} collective-permute-done((bf16[272,1280]{1,0:T(8,128)(2,1)}, bf16[272,1280]{1,0:T(8,128)(2,1)S(1)}, u32[]{:S(2)}, u32[]{:S(2)}) %collective-permute-start.10) | collective-permute-done | bytes 696352 | tf_op jit(solution)/shard_map/ppermute | solution.py:615
  102.8 2.1 %shard_map.113.refs_1_ = bf16[272,1280]{1,0:T(8,128)(2,1)} custom-call(f32[40,512]{1,0:T(8,128)} %get-tuple-element.41.low_ref, bf16[272,1280]{1,0:T(8,128)(2,1)} %copy-done.2, bf16[4,512,256]{2,1,0:T(8,128)(2,1)} %get-tuple-element.46.refs_3_.refs_1_), custom_call_target="tpu_custom_call" | custom-call | bytes 1000 | tf_op jit(solution)/shard_map/pallas_call | solution.py:195
  105.5 10.5 %shard_map.115 = (f32[512,1024]{1,0:T(8,128)}, f32[512,128]{1,0:T(8,128)}) custom-call(f32[40,512]{1,0:T(8,128)} %get-tuple-element.41.low_ref, f32[40,512]{1,0:T(8,128)} %copy-done.7, bf16[272,1280]{1,0:T(8,128)(2,1)} %copy-done, bf16[272,1280]{1,0:T(8,128)(2,1)} %copy-done.2, f32[512,128]{1,0:T(8,128)} %get-tuple-element.68.side_ref, bf16[4096,1024]{1,0:T(8,128)(2,1)} %w_ref.4), custom_call_target="tpu_custom_call" | custom-call | bytes 1000 | tf_op jit(solution)/shard_map/pallas_call | solution.py:373
  116.0 5.3 %shard_map.114.total_b_ref = f32[256,1024]{1,0:T(8,128)} custom-call(s32[2,8]{1,0:T(2,128)} %dynamic-slice_bitcast_fusion.info_ref, bf16[272,1280]{1,0:T(8,128)(2,1)} %copy-done, bf16[272,1280]{1,0:T(8,128)(2,1)} %shard_map.113.refs_1_, bf16[8192,1024]{1,0:T(8,128)(2,1)} %w_ref.5, f32[256,1024]{1,0:T(8,128)} %shard_map.110.refs_3_), custom_call_target="tpu_custom_call" | custom-call | flops 9200000000 | bytes 1000 | tf_op jit(solution)/shard_map/pallas_call | solution.py:430
  122.2 12.0 %shard_map.116 = bf16[512,1024]{1,0:T(8,128)(2,1)} custom-call(s32[2,8]{1,0:T(2,128)} %dynamic-slice_bitcast_fusion.info_ref, s32[2]{0:T(128)} %lengths_ref.5, f32[256,1024]{1,0:T(8,128)} %shard_map.112.total_a_ref, f32[256,1024]{1,0:T(8,128)} %shard_map.114.total_b_ref, f32[512,1024]{1,0:T(8,128)} %get-tuple-element.69.delta_ref, ...), custom_call_target="tpu_custom_call" | custom-call | bytes 1000 | tf_op jit(solution)/shard_map/pallas_call | solution.py:524
  (44 shorter events, 16.9 us)
Async XLA Ops:
  5.4 29.5 %collective-permute-start = (bf16[256,1280]{1,0:T(8,128)(2,1)}, bf16[256,1280]{1,0:T(8,128)(2,1)}, u32[]{:S(2)}, u32[]{:S(2)}) collective-permute-start(bf16[256,1280]{1,0:T(8,128)(2,1)} %get-tuple-element.38), channel_id=1, source_target_pairs={{0,2},{2,4},{4,6},{6,7},{7,5},{5,3},{3,1},{1,0},{8,10},{10,12},{12... | collective-permute-start | bytes 1966088 | tf_op jit(solution)/shard_map/ppermute | solution.py:585
  8.4 26.5 %collective-permute-start.1 = (bf16[256,1280]{1,0:T(8,128)(2,1)}, bf16[256,1280]{1,0:T(8,128)(2,1)}, u32[]{:S(2)}, u32[]{:S(2)}) collective-permute-start(bf16[256,1280]{1,0:T(8,128)(2,1)} %get-tuple-element.39), channel_id=1, source_target_pairs={{2,0},{4,2},{6,4},{7,6},{5,7},{3,5},{1,3},{0,1},{10,8},{12,10},{14... | collective-permute-start | bytes 1966088 | tf_op jit(solution)/shard_map/ppermute | solution.py:585
  19.8 85.1 %collective-permute-start.12 = (f32[40,512]{1,0:T(8,128)}, f32[40,512]{1,0:T(8,128)S(1)}, u32[]{:S(2)}, u32[]{:S(2)}) collective-permute-start(f32[40,512]{1,0:T(8,128)} %get-tuple-element.41.low_ref), channel_id=1, source_target_pairs={{0,7},{2,5},{4,3},{6,1},{7,0},{5,2},{3,4},{1,6},{8,15},{10,13},{12... | collective-permute-start | bytes 245768 | tf_op jit(solution)/shard_map/ppermute | solution.py:590
  24.8 20.4 %collective-permute-start.4 = (bf16[272,1280]{1,0:T(8,128)(2,1)}, bf16[272,1280]{1,0:T(8,128)(2,1)S(1)}, u32[]{:S(2)}, u32[]{:S(2)}) collective-permute-start(bf16[272,1280]{1,0:T(8,128)(2,1)} %get-tuple-element.49), channel_id=1, source_target_pairs={{0,2},{2,4},{4,6},{6,7},{7,5},{5,3},{3,1},{1,0},{8,10},{10,12},{12... | collective-permute-start | bytes 2088968 | tf_op jit(solution)/shard_map/ppermute | solution.py:589
  24.8 20.4 %collective-permute-start.5 = (bf16[272,1280]{1,0:T(8,128)(2,1)}, bf16[272,1280]{1,0:T(8,128)(2,1)S(1)}, u32[]{:S(2)}, u32[]{:S(2)}) collective-permute-start(bf16[272,1280]{1,0:T(8,128)(2,1)} %get-tuple-element.50), channel_id=1, source_target_pairs={{2,0},{4,2},{6,4},{7,6},{5,7},{3,5},{1,3},{0,1},{10,8},{12,10},{14... | collective-permute-start | bytes 2088968 | tf_op jit(solution)/shard_map/ppermute | solution.py:589
  36.8 21.3 %collective-permute-start.2 = (bf16[256,1280]{1,0:T(8,128)(2,1)}, bf16[256,1280]{1,0:T(8,128)(2,1)}, u32[]{:S(2)}, u32[]{:S(2)}) collective-permute-start(bf16[256,1280]{1,0:T(8,128)(2,1)} %get-tuple-element.47.refs_1_), channel_id=1, source_target_pairs={{0,2},{2,4},{4,6},{6,7},{7,5},{5,3},{3,1},{1,0},{8,10},{10,12},{12... | collective-permute-start | bytes 1966088 | tf_op jit(solution)/shard_map/ppermute | solution.py:615
  36.8 21.7 %collective-permute-start.3 = (bf16[256,1280]{1,0:T(8,128)(2,1)}, bf16[256,1280]{1,0:T(8,128)(2,1)}, u32[]{:S(2)}, u32[]{:S(2)}) collective-permute-start(bf16[256,1280]{1,0:T(8,128)(2,1)} %get-tuple-element.48.refs_2_), channel_id=1, source_target_pairs={{2,0},{4,2},{6,4},{7,6},{5,7},{3,5},{1,3},{0,1},{10,8},{12,10},{14... | collective-permute-start | bytes 1966088 | tf_op jit(solution)/shard_map/ppermute | solution.py:615
  45.2 0.9 copy-start.3
  46.0 0.9 copy-start.4
  49.5 23.4 %collective-permute-start.8 = (bf16[272,1280]{1,0:T(8,128)(2,1)}, bf16[272,1280]{1,0:T(8,128)(2,1)S(1)}, u32[]{:S(2)}, u32[]{:S(2)}) collective-permute-start(bf16[272,1280]{1,0:T(8,128)(2,1)} %get-tuple-element.53.refs_1_), channel_id=1, source_target_pairs={{0,2},{2,4},{4,6},{6,7},{7,5},{5,3},{3,1},{1,0},{8,10},{10,12},{12... | collective-permute-start | bytes 2088968 | tf_op jit(solution)/shard_map/ppermute | solution.py:615
  49.8 23.5 %collective-permute-start.9 = (bf16[272,1280]{1,0:T(8,128)(2,1)}, bf16[272,1280]{1,0:T(8,128)(2,1)S(1)}, u32[]{:S(2)}, u32[]{:S(2)}) collective-permute-start(bf16[272,1280]{1,0:T(8,128)(2,1)} %get-tuple-element.54.refs_2_), channel_id=1, source_target_pairs={{2,0},{4,2},{6,4},{7,6},{5,7},{3,5},{1,3},{0,1},{10,8},{12,10},{14... | collective-permute-start | bytes 2088968 | tf_op jit(solution)/shard_map/ppermute | solution.py:615
  60.3 26.8 %collective-permute-start.6 = (bf16[256,1280]{1,0:T(8,128)(2,1)}, bf16[256,1280]{1,0:T(8,128)(2,1)}, u32[]{:S(2)}, u32[]{:S(2)}) collective-permute-start(bf16[256,1280]{1,0:T(8,128)(2,1)} %get-tuple-element.57.refs_0_), channel_id=1, source_target_pairs={{0,2},{2,4},{4,6},{6,7},{7,5},{5,3},{3,1},{1,0},{8,10},{10,12},{12... | collective-permute-start | bytes 1966088 | tf_op jit(solution)/shard_map/ppermute | solution.py:615
  62.3 25.1 %collective-permute-start.7 = (bf16[256,1280]{1,0:T(8,128)(2,1)}, bf16[256,1280]{1,0:T(8,128)(2,1)}, u32[]{:S(2)}, u32[]{:S(2)}) collective-permute-start(bf16[256,1280]{1,0:T(8,128)(2,1)} %get-tuple-element.58.refs_1_), channel_id=1, source_target_pairs={{2,0},{4,2},{6,4},{7,6},{5,7},{3,5},{1,3},{0,1},{10,8},{12,10},{14... | collective-permute-start | bytes 1966088 | tf_op jit(solution)/shard_map/ppermute | solution.py:615
  72.9 0.9 copy-start.5
  73.8 0.9 copy-start.6
  77.2 24.7 %collective-permute-start.10 = (bf16[272,1280]{1,0:T(8,128)(2,1)}, bf16[272,1280]{1,0:T(8,128)(2,1)S(1)}, u32[]{:S(2)}, u32[]{:S(2)}) collective-permute-start(bf16[272,1280]{1,0:T(8,128)(2,1)} %get-tuple-element.61.refs_0_), channel_id=1, source_target_pairs={{0,2},{2,4},{4,6},{6,7},{7,5},{5,3},{3,1},{1,0},{8,10},{10,12},{12... | collective-permute-start | bytes 2088968 | tf_op jit(solution)/shard_map/ppermute | solution.py:615
  78.7 23.2 %collective-permute-start.11 = (bf16[272,1280]{1,0:T(8,128)(2,1)}, bf16[272,1280]{1,0:T(8,128)(2,1)S(1)}, u32[]{:S(2)}, u32[]{:S(2)}) collective-permute-start(bf16[272,1280]{1,0:T(8,128)(2,1)} %get-tuple-element.62.refs_1_), channel_id=1, source_target_pairs={{2,0},{4,2},{6,4},{7,6},{5,7},{3,5},{1,3},{0,1},{10,8},{12,10},{14... | collective-permute-start | bytes 2088968 | tf_op jit(solution)/shard_map/ppermute | solution.py:615
  89.1 32.3 %collective-permute-start.13 = (bf16[256,1280]{1,0:T(8,128)(2,1)}, bf16[256,1280]{1,0:T(8,128)(2,1)}, u32[]{:S(2)}, u32[]{:S(2)}) collective-permute-start(bf16[256,1280]{1,0:T(8,128)(2,1)} %shard_map.111.refs_0_), channel_id=1, source_target_pairs={{0,2},{2,4},{4,6},{6,7},{7,5},{5,3},{3,1},{1,0},{8,10},{10,12},{12... | collective-permute-start | bytes 1966088 | tf_op jit(solution)/shard_map/ppermute | solution.py:618
  101.9 3.5 %copy-start = (bf16[272,1280]{1,0:T(8,128)(2,1)}, bf16[272,1280]{1,0:T(8,128)(2,1)S(1)}, u32[]{:S(2)}) copy-start(bf16[272,1280]{1,0:T(8,128)(2,1)S(1)} %collective-permute-done.10.refs_0_.cw_ref.refs_3_) | copy-start | bytes 2088964
  101.9 0.9 copy-start.2
  104.9 0.6 copy-start.7
  104.9 16.5 %collective-permute-start.14 = (bf16[272,1280]{1,0:T(8,128)(2,1)}, bf16[272,1280]{1,0:T(8,128)(2,1)S(1)}, u32[]{:S(2)}, u32[]{:S(2)}) collective-permute-start(bf16[272,1280]{1,0:T(8,128)(2,1)} %shard_map.113.refs_1_), channel_id=1, source_target_pairs={{2,0},{4,2},{6,4},{7,6},{5,7},{3,5},{1,3},{0,1},{10,8},{12,10},{14... | collective-permute-start | bytes 2088968 | tf_op jit(solution)/shard_map/ppermute | solution.py:621
  121.4 0.9 copy-start.1

commit v3 on v2

v3 whole, which is shorter than its diff:
```python
import functools
import math

import jax
import jax.numpy as jnp
import numpy as np
from jax import lax
from jax.experimental import pallas as pl
from jax.experimental.pallas import tpu as pltpu
from jax.sharding import PartitionSpec as P

QUERY_HEADS = 64
KV_HEADS = 8
HEAD_WIDTH = 128
ADAPTER_RANK = 16
SLOT = 256
LANES = 128
LOW_ROWS = 40

EPS = 1e-05
ROPE_BASE = 500000.0

SIDE_SQUARES = 0
SIDE_MIX = 1
SIDE_INDEX = 3

DEPTH = 3
CHUNK = 512
HEADS_AT_ONCE = 8
DELTA_TILE = 1024
ADD_WEIGHT = 8.0
QUERY_WEIGHT = 8.0
VMEM_LIMIT = 64 * 1024 * 1024 - 64 * 1024
F32 = jnp.float32
BF16 = jnp.bfloat16


def call(kernel, out_shape, microseconds=0.0, **kwargs):
    return pl.pallas_call(
        kernel,
        out_shape=out_shape,
        compiler_params=pltpu.CompilerParams(vmem_limit_bytes=VMEM_LIMIT),
        cost_estimate=pl.CostEstimate(
            flops=int(1.15e9 * microseconds), bytes_accessed=1000, transcendentals=0
        ),
        **kwargs,
    )


def whole(shape):
    return pl.BlockSpec(shape, lambda *_: (0,) * len(shape))


def shape_of(shape, dtype):
    return jax.ShapeDtypeStruct(shape, dtype)


def prefetch(count, grid, in_specs, out_specs, scratch_shapes=()):
    return pltpu.PrefetchScalarGridSpec(
        num_scalar_prefetch=count,
        grid=grid,
        in_specs=in_specs,
        out_specs=out_specs,
        scratch_shapes=scratch_shapes,
    )


def second_start(rows, lengths_ref):
    if rows == 2 * SLOT:
        return SLOT
    return pl.multiple_of((lengths_ref[0] + 15) // 16 * 16, 16)


def write_message(message, block, w_ref):
    half, width = block.shape
    message[:half, :width] = block
    product = jnp.dot(block, w_ref[...], preferred_element_type=F32)
    message[:half, width:] = product.astype(BF16)


def scale_kernel(
    rows, lengths_ref, info_ref, x_ref, scale_ref, cw_w_ref, ccw_w_ref, cw_ref, ccw_ref, packed
):
    packed[...] = (x_ref[...].astype(F32) * scale_ref[...]).astype(BF16)
    if rows != 2 * SLOT:
        packed[pl.ds(second_start(rows, lengths_ref), SLOT), :] = packed[SLOT:, :]
    block = packed[: rows // 2, :]
    write_message(cw_ref, block, cw_w_ref)
    write_message(ccw_ref, block, ccw_w_ref)


def scale_rows(lengths, info, x, scale, weight, rows, reach):
    tokens, width = x.shape
    pair = 2 * HEAD_WIDTH
    message = (rows // 2, width + pair)
    column = [
        pl.BlockSpec((width, pair), lambda j, lengths, info, away=away: (0, info[1, away]))
        for away in (reach, reach + 1)
    ]
    return call(
        functools.partial(scale_kernel, rows),
        (shape_of(message, BF16),) * 2 + (shape_of((tokens, width), BF16),),
        grid_spec=prefetch(
            2,
            (1,),
            [
                whole((tokens, width)),
                pl.BlockSpec((1, width), lambda j, lengths, info: (0, info[0, 0])),
                *column,
            ],
            (whole(message),) * 2 + (whole((tokens, width)),),
        ),
    )(lengths, info, x, scale.reshape(1, -1), weight, weight)


def low_places(tokens, full):
    if full >= 2 * tokens + SLOT:
        second = (slice(0, ADAPTER_RANK), slice(tokens, 2 * tokens))
        squares = (0, slice(2 * tokens, 2 * tokens + SLOT))
        extra = ADAPTER_RANK
    else:
        second = (slice(ADAPTER_RANK, 2 * ADAPTER_RANK), slice(0, tokens))
        squares = (2 * ADAPTER_RANK, slice(0, SLOT))
        extra = 3 * ADAPTER_RANK
    return extra, (slice(0, ADAPTER_RANK), slice(0, tokens)), second, squares


def read_low(region):
    tokens = 2 * SLOT
    _, first, second, (row, lanes) = low_places(tokens, region.shape[1])
    squares = jnp.concatenate(
        [region[row + i : row + i + 1, lanes] + region[row + 2 + i : row + 3 + i, lanes] for i in range(2)],
        axis=1,
    )
    return jnp.concatenate(
        [region[first], region[second], squares, jnp.zeros((LOW_ROWS - 33, tokens), F32)], axis=0
    )


def write_low(message, half, low):
    tokens = 2 * SLOT
    extra, first, second, (row, lanes) = low_places(tokens, message.shape[1])
    message[half : half + extra, :] = jnp.zeros((extra, message.shape[1]), BF16)
    squares = low[2 * ADAPTER_RANK : 2 * ADAPTER_RANK + 1, :]
    rounded = squares.astype(BF16)
    rest = (squares - rounded.astype(F32)).astype(BF16)
    for place, value in ((first, low[:ADAPTER_RANK]), (second, low[ADAPTER_RANK : 2 * ADAPTER_RANK])):
        span = slice(half + place[0].start, half + place[0].stop)
        message[span, place[1]] = value.astype(BF16)
    block = jnp.concatenate(
        [rounded[:, :SLOT], rounded[:, SLOT:], rest[:, :SLOT], rest[:, SLOT:]]
        + [jnp.zeros((ADAPTER_RANK - 4, SLOT), BF16)],
        axis=0,
    )
    message[half + row : half + row + ADAPTER_RANK, lanes] = block


def add_kernel(info_ref, block_ref, *refs):
    count = len(refs) // 3
    for i in range(count):
        own = jnp.dot(block_ref[...], refs[count + i][...], preferred_element_type=F32)
        refs[2 * count + i][...] = (refs[i][...].astype(F32) + own).astype(BF16)


def add_terms(info, messages, aways, packed, weight, rows):
    half = rows // 2
    width = weight.shape[0]
    full = messages[0].shape[1]
    pair = 2 * HEAD_WIDTH
    lanes = pl.BlockSpec((half, pair), lambda j, info: (0, full // pair - 1))
    columns = [
        pl.BlockSpec((width, pair), lambda j, info, away=away: (0, info[1, away]))
        for away in aways
    ]
    count = len(messages)
    return call(
        add_kernel,
        (shape_of((half, full), BF16),) * count,
        ADD_WEIGHT,
        grid_spec=prefetch(
            1,
            (1,),
            [pl.BlockSpec((half, width), lambda j, info: (0, 0))] + [lanes] * count + columns,
            (lanes,) * count,
        ),
        input_output_aliases={2 + i: i for i in range(count)},
    )(info, packed, *messages, *[weight] * count)


def add_low_kernel(half, info_ref, block_ref, low_ref, *refs):
    count = len(refs) // 3
    pair = 2 * HEAD_WIDTH
    around = low_ref[...]
    for i in range(count):
        given, w_ref, out = refs[i], refs[count + i], refs[2 * count + i]
        full = given.shape[1]
        out[:half, : full - pair] = given[:half, : full - pair]
        own = jnp.dot(block_ref[...], w_ref[...], preferred_element_type=F32)
        out[:half, full - pair :] = (given[:half, full - pair :].astype(F32) + own).astype(BF16)
        sums = read_low(given[half:, :].astype(F32))
        around = around + sums
        write_low(out, half, sums + low_ref[...])
    refs[3 * count][...] = around


def add_terms_low(info, messages, aways, packed, weight, low, rows):
    half = rows // 2
    width = weight.shape[0]
    shape = messages[0].shape
    pair = 2 * HEAD_WIDTH
    columns = [
        pl.BlockSpec((width, pair), lambda j, info, away=away: (0, info[1, away]))
        for away in aways
    ]
    count = len(messages)
    return call(
        functools.partial(add_low_kernel, half),
        (shape_of(shape, BF16),) * count + (shape_of(low.shape, F32),),
        ADD_WEIGHT,
        grid_spec=prefetch(
            1,
            (1,),
            [pl.BlockSpec((half, width), lambda j, info: (1, 0)), whole(low.shape)]
            + [whole(shape)] * count
            + columns,
            (whole(shape),) * count + (whole(low.shape),),
        ),
    )(info, packed, low, *messages, *[weight] * count)


def chosen_group(index):
    rows = index.shape[0]
    lane = lax.broadcasted_iota(jnp.int32, (rows, LANES), 1)
    return index - (lane // ADAPTER_RANK).astype(F32)


def fold(value):
    shift = ADAPTER_RANK
    while shift < LANES:
        value = value + pltpu.roll(value, shift, 1)
        shift *= 2
    return value


def low_kernel(
    rows, lengths_ref, info_ref, x_ref, packed_ref, w_ref, index_ref, mix_ref, cw_w_ref, ccw_w_ref,
    own_w_ref, out_ref, side_ref, cw_ref, ccw_ref, own_ref, acc_ref, group_ref,
):
    step = pl.program_id(0)
    half = rows // 2
    tile = w_ref.shape[1]
    tokens = x_ref.shape[0]

    @pl.when(step == 0)
    def _():
        acc_ref[...] = jnp.zeros_like(acc_ref)
        x = x_ref[...].astype(F32)
        squares = jnp.sum(x * x, axis=1, keepdims=True)
        given = jnp.concatenate(
            [
                jnp.zeros((1, tokens), F32),
                mix_ref[...],
                index_ref[...].astype(F32),
                jnp.zeros((LANES - 5, tokens), F32),
            ],
            axis=0,
        ).T
        lane = lax.broadcasted_iota(jnp.int32, (tokens, LANES), 1)
        side = jnp.where(lane == SIDE_SQUARES, squares, given)
        side_ref[...] = side
        if rows != tokens:
            side_ref[pl.ds(second_start(rows, lengths_ref), SLOT), :] = side[SLOT:]
        for k in range(2):
            group_ref[k] = chosen_group(side_ref[:, SIDE_INDEX + k : SIDE_INDEX + k + 1])

    chunk = min(CHUNK, tile)

    def part(n, carry):
        first = pl.multiple_of(n * chunk, chunk)
        product = jnp.dot(
            packed_ref[...], w_ref[:, pl.ds(first, chunk)], preferred_element_type=F32
        )
        for k in range(2):
            total = acc_ref[k, :rows, :]
            for s in range(chunk // LANES):
                group = (step * tile + first + s * LANES) // ADAPTER_RANK
                here = group_ref[k, :rows, :] == group.astype(F32)
                total += jnp.where(here, product[:, s * LANES : (s + 1) * LANES], 0.0)
            acc_ref[k, :rows, :] = total
        return carry

    lax.fori_loop(0, tile // chunk, part, 0)

    @pl.when(step == pl.num_programs(0) - 1)
    def _():
        lane = lax.broadcasted_iota(jnp.int32, (tokens, LANES), 1)
        packed = jnp.where(lane < ADAPTER_RANK, fold(acc_ref[0]), fold(acc_ref[1]))
        packed = jnp.where(lane < 2 * ADAPTER_RANK, packed, 0.0)
        squares = side_ref[:, SIDE_SQUARES : SIDE_SQUARES + 1]
        packed = jnp.where(lane == 2 * ADAPTER_RANK, squares, packed)
        low = packed.T[:LOW_ROWS]
        out_ref[...] = low
        for message, w_ref in ((cw_ref, cw_w_ref), (ccw_ref, ccw_w_ref)):
            write_message(message, packed_ref[half:, :], w_ref)
            write_low(message, half, low)
        own = jnp.dot(packed_ref[...], own_w_ref[...], preferred_element_type=F32)
        own_ref[...] = own.astype(BF16)


def low_partials(lengths, info, x, packed, weight, index, mix, kv_weight, rows, reach):
    width, columns = weight.shape
    tile = min(1024, columns)
    tokens = x.shape[0]
    pair = 2 * HEAD_WIDTH
    message = (rows // 2 + low_places(tokens, width + pair)[0], width + pair)
    column = [
        pl.BlockSpec((width, pair), lambda j, lengths, info, away=away: (0, info[1, away]))
        for away in (reach - 1, reach, 0)
    ]
    return call(
        functools.partial(low_kernel, rows),
        (shape_of((LOW_ROWS, tokens), F32), shape_of((tokens, LANES), F32))
        + (shape_of(message, BF16),) * 2
        + (shape_of((rows, pair), BF16),),
        grid_spec=prefetch(
            2,
            (columns // tile,),
            [
                whole((tokens, width)),
                whole((rows, width)),
                pl.BlockSpec((width, tile), lambda j, *_: (0, j)),
                whole((2, tokens)),
                whole((2, tokens)),
                *column,
            ],
            (whole((LOW_ROWS, tokens)), whole((tokens, LANES)), whole(message), whole(message))
            + (whole((rows, pair)),),
            [pltpu.VMEM((2, tokens, LANES), F32)] * 2,
        ),
    )(lengths, info, x, packed, weight, index.T, mix.T, kv_weight, kv_weight, kv_weight)


def delta_kernel(
    half, model_width, low_ref, opposite_ref, cw_ref, ccw_ref, side_ref, w_ref, out_ref, inv_ref,
    co_ref, group_ref, ends, sems,
):
    step = pl.program_id(0)
    tile = w_ref.shape[0]

    @pl.when(step == 0)
    def _():
        copies = [
            pltpu.make_async_copy(ref.at[pl.ds(half, ends.shape[1])], ends.at[i], sems.at[i])
            for i, ref in enumerate((cw_ref, ccw_ref))
        ]
        for copy in copies:
            copy.start()
        for k in range(2):
            group_ref[k] = chosen_group(side_ref[:, SIDE_INDEX + k : SIDE_INDEX + k + 1])
        for copy in copies:
            copy.wait()
        tokens = low_ref.shape[1]
        sums = low_ref[...] + opposite_ref[...]
        for i in range(2):
            sums = sums + read_low(ends[i].astype(F32))
        padding = jnp.zeros((LANES - LOW_ROWS, tokens), F32)
        low = jnp.concatenate([sums, padding], axis=0).T
        lane = lax.broadcasted_iota(jnp.int32, (tokens, LANES), 1)
        squares = low[:, 2 * ADAPTER_RANK : 2 * ADAPTER_RANK + 1]
        inverse = lax.rsqrt(squares * (1.0 / model_width) + EPS)
        inv_ref[...] = jnp.broadcast_to(inverse, (tokens, LANES))
        for k in range(2):
            value = fold(jnp.where(lane // ADAPTER_RANK == k, low, 0.0))
            co_ref[k] = value * inverse * side_ref[:, SIDE_MIX + k : SIDE_MIX + k + 1]
        out_ref[...] = jnp.zeros_like(out_ref)

    pieces = []
    for s in range(tile // LANES):
        group = ((step * tile + s * LANES) // ADAPTER_RANK).astype(F32)
        piece = jnp.where(group_ref[0] == group, co_ref[0], 0.0)
        piece = jnp.where(group_ref[1] == group, co_ref[1], piece)
        pieces.append(piece.astype(BF16))
    coefficients = jnp.concatenate(pieces, axis=1)
    out_ref[...] += jnp.dot(coefficients, w_ref[...], preferred_element_type=F32)


def query_delta(low, opposite, cw, ccw, side, weight, model_width):
    depth, columns = weight.shape
    tile = min(DELTA_TILE, depth)
    tokens = side.shape[0]
    anywhere = pl.BlockSpec(memory_space=pl.ANY)
    extra = low_places(tokens, cw.shape[1])[0]
    return call(
        functools.partial(delta_kernel, tokens // 2, model_width),
        (shape_of((tokens, columns), F32), shape_of((tokens, LANES), F32)),
        QUERY_WEIGHT,
        grid=(depth // tile,),
        in_specs=[whole(low.shape), whole(low.shape), anywhere, anywhere, whole(side.shape)]
        + [pl.BlockSpec((tile, columns), lambda j: (j, 0))],
        out_specs=(whole((tokens, columns)), whole((tokens, LANES))),
        scratch_shapes=[
            pltpu.VMEM((2, tokens, LANES), F32),
            pltpu.VMEM((2, tokens, LANES), F32),
            pltpu.VMEM((2, extra, cw.shape[1]), BF16),
            pltpu.SemaphoreType.DMA((2,)),
        ],
    )(low, opposite, cw, ccw, side, weight)


def product_kernel(slots, starts, has_total, place, info_ref, *refs):
    refs = list(refs)
    count = len(slots)
    blocks = [refs.pop(0) for _ in range(count)]
    weight = refs.pop(0)
    total_ref = refs.pop(0) if has_total else None
    delta_ref, inv_ref = (None, None) if place is None else (refs.pop(0), refs.pop(0))
    out_ref, x_buf, w_buf, sems, total_sems, *refs = refs
    depth, half, width = x_buf.shape
    columns = w_buf.shape[2]
    chunk = min(CHUNK, columns)

    def copies(i):
        buf = i % depth
        first = pl.multiple_of(info_ref[0, slots[i]] * width, width)
        block = blocks[i].at[pl.ds(starts[i], half), pl.ds(0, width)]
        return [
            pltpu.make_async_copy(weight.at[pl.ds(first, width)], w_buf.at[buf], sems.at[buf, 0]),
            pltpu.make_async_copy(block, x_buf.at[buf], sems.at[buf, 1]),
        ]

    for i in range(min(depth - 1, count)):
        for copy in copies(i):
            copy.start()
    if has_total:
        total_copy = pltpu.make_async_copy(total_ref, out_ref, total_sems.at[0])
        total_copy.start()
    if place is not None:
        given = delta_ref.at[pl.ds(place * half, half)]
        delta_copy = pltpu.make_async_copy(given, refs[0], total_sems.at[1])
        delta_copy.start()
    for i in range(count):
        buf = i % depth
        if i + depth - 1 < count:
            for copy in copies(i + depth - 1):
                copy.start()
        for copy in copies(i):
            copy.wait()
        if i == 0 and has_total:
            total_copy.wait()
        if i == count - 1 and place is not None:
            delta_copy.wait()
        for first in range(0, columns, chunk):
            span = slice(first, first + chunk)
            value = jnp.dot(x_buf[buf], w_buf[buf, :, span], preferred_element_type=F32)
            if i > 0 or has_total:
                value = out_ref[:, span] + value
            if i == count - 1 and place is not None:
                value = value * inv_ref[:, 0:1] + refs[0][:, span]
            out_ref[:, span] = value


def product(info, total, sources, weight, half, ending=None, place=None):
    columns = weight.shape[1]
    width = weight.shape[0] // info.shape[1]
    operands = [block for _, block, _ in sources]
    operands += [weight] + ([] if total is None else [total])
    in_specs = [pl.BlockSpec(memory_space=pl.ANY)] * len(operands)
    scratch = [
        pltpu.VMEM((DEPTH, half, width), BF16),
        pltpu.VMEM((DEPTH, width, columns), BF16),
        pltpu.SemaphoreType.DMA((DEPTH, 2)),
        pltpu.SemaphoreType.DMA((2,)),
    ]
    if ending is not None:
        operands += ending
        in_specs += [pl.BlockSpec(memory_space=pl.ANY)]
        in_specs += [pl.BlockSpec((half, LANES), lambda j, info: (place, 0))]
        scratch += [pltpu.VMEM((half, columns), F32)]
    slots = [slot for slot, _, _ in sources]
    starts = [start for _, _, start in sources]
    return call(
        functools.partial(product_kernel, slots, starts, total is not None, place),
        shape_of((half, columns), F32),
        QUERY_WEIGHT,
        grid_spec=prefetch(1, (1,), in_specs, whole((half, columns)), scratch),
    )(info, *operands)


def rotate(values, cosines, sines):
    lane = lax.broadcasted_iota(jnp.int32, values.shape, 1)
    after = pltpu.roll(values, LANES - 1, 1)
    before = pltpu.roll(values, 1, 1)
    other = jnp.where(lane % 2 == 0, after, before)
    return values * cosines + other * sines


def attention_kernel(
    prompt, info_ref, lengths_ref, total_ref, inv_ref, last_ref, w_ref, cos_ref, sin_ref, own_ref,
    cw_ref, ccw_ref, out_ref, key_s, value_s, bias_s,
):
    length = lengths_ref[prompt]
    inverse = inv_ref[:, 0:1]
    row_narrow = lax.broadcasted_iota(jnp.int32, (SLOT, HEAD_WIDTH), 0)

    @pl.when(pl.program_id(0) == 0)
    def _():
        pair = own_ref[...].astype(F32) + cw_ref[...].astype(F32) + ccw_ref[...].astype(F32)
        pair = pair * inverse
        key_s[...] = rotate(pair[:, :HEAD_WIDTH], cos_ref[...], sin_ref[...]).astype(BF16)
        value_s[...] = pair[:, HEAD_WIDTH:].astype(BF16)
        row = lax.broadcasted_iota(jnp.int32, (SLOT, SLOT), 0)
        col = lax.broadcasted_iota(jnp.int32, (SLOT, SLOT), 1)
        bias_s[...] = jnp.where((col <= row) & (col < length), 0.0, -1e30)

    product = jnp.dot(last_ref[...], w_ref[...], preferred_element_type=F32)
    queries = total_ref[...] + product * inverse
    factor = math.log2(math.e) / math.sqrt(HEAD_WIDTH)
    for head in range(w_ref.shape[1] // HEAD_WIDTH):
        span = slice(head * HEAD_WIDTH, (head + 1) * HEAD_WIDTH)
        query = rotate(queries[:, span], cos_ref[...], sin_ref[...]).astype(BF16)
        scores = lax.dot_general(
            query, key_s[...], (((1,), (1,)), ((), ())), preferred_element_type=F32
        )
        scores = scores * factor + bias_s[...]
        top = jnp.max(scores, axis=1, keepdims=True)
        weights = jnp.exp2(scores - top)
        totals = jnp.sum(weights, axis=1, keepdims=True)
        mixed = jnp.dot(weights.astype(BF16), value_s[...], preferred_element_type=F32)
        mixed = jnp.where(row_narrow < length, mixed * (1.0 / totals), 0.0)
        out_ref[:, span] = mixed.astype(BF16)


def attention(info, lengths, total, inv, last, last_slot, weight, kv, tables, prompt, done=None):
    width = weight.shape[0] // info.shape[1]
    columns = weight.shape[1]
    tile = min(HEADS_AT_ONCE * HEAD_WIDTH, columns)
    pair = 2 * HEAD_WIDTH
    own, cw, ccw = kv
    kernel = functools.partial(attention_kernel, prompt)
    operands = [total, inv, last, weight, *tables, own, cw, ccw]
    in_specs = [
        pl.BlockSpec((SLOT, tile), lambda j, *_: (0, j)),
        pl.BlockSpec((SLOT, LANES), lambda j, *_: (prompt, 0)),
        pl.BlockSpec((SLOT, width), lambda j, *_: (0, 0)),
        pl.BlockSpec((width, tile), lambda j, info, _: (info[0, last_slot], j)),
        whole((SLOT, HEAD_WIDTH)),
        whole((SLOT, HEAD_WIDTH)),
        pl.BlockSpec((SLOT, pair), lambda j, *_: (prompt, 0)),
        pl.BlockSpec((SLOT, pair), lambda j, *_: (0, width // pair)),
        pl.BlockSpec((SLOT, pair), lambda j, *_: (0, width // pair)),
    ]
    aliases = {}
    if done is not None:
        inner = kernel

        def kernel(*refs):
            return inner(*refs[:11], *refs[12:])

        operands.append(done)
        in_specs.append(pl.BlockSpec(memory_space=pl.ANY))
        aliases = {11: 0}
    return call(
        kernel,
        shape_of((2 * SLOT, columns), BF16),
        grid_spec=prefetch(
            2,
            (columns // tile,),
            in_specs,
            pl.BlockSpec((SLOT, tile), lambda j, *_: (prompt, j)),
            [
                pltpu.VMEM((SLOT, HEAD_WIDTH), BF16),
                pltpu.VMEM((SLOT, HEAD_WIDTH), BF16),
                pltpu.VMEM((SLOT, SLOT), F32),
            ],
        ),
        input_output_aliases=aliases,
    )(info, lengths, *operands)


def rotation_tables():
    lane = jnp.arange(HEAD_WIDTH)
    inverse = jnp.power(F32(ROPE_BASE), -2.0 * (lane // 2).astype(F32) / HEAD_WIDTH)
    angles = jnp.arange(SLOT).astype(F32)[:, None] * inverse[None, :]
    sines = jnp.sin(angles)
    return jnp.cos(angles), jnp.where(lane[None, :] % 2 == 0, -sines, sines)


def ring_order(count):
    if count > 8:
        return list(range(count))
    return list(range(0, count, 2)) + list(range(1, count, 2))[::-1]


def after(value, *earlier):
    return lax.optimization_barrier((value, *earlier))[0]


def program(count, rows, lengths, info, x, scale, wq, wkv, wdown, wup, index, mix):
    order = ring_order(count)
    reach = count // 2
    cw = [(order[i], order[(i + 1) % count]) for i in range(count)]
    ccw = [(b, a) for a, b in cw]
    send_cw = functools.partial(lax.ppermute, axis_name="tensor", perm=cw)
    send_ccw = functools.partial(lax.ppermute, axis_name="tensor", perm=ccw)

    opposite = [(order[i], order[(i + reach) % count]) for i in range(count)]

    cw_first, ccw_first, packed = scale_rows(lengths, info, x, scale, wkv, rows, reach)
    from_cw, from_ccw = [send_cw(cw_first), None], [send_ccw(ccw_first), None]
    low, side, cw_second, ccw_second, own = low_partials(
        lengths, info, x, packed, wdown, index, mix, wkv, rows, reach
    )
    from_cw[1], from_ccw[1] = send_cw(cw_second), send_ccw(ccw_second)
    done = low
    totals = [None, None]
    half = rows // 2
    pending = [[(0, packed, piece * half)] for piece in range(2)]

    for step in range(1, reach):
        final = step + 1 == reach
        for piece in range(2):
            got_cw, got_ccw, _ = lax.optimization_barrier((from_cw[piece], from_ccw[piece], done))
            aways = [reach - step - piece, count - reach + step + 1 - piece]
            ends = got_cw, got_ccw
            if final:
                moving, aways = [ends[piece]], [aways[piece]]
            else:
                moving = list(ends)
            if piece == 0:
                moved = add_terms(info, moving, aways, packed, wkv, rows)
            else:
                *moved, around = add_terms_low(info, moving, aways, packed, wkv, low, rows)
            if final and piece == 0:
                moved = [*moved, got_ccw]
            elif final:
                moved = [got_cw, *moved]
            if not (final and piece == 1):
                from_cw[piece] = send_cw(moved[0])
            else:
                from_cw[piece] = moved[0]
            if not (final and piece == 0):
                from_ccw[piece] = send_ccw(moved[1])
            else:
                from_ccw[piece] = moved[1]
            done = moved[piece]
            pending[piece] += [(count - step, moved[0], 0), (step, moved[1], 0)]
            if step == 1 and piece == 1:
                opposite_low = lax.ppermute(around, "tensor", opposite)
            if step == reach - 2 and piece == 1:
                late, _ = lax.optimization_barrier((opposite_low, done))
                delta, inv = query_delta(low, late, *ends, side, wup, wq.shape[0])
                done = delta
            else:
                ending = (delta, inv) if final else None
                totals[piece] = product(
                    info, totals[piece], pending[piece], wq, half, ending, piece if final else None
                )
                pending[piece] = []
                done = totals[piece]
    tables = rotation_tables()
    context = None
    for prompt in range(2):
        last = (from_cw[0], from_ccw[1])[prompt]
        kv = (own, from_cw[prompt], from_ccw[prompt])
        context = attention(
            info, lengths, totals[prompt], inv, last, reach, wq, kv, tables, prompt, context
        )
    return context


def shards(count, x, scale, wq, wkv, wdown, wup, index, mix, lengths):
    shard = lax.axis_index("tensor")
    order = ring_order(count)
    heads = wq.shape[1] // HEAD_WIDTH
    table = np.zeros((count, 2, count), np.int32)
    for place, device in enumerate(order):
        for i in range(count):
            other = order[(place + i) % count]
            table[device, 0, i] = other
            table[device, 1, i] = other * heads // (QUERY_HEADS // KV_HEADS)
    info = lax.dynamic_index_in_dim(jnp.asarray(table), shard, 0, keepdims=False)
    return program(count, x.shape[0], lengths, info, x, scale, wq, wkv, wdown, wup, index, mix)


def solution(mesh):
    placed = (
        P(("groups", "replica"), "tensor"),
        P(),
        P(None, "tensor"),
        P("tensor", None),
        P("tensor", None),
        P(None, "tensor"),
        P(("groups", "replica"), None),
        P(("groups", "replica"), None),
        P(("groups", "replica")),
    )
    return jax.shard_map(
        functools.partial(shards, mesh.shape["tensor"]),
        mesh=mesh,
        in_specs=placed,
        out_specs=P(("groups", "replica"), "tensor"),
        check_vma=False,
    )
```

time: 135 us -> 127 us (0.941)
  local copies, waits for them, and re-layouts: 6.19 us -> 1.27 us
  waiting for transfers between devices: 14.5 us -> 10.8 us
  Pallas kernels: 91.4 us -> 92.8 us
    ppermute x11, waiting for transfers between devices: 14.5 us -> 4.33 us  [the longest x5 3.75 us: program(): from_ccw[piece] = send_ccw(moved[1])]
    ppermute x2, waiting for transfers between devices: 0.01 us -> 5.97 us  [program(): from_cw[1], from_ccw[1] = (send_cw(cw_second), send_ccw(ccw_second))]
    unnamed x16 -> x0, local copies, waits for them, and re-layouts: 4.93 us -> none
    pallas_call x3, Pallas kernels: 7.29 us -> 11.6 us  [add_terms_low(): call(functools.partial(add_low_kernel, half), (shape_of(shape, BF16),) *...]
    pallas_call x12 -> x11, Pallas kernels: 68.6 us -> 64.4 us  [the longest x5 32.2 us: product(): call(functools.partial(product_kernel, slots, starts, total is not None,...]
  transfers between devices with their start and end apart: 15 -> 15, of which waited for: 7 -> 6; matrix products, arithmetic and copies ran while one was open for 1% -> 1% of each run, Pallas kernels for 56% -> 65%
where the time goes in v3:
time: 127 us
  Pallas kernels  92.8 us (73%)
  starting transfers between devices  20.3 us (16%)
  waiting for transfers between devices  10.8 us (9%)
  other arithmetic  1.29 us (1%)
  local copies, waits for them, and re-layouts  1.27 us (1%)
    pallas_call x5, Pallas kernels, product(): call(functools.partial(product_kernel, slots, starts, total is not None,...  32.2 us
    pallas_call x1, Pallas kernels, low_partials(): call(functools.partial(low_kernel, rows), (shape_of((LOW_ROWS, tokens), F...  12.6 us
    pallas_call x2, Pallas kernels, attention(): call(kernel, shape_of((2 * SLOT, columns), BF16), grid_spec=prefetch(2, (...  12.3 us
    pallas_call x3, Pallas kernels, add_terms_low(): call(functools.partial(add_low_kernel, half), (shape_of(shape, BF16),) *...  11.6 us
    pallas_call x1, Pallas kernels, query_delta(): call(functools.partial(delta_kernel, tokens // 2, model_width), (shape_of...  10.3 us
    pallas_call x3, Pallas kernels, add_terms(): call(add_kernel, (shape_of((half, full), BF16),) * count, ADD_WEIGHT, gri...  9.63 us
    ppermute x5, starting transfers between devices, program(): from_cw[piece] = send_cw(moved[0])  7.26 us
    ppermute x2, waiting for transfers between devices, program(): from_cw[1], from_ccw[1] = (send_cw(cw_second), send_ccw(ccw_second))  5.97 us
  transfers between devices with their start and end apart: 15, of which 6 were waited for; matrix products, arithmetic and copies ran while one was open for 1% of the time, Pallas kernels for 65%

profile of v3, /device:TPU:0, one launch (start us, length us, event | category | flops | bytes accessed | tf_op | source)
XLA Modules:
  0.0 126.6 jit_solution(12294268941119277554)
XLA Ops:
  1.3 4.1 %shard_map.100 = (bf16[256,1280]{1,0:T(8,128)(2,1)}, bf16[256,1280]{1,0:T(8,128)(2,1)}, bf16[512,1024]{1,0:T(8,128)(2,1)}) custom-call(s32[2]{0:T(128)} %refs_1_.5, s32[2,8]{1,0:T(2,128)} %dynamic-slice_bitcast_fusion.info_ref.refs_0_, bf16[512,1024]{1,0:T(8,128)(2,1)} %x_ref.3, f32[1,8192]{1,0:T(1,128)} %bitcast.5, bf16[1024,2048]{1,0:T(8,128)(2,1)} %refs_1_.4, ...), custom_call_target="tpu_custom_call" | custom-call | bytes 1000 | tf_op jit(solution)/shard_map/pallas_call | solution.py:100
  5.4 3.0 %collective-permute-start.2 = (bf16[256,1280]{1,0:T(8,128)(2,1)}, bf16[256,1280]{1,0:T(8,128)(2,1)}, u32[]{:S(2)}, u32[]{:S(2)}) collective-permute-start(bf16[256,1280]{1,0:T(8,128)(2,1)} %get-tuple-element.42), channel_id=1, source_target_pairs={{0,2},{2,4},{4,6},{6,7},{7,5},{5,3},{3,1},{1,0},{8,10},{10,12},{12... | collective-permute-start | bytes 1966088 | tf_op jit(solution)/shard_map/ppermute | solution.py:609
  8.4 12.6 %shard_map.101 = (f32[40,512]{1,0:T(8,128)}, f32[512,128]{1,0:T(8,128)}, bf16[272,1280]{1,0:T(8,128)(2,1)}, bf16[272,1280]{1,0:T(8,128)(2,1)}, bf16[512,256]{1,0:T(8,128)(2,1)}) custom-call(s32[2]{0:T(128)} %refs_1_.5, s32[2,8]{1,0:T(2,128)} %dynamic-slice_bitcast_fusion.info_ref.refs_0_, bf16[512,1024]{1,0:T(8,128)(2,1)} %x_ref.3, ...), custom_call_target="tpu_custom_call" | custom-call | bytes 1000 | tf_op jit(solution)/shard_map/pallas_call | solution.py:320
  21.1 2.0 %collective-permute-start = (bf16[272,1280]{1,0:T(8,128)(2,1)}, bf16[272,1280]{1,0:T(8,128)(2,1)}, u32[]{:S(2)}, u32[]{:S(2)}) collective-permute-start(bf16[272,1280]{1,0:T(8,128)(2,1)} %get-tuple-element.40), channel_id=1, source_target_pairs={{0,2},{2,4},{4,6},{6,7},{7,5},{5,3},{3,1},{1,0},{8,10},{10,12},{12... | collective-permute-start | bytes 2088968 | tf_op jit(solution)/shard_map/ppermute | solution.py:613
  24.9 3.4 %shard_map.102 = (bf16[256,1280]{1,0:T(8,128)(2,1)}, bf16[256,1280]{1,0:T(8,128)(2,1)}) custom-call(s32[2,8]{1,0:T(2,128)} %dynamic-slice_bitcast_fusion.info_ref.refs_0_, bf16[512,1024]{1,0:T(8,128)(2,1)} %get-tuple-element.38.packed_ref.block_ref.refs_0_, ...), custom_call_target="tpu_custom_call", output_to_operand_aliasing={{0}: (2, {}), {1}: (3, {})} | custom-call | flops 9200000000 | bytes 1000 | tf_op jit(solution)/shard_map/pallas_call | solution.py:176
  30.3 5.7 %shard_map.103.refs_3_ = f32[256,1024]{1,0:T(8,128)} custom-call(s32[2,8]{1,0:T(2,128)} %dynamic-slice_bitcast_fusion.info_ref.refs_0_, bf16[512,1024]{1,0:T(8,128)(2,1)} %get-tuple-element.38.packed_ref.block_ref.refs_0_, bf16[256,1280]{1,0:T(8,128)(2,1)} %get-tuple-element.46.refs_1_, bf16[256,1280]{1,0:T(8,128)(2,1)} %get-tuple-element.47.refs_2_, ...), custom_call_target="tpu_custom_call" | custom-call | flops 9200000000 | bytes 1000 | tf_op jit(solution)/shard_map/pallas_call | solution.py:481
  36.0 3.9 %collective-permute-done.refs_0_ = bf16[272,1280]{1,0:T(8,128)(2,1)} collective-permute-done((bf16[272,1280]{1,0:T(8,128)(2,1)}, bf16[272,1280]{1,0:T(8,128)(2,1)}, u32[]{:S(2)}, u32[]{:S(2)}) %collective-permute-start) | collective-permute-done | bytes 696352 | tf_op jit(solution)/shard_map/ppermute | solution.py:613
  39.9 2.0 %collective-permute-done.1.refs_1_ = bf16[272,1280]{1,0:T(8,128)(2,1)} collective-permute-done((bf16[272,1280]{1,0:T(8,128)(2,1)}, bf16[272,1280]{1,0:T(8,128)(2,1)}, u32[]{:S(2)}, u32[]{:S(2)}) %collective-permute-start.1) | collective-permute-done | bytes 696352 | tf_op jit(solution)/shard_map/ppermute | solution.py:613
  42.0 4.1 %shard_map.104 = (bf16[272,1280]{1,0:T(8,128)(2,1)}, bf16[272,1280]{1,0:T(8,128)(2,1)}, f32[40,512]{1,0:T(8,128)}) custom-call(s32[2,8]{1,0:T(2,128)} %dynamic-slice_bitcast_fusion.info_ref.refs_0_, bf16[512,1024]{1,0:T(8,128)(2,1)} %get-tuple-element.38.packed_ref.block_ref.refs_0_, f32[40,512]{1,0:T(8,128)} %get-tuple-element.39.low_ref, ...), custom_call_target="tpu_custom_call" | custom-call | flops 9200000000 | bytes 1000 | tf_op jit(solution)/shard_map/pallas_call | solution.py:216
  48.1 3.4 %collective-permute-start.12 = (f32[40,512]{1,0:T(8,128)}, f32[40,512]{1,0:T(8,128)}, u32[]{:S(2)}, u32[]{:S(2)}) collective-permute-start(f32[40,512]{1,0:T(8,128)} %get-tuple-element.60), channel_id=1, source_target_pairs={{0,7},{2,5},{4,3},{6,1},{7,0},{5,2},{3,4},{1,6},{8,15},{10,13},{12... | collective-permute-start | bytes 245768 | tf_op jit(solution)/shard_map/ppermute | solution.py:648
  51.5 5.7 %shard_map.105.refs_5_ = f32[256,1024]{1,0:T(8,128)} custom-call(s32[2,8]{1,0:T(2,128)} %dynamic-slice_bitcast_fusion.info_ref.refs_0_, bf16[512,1024]{1,0:T(8,128)(2,1)} %get-tuple-element.38.packed_ref.block_ref.refs_0_, bf16[272,1280]{1,0:T(8,128)(2,1)} %get-tuple-element.50.refs_1_, bf16[272,1280]{1,0:T(8,128)(2,1)} %get-tuple-element.51.refs_2_, ...), custom_call_target="tpu_custom_call" | custom-call | flops 9200000000 | bytes 1000 | tf_op jit(solution)/shard_map/pallas_call | solution.py:481
  57.2 3.3 %shard_map.106 = (bf16[256,1280]{1,0:T(8,128)(2,1)}, bf16[256,1280]{1,0:T(8,128)(2,1)}) custom-call(s32[2,8]{1,0:T(2,128)} %dynamic-slice_bitcast_fusion.info_ref.refs_0_, bf16[512,1024]{1,0:T(8,128)(2,1)} %get-tuple-element.38.packed_ref.block_ref.refs_0_, ...), custom_call_target="tpu_custom_call", output_to_operand_aliasing={{0}: (2, {}), {1}: (3, {})} | custom-call | flops 9200000000 | bytes 1000 | tf_op jit(solution)/shard_map/pallas_call | solution.py:176
  62.6 5.8 %shard_map.107.refs_3_ = f32[256,1024]{1,0:T(8,128)} custom-call(s32[2,8]{1,0:T(2,128)} %dynamic-slice_bitcast_fusion.info_ref.refs_0_, bf16[256,1280]{1,0:T(8,128)(2,1)} %get-tuple-element.54.refs_0_, bf16[256,1280]{1,0:T(8,128)(2,1)} %get-tuple-element.55.refs_1_, bf16[8192,1024]{1,0:T(8,128)(2,1)} %refs_5_.1, f32[256,1024]{1,0:T(8,128)} %shard_map.103.refs_3_), custom_call_target="tpu_custom_call" | custom-call | flops 9200000000 | bytes 1000 | tf_op jit(solution)/shard_map/pallas_call | solution.py:481
  69.0 2.8 %collective-permute-done.5.refs_1_.ccw_ref = bf16[272,1280]{1,0:T(8,128)(2,1)} collective-permute-done((bf16[272,1280]{1,0:T(8,128)(2,1)}, bf16[272,1280]{1,0:T(8,128)(2,1)}, u32[]{:S(2)}, u32[]{:S(2)}) %collective-permute-start.5) | collective-permute-done | bytes 696352 | tf_op jit(solution)/shard_map/ppermute | solution.py:642
  71.8 4.1 %shard_map.108 = (bf16[272,1280]{1,0:T(8,128)(2,1)}, bf16[272,1280]{1,0:T(8,128)(2,1)}, f32[40,512]{1,0:T(8,128)}) custom-call(s32[2,8]{1,0:T(2,128)} %dynamic-slice_bitcast_fusion.info_ref.refs_0_, bf16[512,1024]{1,0:T(8,128)(2,1)} %get-tuple-element.38.packed_ref.block_ref.refs_0_, f32[40,512]{1,0:T(8,128)} %get-tuple-element.39.low_ref, ...), custom_call_target="tpu_custom_call" | custom-call | flops 9200000000 | bytes 1000 | tf_op jit(solution)/shard_map/pallas_call | solution.py:216
  75.9 2.0 %collective-permute-start.8 = (bf16[272,1280]{1,0:T(8,128)(2,1)}, bf16[272,1280]{1,0:T(8,128)(2,1)}, u32[]{:S(2)}, u32[]{:S(2)}) collective-permute-start(bf16[272,1280]{1,0:T(8,128)(2,1)} %get-tuple-element.58.refs_0_), channel_id=1, source_target_pairs={{0,2},{2,4},{4,6},{6,7},{7,5},{5,3},{3,1},{1,0},{8,10},{10,12},{12... | collective-permute-start | bytes 2088968 | tf_op jit(solution)/shard_map/ppermute | solution.py:638
  77.9 10.3 %shard_map.109 = (f32[512,1024]{1,0:T(8,128)}, f32[512,128]{1,0:T(8,128)}) custom-call(f32[40,512]{1,0:T(8,128)} %get-tuple-element.39.low_ref, f32[40,512]{1,0:T(8,128)} %collective-permute-done.12.opposite_ref, bf16[272,1280]{1,0:T(8,128)(2,1)} %collective-permute-done.4.refs_0_.cw_ref, bf16[272,1280]{1,0:T(8,128)(2,1)} %collective-permute-done.5.refs_1_.ccw_ref, ...), custom_call_target="tpu_custom_call" | custom-call | flops 9200000000 | bytes 1000 | tf_op jit(solution)/shard_map/pallas_call | solution.py:393
  88.3 2.9 %shard_map.110.refs_0_ = bf16[256,1280]{1,0:T(8,128)(2,1)} custom-call(s32[2,8]{1,0:T(2,128)} %dynamic-slice_bitcast_fusion.info_ref.refs_0_, bf16[512,1024]{1,0:T(8,128)(2,1)} %get-tuple-element.38.packed_ref.block_ref.refs_0_, bf16[256,1280]{1,0:T(8,128)(2,1)} %collective-permute-done.10.refs_0_, ...), custom_call_target="tpu_custom_call", output_to_operand_aliasing={{}: (2, {})} | custom-call | flops 9200000000 | bytes 1000 | tf_op jit(solution)/shard_map/pallas_call | solution.py:176
  93.0 6.6 %shard_map.111.total_ref = f32[256,1024]{1,0:T(8,128)} custom-call(s32[2,8]{1,0:T(2,128)} %dynamic-slice_bitcast_fusion.info_ref.refs_0_, bf16[256,1280]{1,0:T(8,128)(2,1)} %shard_map.110.refs_0_, bf16[256,1280]{1,0:T(8,128)(2,1)} %collective-permute-done.11.refs_1_.ccw_ref, bf16[8192,1024]{1,0:T(8,128)(2,1)} %refs_5_.1, f32[256,1024]{1,0:T(8,128)} %shard_map.107.refs_3_, ...), custom_call_target="tpu_custom_call" | custom-call | flops 9200000000 | bytes 1000 | tf_op jit(solution)/shard_map/pallas_call | solution.py:481
  99.6 3.4 %shard_map.112 = (bf16[272,1280]{1,0:T(8,128)(2,1)}, f32[40,512]{1,0:T(8,128)}) custom-call(s32[2,8]{1,0:T(2,128)} %dynamic-slice_bitcast_fusion.info_ref.refs_0_, bf16[512,1024]{1,0:T(8,128)(2,1)} %get-tuple-element.38.packed_ref.block_ref.refs_0_, f32[40,512]{1,0:T(8,128)} %get-tuple-element.39.low_ref, bf16[272,1280]{1,0:T(8,128)(2,1)} %collective-permute-done.9.refs_0_, ...), custom_call_target="tpu_custom_call" | custom-call | flops 9200000000 | bytes 1000 | tf_op jit(solution)/shard_map/pallas_call | solution.py:216
  103.0 2.0 %collective-permute-start.13 = (bf16[272,1280]{1,0:T(8,128)(2,1)}, bf16[272,1280]{1,0:T(8,128)(2,1)}, u32[]{:S(2)}, u32[]{:S(2)}) collective-permute-start(bf16[272,1280]{1,0:T(8,128)(2,1)} %get-tuple-element.69.refs_3_), channel_id=1, source_target_pairs={{2,0},{4,2},{6,4},{7,6},{5,7},{3,5},{1,3},{0,1},{10,8},{12,10},{14... | collective-permute-start | bytes 2088968 | tf_op jit(solution)/shard_map/ppermute | solution.py:642
  104.9 8.4 %shard_map.113.refs_2_ = f32[256,1024]{1,0:T(8,128)} custom-call(s32[2,8]{1,0:T(2,128)} %dynamic-slice_bitcast_fusion.info_ref.refs_0_, bf16[272,1280]{1,0:T(8,128)(2,1)} %get-tuple-element.58.refs_0_, bf16[272,1280]{1,0:T(8,128)(2,1)} %get-tuple-element.59.refs_1_, bf16[272,1280]{1,0:T(8,128)(2,1)} %collective-permute-done.8.refs_2_.refs_9_, ...), custom_call_target="tpu_custom_call" | custom-call | flops 9200000000 | bytes 1000 | tf_op jit(solution)/shard_map/pallas_call | solution.py:481
  113.4 6.1 %shard_map.114.refs_11_ = bf16[512,1024]{1,0:T(8,128)(2,1)} custom-call(s32[2,8]{1,0:T(2,128)} %dynamic-slice_bitcast_fusion.info_ref.refs_0_, s32[2]{0:T(128)} %refs_1_.5, f32[256,1024]{1,0:T(8,128)} %shard_map.111.total_ref, f32[512,128]{1,0:T(8,128)} %get-tuple-element.66.refs_5_.refs_7_.inv_ref.refs_3_, ...), custom_call_target="tpu_custom_call" | custom-call | bytes 1000 | tf_op jit(solution)/shard_map/pallas_call | solution.py:562
  120.4 6.1 %shard_map.115 = bf16[512,1024]{1,0:T(8,128)(2,1)} custom-call(s32[2,8]{1,0:T(2,128)} %dynamic-slice_bitcast_fusion.info_ref.refs_0_, s32[2]{0:T(128)} %refs_1_.5, f32[256,1024]{1,0:T(8,128)} %shard_map.113.refs_2_, f32[512,128]{1,0:T(8,128)} %get-tuple-element.66.refs_5_.refs_7_.inv_ref.refs_3_, ...), custom_call_target="tpu_custom_call", output_to_operand_aliasing={{}: (11, {})} | custom-call | bytes 1000 | tf_op jit(solution)/shard_map/pallas_call | solution.py:562
  (27 shorter events, 12.4 us)
Async XLA Ops:
  5.4 19.0 %collective-permute-start.2 = (bf16[256,1280]{1,0:T(8,128)(2,1)}, bf16[256,1280]{1,0:T(8,128)(2,1)}, u32[]{:S(2)}, u32[]{:S(2)}) collective-permute-start(bf16[256,1280]{1,0:T(8,128)(2,1)} %get-tuple-element.42), channel_id=1, source_target_pairs={{0,2},{2,4},{4,6},{6,7},{7,5},{5,3},{3,1},{1,0},{8,10},{10,12},{12... | collective-permute-start | bytes 1966088 | tf_op jit(solution)/shard_map/ppermute | solution.py:609
  8.4 16.5 %collective-permute-start.3 = (bf16[256,1280]{1,0:T(8,128)(2,1)}, bf16[256,1280]{1,0:T(8,128)(2,1)}, u32[]{:S(2)}, u32[]{:S(2)}) collective-permute-start(bf16[256,1280]{1,0:T(8,128)(2,1)} %get-tuple-element.43), channel_id=1, source_target_pairs={{2,0},{4,2},{6,4},{7,6},{5,7},{3,5},{1,3},{0,1},{10,8},{12,10},{14... | collective-permute-start | bytes 1966088 | tf_op jit(solution)/shard_map/ppermute | solution.py:609
  21.1 18.9 %collective-permute-start = (bf16[272,1280]{1,0:T(8,128)(2,1)}, bf16[272,1280]{1,0:T(8,128)(2,1)}, u32[]{:S(2)}, u32[]{:S(2)}) collective-permute-start(bf16[272,1280]{1,0:T(8,128)(2,1)} %get-tuple-element.40), channel_id=1, source_target_pairs={{0,2},{2,4},{4,6},{6,7},{7,5},{5,3},{3,1},{1,0},{8,10},{10,12},{12... | collective-permute-start | bytes 2088968 | tf_op jit(solution)/shard_map/ppermute | solution.py:613
  23.1 18.9 %collective-permute-start.1 = (bf16[272,1280]{1,0:T(8,128)(2,1)}, bf16[272,1280]{1,0:T(8,128)(2,1)}, u32[]{:S(2)}, u32[]{:S(2)}) collective-permute-start(bf16[272,1280]{1,0:T(8,128)(2,1)} %get-tuple-element.41), channel_id=1, source_target_pairs={{2,0},{4,2},{6,4},{7,6},{5,7},{3,5},{1,3},{0,1},{10,8},{12,10},{14... | collective-permute-start | bytes 2088968 | tf_op jit(solution)/shard_map/ppermute | solution.py:613
  28.3 28.9 %collective-permute-start.6 = (bf16[256,1280]{1,0:T(8,128)(2,1)}, bf16[256,1280]{1,0:T(8,128)(2,1)}, u32[]{:S(2)}, u32[]{:S(2)}) collective-permute-start(bf16[256,1280]{1,0:T(8,128)(2,1)} %get-tuple-element.46.refs_1_), channel_id=1, source_target_pairs={{0,2},{2,4},{4,6},{6,7},{7,5},{5,3},{3,1},{1,0},{8,10},{10,12},{12... | collective-permute-start | bytes 1966088 | tf_op jit(solution)/shard_map/ppermute | solution.py:638
  29.9 27.3 %collective-permute-start.7 = (bf16[256,1280]{1,0:T(8,128)(2,1)}, bf16[256,1280]{1,0:T(8,128)(2,1)}, u32[]{:S(2)}, u32[]{:S(2)}) collective-permute-start(bf16[256,1280]{1,0:T(8,128)(2,1)} %get-tuple-element.47.refs_2_), channel_id=1, source_target_pairs={{2,0},{4,2},{6,4},{7,6},{5,7},{3,5},{1,3},{0,1},{10,8},{12,10},{14... | collective-permute-start | bytes 1966088 | tf_op jit(solution)/shard_map/ppermute | solution.py:642
  46.1 22.9 %collective-permute-start.4 = (bf16[272,1280]{1,0:T(8,128)(2,1)}, bf16[272,1280]{1,0:T(8,128)(2,1)}, u32[]{:S(2)}, u32[]{:S(2)}) collective-permute-start(bf16[272,1280]{1,0:T(8,128)(2,1)} %get-tuple-element.50.refs_1_), channel_id=1, source_target_pairs={{0,2},{2,4},{4,6},{6,7},{7,5},{5,3},{3,1},{1,0},{8,10},{10,12},{12... | collective-permute-start | bytes 2088968 | tf_op jit(solution)/shard_map/ppermute | solution.py:638
  47.6 24.2 %collective-permute-start.5 = (bf16[272,1280]{1,0:T(8,128)(2,1)}, bf16[272,1280]{1,0:T(8,128)(2,1)}, u32[]{:S(2)}, u32[]{:S(2)}) collective-permute-start(bf16[272,1280]{1,0:T(8,128)(2,1)} %get-tuple-element.51.refs_2_), channel_id=1, source_target_pairs={{2,0},{4,2},{6,4},{7,6},{5,7},{3,5},{1,3},{0,1},{10,8},{12,10},{14... | collective-permute-start | bytes 2088968 | tf_op jit(solution)/shard_map/ppermute | solution.py:642
  48.1 27.8 %collective-permute-start.12 = (f32[40,512]{1,0:T(8,128)}, f32[40,512]{1,0:T(8,128)}, u32[]{:S(2)}, u32[]{:S(2)}) collective-permute-start(f32[40,512]{1,0:T(8,128)} %get-tuple-element.60), channel_id=1, source_target_pairs={{0,7},{2,5},{4,3},{6,1},{7,0},{5,2},{3,4},{1,6},{8,15},{10,13},{12... | collective-permute-start | bytes 245768 | tf_op jit(solution)/shard_map/ppermute | solution.py:648
  60.5 27.7 %collective-permute-start.10 = (bf16[256,1280]{1,0:T(8,128)(2,1)}, bf16[256,1280]{1,0:T(8,128)(2,1)}, u32[]{:S(2)}, u32[]{:S(2)}) collective-permute-start(bf16[256,1280]{1,0:T(8,128)(2,1)} %get-tuple-element.54.refs_0_), channel_id=1, source_target_pairs={{0,2},{2,4},{4,6},{6,7},{7,5},{5,3},{3,1},{1,0},{8,10},{10,12},{12... | collective-permute-start | bytes 1966088 | tf_op jit(solution)/shard_map/ppermute | solution.py:638
  60.9 27.4 %collective-permute-start.11 = (bf16[256,1280]{1,0:T(8,128)(2,1)}, bf16[256,1280]{1,0:T(8,128)(2,1)}, u32[]{:S(2)}, u32[]{:S(2)}) collective-permute-start(bf16[256,1280]{1,0:T(8,128)(2,1)} %get-tuple-element.55.refs_1_), channel_id=1, source_target_pairs={{2,0},{4,2},{6,4},{7,6},{5,7},{3,5},{1,3},{0,1},{10,8},{12,10},{14... | collective-permute-start | bytes 1966088 | tf_op jit(solution)/shard_map/ppermute | solution.py:642
  75.9 23.7 %collective-permute-start.9 = (bf16[272,1280]{1,0:T(8,128)(2,1)}, bf16[272,1280]{1,0:T(8,128)(2,1)}, u32[]{:S(2)}, u32[]{:S(2)}) collective-permute-start(bf16[272,1280]{1,0:T(8,128)(2,1)} %get-tuple-element.59.refs_1_), channel_id=1, source_target_pairs={{2,0},{4,2},{6,4},{7,6},{5,7},{3,5},{1,3},{0,1},{10,8},{12,10},{14... | collective-permute-start | bytes 2088968 | tf_op jit(solution)/shard_map/ppermute | solution.py:642
  75.9 23.7 %collective-permute-start.8 = (bf16[272,1280]{1,0:T(8,128)(2,1)}, bf16[272,1280]{1,0:T(8,128)(2,1)}, u32[]{:S(2)}, u32[]{:S(2)}) collective-permute-start(bf16[272,1280]{1,0:T(8,128)(2,1)} %get-tuple-element.58.refs_0_), channel_id=1, source_target_pairs={{0,2},{2,4},{4,6},{6,7},{7,5},{5,3},{3,1},{1,0},{8,10},{10,12},{12... | collective-permute-start | bytes 2088968 | tf_op jit(solution)/shard_map/ppermute | solution.py:638
  91.2 22.1 %collective-permute-start.14 = (bf16[256,1280]{1,0:T(8,128)(2,1)}, bf16[256,1280]{1,0:T(8,128)(2,1)}, u32[]{:S(2)}, u32[]{:S(2)}) collective-permute-start(bf16[256,1280]{1,0:T(8,128)(2,1)} %shard_map.110.refs_0_), channel_id=1, source_target_pairs={{0,2},{2,4},{4,6},{6,7},{7,5},{5,3},{3,1},{1,0},{8,10},{10,12},{12... | collective-permute-start | bytes 1966088 | tf_op jit(solution)/shard_map/ppermute | solution.py:638
  103.0 17.5 %collective-permute-start.13 = (bf16[272,1280]{1,0:T(8,128)(2,1)}, bf16[272,1280]{1,0:T(8,128)(2,1)}, u32[]{:S(2)}, u32[]{:S(2)}) collective-permute-start(bf16[272,1280]{1,0:T(8,128)(2,1)} %get-tuple-element.69.refs_3_), channel_id=1, source_target_pairs={{2,0},{4,2},{6,4},{7,6},{5,7},{3,5},{1,3},{0,1},{10,8},{12,10},{14... | collective-permute-start | bytes 2088968 | tf_op jit(solution)/shard_map/ppermute | solution.py:642

commit v4 on v3

v4 whole, which is shorter than its diff:
```python
import functools
import math

import jax
import jax.numpy as jnp
import numpy as np
from jax import lax
from jax.experimental import pallas as pl
from jax.experimental.pallas import tpu as pltpu
from jax.sharding import PartitionSpec as P

QUERY_HEADS = 64
KV_HEADS = 8
HEAD_WIDTH = 128
ADAPTER_RANK = 16
SLOT = 256
LANES = 128
LOW_ROWS = 40

EPS = 1e-05
ROPE_BASE = 500000.0

SIDE_MIX = 0
SIDE_INDEX = 2

DEPTH = 3
CHUNK = 512
HEADS_AT_ONCE = 8
DELTA_TILE = 1024
ADD_WEIGHT = 8.0
QUERY_WEIGHT = 8.0
VMEM_LIMIT = 64 * 1024 * 1024 - 64 * 1024
F32 = jnp.float32
BF16 = jnp.bfloat16


def call(kernel, out_shape, microseconds=0.0, **kwargs):
    return pl.pallas_call(
        kernel,
        out_shape=out_shape,
        compiler_params=pltpu.CompilerParams(vmem_limit_bytes=VMEM_LIMIT),
        cost_estimate=pl.CostEstimate(
            flops=int(1.15e9 * microseconds), bytes_accessed=1000, transcendentals=0
        ),
        **kwargs,
    )


def whole(shape):
    return pl.BlockSpec(shape, lambda *_: (0,) * len(shape))


def shape_of(shape, dtype):
    return jax.ShapeDtypeStruct(shape, dtype)


def prefetch(count, grid, in_specs, out_specs, scratch_shapes=()):
    return pltpu.PrefetchScalarGridSpec(
        num_scalar_prefetch=count,
        grid=grid,
        in_specs=in_specs,
        out_specs=out_specs,
        scratch_shapes=scratch_shapes,
    )


def write_message(message, block, w_ref):
    half, width = block.shape
    message[:half, :width] = block
    product = jnp.dot(block, w_ref[...], preferred_element_type=F32)
    message[:half, width:] = product.astype(BF16)


def scale_kernel(info_ref, x_ref, scale_ref, cw_w_ref, ccw_w_ref, cw_ref, ccw_ref, packed):
    half = cw_ref.shape[0]
    packed[...] = (x_ref[...].astype(F32) * scale_ref[...]).astype(BF16)
    block = packed[:half, :]
    write_message(cw_ref, block, cw_w_ref)
    write_message(ccw_ref, block, ccw_w_ref)


def scale_rows(info, x, scale, weight, reach):
    tokens, width = x.shape
    pair = 2 * HEAD_WIDTH
    message = (tokens // 2, width + pair)
    column = [
        pl.BlockSpec((width, pair), lambda j, info, away=away: (0, info[1, away]))
        for away in (reach, reach + 1)
    ]
    return call(
        scale_kernel,
        (shape_of(message, BF16),) * 2 + (shape_of((tokens, width), BF16),),
        grid_spec=prefetch(
            1,
            (1,),
            [
                whole((tokens, width)),
                pl.BlockSpec((1, width), lambda j, info: (0, info[0, 0])),
                *column,
            ],
            (whole(message),) * 2 + (whole((tokens, width)),),
        ),
    )(info, x, scale.reshape(1, -1), weight, weight)


def low_places(tokens, full):
    if full >= 2 * tokens + SLOT:
        second = (slice(0, ADAPTER_RANK), slice(tokens, 2 * tokens))
        squares = (0, slice(2 * tokens, 2 * tokens + SLOT))
        extra = ADAPTER_RANK
    else:
        second = (slice(ADAPTER_RANK, 2 * ADAPTER_RANK), slice(0, tokens))
        squares = (2 * ADAPTER_RANK, slice(0, SLOT))
        extra = 3 * ADAPTER_RANK
    return extra, (slice(0, ADAPTER_RANK), slice(0, tokens)), second, squares


def read_low(region):
    tokens = 2 * SLOT
    _, first, second, (row, lanes) = low_places(tokens, region.shape[1])
    squares = jnp.concatenate(
        [region[row + i : row + i + 1, lanes] + region[row + 2 + i : row + 3 + i, lanes] for i in range(2)],
        axis=1,
    )
    return jnp.concatenate(
        [region[first], region[second], squares, jnp.zeros((LOW_ROWS - 33, tokens), F32)], axis=0
    )


def write_low(message, half, low):
    tokens = 2 * SLOT
    extra, first, second, (row, lanes) = low_places(tokens, message.shape[1])
    message[half : half + extra, :] = jnp.zeros((extra, message.shape[1]), BF16)
    squares = low[2 * ADAPTER_RANK : 2 * ADAPTER_RANK + 1, :]
    rounded = squares.astype(BF16)
    rest = (squares - rounded.astype(F32)).astype(BF16)
    for place, value in ((first, low[:ADAPTER_RANK]), (second, low[ADAPTER_RANK : 2 * ADAPTER_RANK])):
        span = slice(half + place[0].start, half + place[0].stop)
        message[span, place[1]] = value.astype(BF16)
    block = jnp.concatenate(
        [rounded[:, :SLOT], rounded[:, SLOT:], rest[:, :SLOT], rest[:, SLOT:]]
        + [jnp.zeros((ADAPTER_RANK - 4, SLOT), BF16)],
        axis=0,
    )
    message[half + row : half + row + ADAPTER_RANK, lanes] = block


def terms_kernel(info_ref, x_ref, ahead_w_ref, behind_w_ref, ahead_ref, behind_ref):
    for w_ref, out_ref in ((ahead_w_ref, ahead_ref), (behind_w_ref, behind_ref)):
        out_ref[0] = jnp.dot(x_ref[...], w_ref[...], preferred_element_type=F32).astype(BF16)


def late_terms(info, packed, weight, count):
    rows, width = packed.shape
    pair = 2 * HEAD_WIDTH
    number = count // 2 - 2
    out = shape_of((number, rows, pair), BF16)
    block = pl.BlockSpec((1, rows, pair), lambda i, info: (i, 0, 0))
    return call(
        terms_kernel,
        (out, out),
        grid_spec=prefetch(
            1,
            (number,),
            [
                whole((rows, width)),
                pl.BlockSpec((width, pair), lambda i, info: (0, info[1, 1 + i])),
                pl.BlockSpec((width, pair), lambda i, info: (0, info[1, count - 1 - i])),
            ],
            (block, block),
        ),
    )(info, packed, weight, weight)


def own_term(block_ref, w_ref):
    if block_ref is None:
        return w_ref[0].astype(F32)
    return jnp.dot(block_ref[...], w_ref[...], preferred_element_type=F32)


def term_specs(info, aways, packed, weight, terms, piece):
    rows, width = packed.shape
    half = rows // 2
    pair = 2 * HEAD_WIDTH
    if terms is None:
        specs = [pl.BlockSpec((half, width), lambda j, info: (piece, 0))]
        specs += [
            pl.BlockSpec((width, pair), lambda j, info, away=away: (0, info[1, away]))
            for away in aways
        ]
        return [packed] + [weight] * len(aways), specs
    count = info.shape[1]
    operands, specs = [], []
    for away in aways:
        ahead = away < count // 2
        operands.append(terms[0 if ahead else 1])
        place = away - 1 if ahead else count - 1 - away
        specs.append(pl.BlockSpec((1, half, pair), lambda j, info, place=place: (place, piece, 0)))
    return operands, specs


def add_kernel(ready, info_ref, *refs):
    refs = list(refs)
    messages = [refs.pop(0), refs.pop(0)]
    block = None if ready else refs.pop(0)
    for i, message in enumerate(messages):
        total = message[...].astype(F32) + own_term(block, refs[i])
        refs[2 + i][...] = total.astype(BF16)


def add_terms(info, messages, aways, packed, weight, terms, rows):
    half = rows // 2
    full = messages[0].shape[1]
    pair = 2 * HEAD_WIDTH
    lanes = pl.BlockSpec((half, pair), lambda j, info: (0, full // pair - 1))
    operands, specs = term_specs(info, aways, packed, weight, terms, 0)
    return call(
        functools.partial(add_kernel, terms is not None),
        (shape_of((half, full), BF16),) * 2,
        ADD_WEIGHT,
        grid_spec=prefetch(1, (1,), [lanes] * 2 + specs, (lanes,) * 2),
        input_output_aliases={1: 0, 2: 1},
    )(info, *messages, *operands)


def add_low_kernel(half, ready, info_ref, low_ref, *refs):
    refs = list(refs)
    pair = 2 * HEAD_WIDTH
    around = low_ref[...]
    messages = [refs.pop(0), refs.pop(0)]
    block = None if ready else refs.pop(0)
    for i, given in enumerate(messages):
        out = refs[2 + i]
        full = given.shape[1]
        out[:half, : full - pair] = given[:half, : full - pair]
        own = own_term(block, refs[i])
        out[:half, full - pair :] = (given[:half, full - pair :].astype(F32) + own).astype(BF16)
        if out.shape[0] > half:
            sums = read_low(given[half:, :].astype(F32))
            around = around + sums
            write_low(out, half, sums + low_ref[...])
    if len(refs) > 4:
        refs[4][...] = around


def add_terms_low(info, messages, aways, packed, weight, terms, low, rows, keep):
    half = rows // 2
    shape = messages[0].shape
    after = shape if keep else (half, shape[1])
    out = (shape_of(after, BF16),) * 2 + ((shape_of(low.shape, F32),) if keep else ())
    operands, specs = term_specs(info, aways, packed, weight, terms, 1)
    return call(
        functools.partial(add_low_kernel, half, terms is not None),
        out,
        ADD_WEIGHT,
        grid_spec=prefetch(
            1,
            (1,),
            [whole(low.shape)] + [whole(shape)] * 2 + specs,
            tuple(whole(each.shape) for each in out),
        ),
    )(info, low, *messages, *operands)


def last_kernel(half, ready, info_ref, with_sums, other, *refs):
    refs = list(refs)
    block = None if ready else refs.pop(0)
    term, first_ref, second_ref = refs
    width = second_ref.shape[1]
    mid = half // 2
    pair = 2 * HEAD_WIDTH
    own = own_term(block, term)
    sums = (with_sums[:half, width:].astype(F32) + own).astype(BF16)
    first_ref[:, :width] = with_sums[:mid, :width]
    first_ref[:, width : width + pair] = sums[:mid]
    first_ref[:, width + pair :] = sums[mid:]
    second_ref[...] = other[mid:half, :width]


def last_messages(info, with_sums, other, away, packed, weight, terms, rows, piece):
    half = rows // 2
    width = weight.shape[0]
    pair = 2 * HEAD_WIDTH
    out = (shape_of((half // 2, width + 2 * pair), BF16), shape_of((half // 2, width), BF16))
    operands, specs = term_specs(info, [away], packed, weight, terms, piece)
    return call(
        functools.partial(last_kernel, half, terms is not None),
        out,
        ADD_WEIGHT,
        grid_spec=prefetch(
            1,
            (1,),
            [whole(with_sums.shape), whole(other.shape)] + specs,
            tuple(whole(each.shape) for each in out),
        ),
    )(info, with_sums, other, *operands)


def chosen_group(index):
    rows = index.shape[0]
    lane = lax.broadcasted_iota(jnp.int32, (rows, LANES), 1)
    return index - (lane // ADAPTER_RANK).astype(F32)


def fold(value):
    shift = ADAPTER_RANK
    while shift < LANES:
        value = value + pltpu.roll(value, shift, 1)
        shift *= 2
    return value


def low_kernel(
    aways, info_ref, packed_ref, w_ref, index_ref, mix_ref, x_ref, kv_ref, out_ref, side_ref,
    cw_ref, ccw_ref, own_ref, acc_ref, group_ref, squares_ref, x_s, columns_s, messages_s, sems,
    out_sems,
):
    step = pl.program_id(0)
    tile = w_ref.shape[1]
    tokens = x_ref.shape[0]
    half = tokens // 2
    pair = 2 * HEAD_WIDTH
    reads = [pltpu.make_async_copy(x_ref, x_s, sems.at[0])]
    for i, away in enumerate(aways):
        first = pl.multiple_of(info_ref[1, away] * pair, pair)
        column = kv_ref.at[:, pl.ds(first, pair)]
        reads.append(pltpu.make_async_copy(column, columns_s.at[i], sems.at[1 + i]))
    writes = []
    for i, ref in enumerate((cw_ref, ccw_ref)):
        extra = ref.shape[0] - half
        for j, span in enumerate((pl.ds(0, half), pl.ds(half, extra))):
            block = messages_s.at[i, span]
            writes.append(pltpu.make_async_copy(block, ref.at[span], out_sems.at[i, j]))

    @pl.when(step == 0)
    def _():
        for copy in reads:
            copy.start()
        acc_ref[...] = jnp.zeros_like(acc_ref)
        side = jnp.concatenate(
            [mix_ref[...], index_ref[...].astype(F32), jnp.zeros((LANES - 4, tokens), F32)],
            axis=0,
        ).T
        side_ref[...] = side
        for k in range(2):
            group_ref[k] = chosen_group(side[:, SIDE_INDEX + k : SIDE_INDEX + k + 1])

    @pl.when(step == 1)
    def _():
        for copy in reads:
            copy.wait()
        x = x_s[...].astype(F32)
        squares = jnp.sum(x * x, axis=1, keepdims=True)
        squares_ref[...] = jnp.broadcast_to(squares, squares_ref.shape)
        for i in range(2):
            write_message(messages_s.at[i], packed_ref[half:, :], columns_s.at[i])
            writes[2 * i].start()
        own = jnp.dot(packed_ref[...], columns_s[2], preferred_element_type=F32)
        own_ref[...] = own.astype(BF16)

    chunk = min(CHUNK, tile)
    for first in range(0, tile, chunk):
        product = jnp.dot(
            packed_ref[...], w_ref[:, first : first + chunk], preferred_element_type=F32
        )
        for k in range(2):
            total = acc_ref[k]
            for s in range(chunk // LANES):
                group = (step * tile + first + s * LANES) // ADAPTER_RANK
                here = group_ref[k] == group.astype(F32)
                total += jnp.where(here, product[:, s * LANES : (s + 1) * LANES], 0.0)
            acc_ref[k] = total

    @pl.when(step == pl.num_programs(0) - 1)
    def _():
        lane = lax.broadcasted_iota(jnp.int32, (tokens, LANES), 1)
        sums = jnp.where(lane < ADAPTER_RANK, fold(acc_ref[0]), fold(acc_ref[1]))
        sums = jnp.where(lane < 2 * ADAPTER_RANK, sums, 0.0)
        sums = jnp.where(lane == 2 * ADAPTER_RANK, squares_ref[...], sums)
        low = sums.T[:LOW_ROWS]
        out_ref[...] = low
        for i in range(2):
            write_low(messages_s.at[i], half, low)
            writes[2 * i + 1].start()
        for copy in writes:
            copy.wait()


def low_partials(info, x, packed, weight, index, mix, kv_weight, reach):
    width, columns = weight.shape
    tile = min(1024, columns)
    tokens = x.shape[0]
    pair = 2 * HEAD_WIDTH
    message = (tokens // 2 + low_places(tokens, width + pair)[0], width + pair)
    anywhere = pl.BlockSpec(memory_space=pl.ANY)
    return call(
        functools.partial(low_kernel, (reach - 1, reach, 0)),
        (shape_of((LOW_ROWS, tokens), F32), shape_of((tokens, LANES), F32))
        + (shape_of(message, BF16),) * 2
        + (shape_of((tokens, pair), BF16),),
        grid_spec=prefetch(
            1,
            (columns // tile,),
            [
                whole((tokens, width)),
                pl.BlockSpec((width, tile), lambda j, info: (0, j)),
                whole((2, tokens)),
                whole((2, tokens)),
                anywhere,
                anywhere,
            ],
            (whole((LOW_ROWS, tokens)), whole((tokens, LANES)), anywhere, anywhere)
            + (whole((tokens, pair)),),
            [
                pltpu.VMEM((2, tokens, LANES), F32),
                pltpu.VMEM((2, tokens, LANES), F32),
                pltpu.VMEM((tokens, LANES), F32),
                pltpu.VMEM((tokens, width), BF16),
                pltpu.VMEM((3, width, pair), BF16),
                pltpu.VMEM((2, *message), BF16),
                pltpu.SemaphoreType.DMA((4,)),
                pltpu.SemaphoreType.DMA((2, 2)),
            ],
        ),
    )(info, packed, weight, index.T, mix.T, x, kv_weight)


def delta_kernel(
    model_width, slots, info_ref, low_ref, opposite_ref, cw_ref, ccw_ref, total_a_ref, total_b_ref,
    weight_ref, side_ref, w_ref, out_a_ref, out_b_ref, inv_ref, co_ref, group_ref, ends, x_buf,
    w_buf, sems,
):
    step = pl.program_id(0)
    tile = w_ref.shape[0]
    half, width = x_buf.shape[1:]
    outs = (out_a_ref, out_b_ref)
    messages = (cw_ref, ccw_ref)
    end_copies = [
        pltpu.make_async_copy(ref.at[pl.ds(half, ends.shape[1])], ends.at[i], sems.at[i])
        for i, ref in enumerate(messages)
    ]
    total_copies = [
        pltpu.make_async_copy(ref, outs[i], sems.at[2 + i])
        for i, ref in enumerate((total_a_ref, total_b_ref))
    ]
    row_copies = [
        pltpu.make_async_copy(
            ref.at[pl.ds(0, half), pl.ds(0, width)], x_buf.at[i], sems.at[4 + i]
        )
        for i, ref in enumerate(messages)
    ]
    weight_copies = []
    for i in range(2):
        first = pl.multiple_of(info_ref[0, slots[i]] * width, width)
        block = weight_ref.at[pl.ds(first, width)]
        weight_copies.append(pltpu.make_async_copy(block, w_buf.at[i], sems.at[6 + i]))

    @pl.when(step == 0)
    def _():
        for copy in end_copies + total_copies + row_copies + weight_copies:
            copy.start()
        for k in range(2):
            group_ref[k] = chosen_group(side_ref[:, SIDE_INDEX + k : SIDE_INDEX + k + 1])
        for copy in end_copies:
            copy.wait()
        tokens = low_ref.shape[1]
        sums = low_ref[...] + opposite_ref[...]
        for i in range(2):
            sums = sums + read_low(ends[i].astype(F32))
        padding = jnp.zeros((LANES - LOW_ROWS, tokens), F32)
        low = jnp.concatenate([sums, padding], axis=0).T
        lane = lax.broadcasted_iota(jnp.int32, (tokens, LANES), 1)
        squares = low[:, 2 * ADAPTER_RANK : 2 * ADAPTER_RANK + 1]
        inverse = lax.rsqrt(squares * (1.0 / model_width) + EPS)
        inv_ref[...] = jnp.broadcast_to(inverse, (tokens, LANES))
        for k in range(2):
            value = fold(jnp.where(lane // ADAPTER_RANK == k, low, 0.0))
            co_ref[k] = value * inverse * side_ref[:, SIDE_MIX + k : SIDE_MIX + k + 1]
        for i in range(2):
            total_copies[i].wait()
            outs[i][...] = outs[i][...] * inverse[i * half : (i + 1) * half]

    pieces = []
    for s in range(tile // LANES):
        group = ((step * tile + s * LANES) // ADAPTER_RANK).astype(F32)
        piece = jnp.where(group_ref[0] == group, co_ref[0], 0.0)
        piece = jnp.where(group_ref[1] == group, co_ref[1], piece)
        pieces.append(piece.astype(BF16))
    coefficients = jnp.concatenate(pieces, axis=1)
    product = jnp.dot(coefficients, w_ref[...], preferred_element_type=F32)
    for i in range(2):
        outs[i][...] += product[i * half : (i + 1) * half]

    @pl.when(step == pl.num_programs(0) - 1)
    def _():
        for i in range(2):
            row_copies[i].wait()
            weight_copies[i].wait()
            product = jnp.dot(x_buf[i], w_buf[i], preferred_element_type=F32)
            out_b_ref[...] += product * inv_ref[half:, 0:1]


def query_delta(info, low, opposite, messages, slots, totals, weight, side, up):
    depth, columns = up.shape
    tile = min(DELTA_TILE, depth)
    tokens = side.shape[0]
    half = tokens // 2
    full = messages[0].shape[1]
    width = weight.shape[0] // info.shape[1]
    anywhere = pl.BlockSpec(memory_space=pl.ANY)
    extra = low_places(tokens, full)[0]
    return call(
        functools.partial(delta_kernel, weight.shape[0], slots),
        (shape_of((half, columns), F32),) * 2 + (shape_of((tokens, LANES), F32),),
        QUERY_WEIGHT,
        grid_spec=prefetch(
            1,
            (depth // tile,),
            [whole(low.shape), whole(low.shape)]
            + [anywhere] * 5
            + [whole(side.shape), pl.BlockSpec((tile, columns), lambda j, _: (j, 0))],
            (whole((half, columns)), whole((half, columns)), whole((tokens, LANES))),
            [
                pltpu.VMEM((2, tokens, LANES), F32),
                pltpu.VMEM((2, tokens, LANES), F32),
                pltpu.VMEM((2, extra, full), BF16),
                pltpu.VMEM((2, half, width), BF16),
                pltpu.VMEM((2, width, columns), BF16),
                pltpu.SemaphoreType.DMA((8,)),
            ],
        ),
    )(info, low, opposite, *messages, *totals, weight, side, up)


def product_kernel(slots, starts, has_total, has_inv, info_ref, *refs):
    refs = list(refs)
    count = len(slots)
    blocks = [refs.pop(0) for _ in range(count)]
    weight = refs.pop(0)
    total_ref = refs.pop(0) if has_total else None
    inv_ref = refs.pop(0) if has_inv else None
    out_ref, x_buf, w_buf, sems, total_sem = refs
    depth, half, width = x_buf.shape
    columns = w_buf.shape[2]
    chunk = min(CHUNK, columns)

    def copies(i):
        buf = i % depth
        first = pl.multiple_of(info_ref[0, slots[i]] * width, width)
        block = blocks[i].at[pl.ds(starts[i], half), pl.ds(0, width)]
        return [
            pltpu.make_async_copy(weight.at[pl.ds(first, width)], w_buf.at[buf], sems.at[buf, 0]),
            pltpu.make_async_copy(block, x_buf.at[buf], sems.at[buf, 1]),
        ]

    for i in range(min(depth - 1, count)):
        for copy in copies(i):
            copy.start()
    if has_total:
        total_copy = pltpu.make_async_copy(total_ref, out_ref, total_sem)
        total_copy.start()
    for i in range(count):
        buf = i % depth
        if i + depth - 1 < count:
            for copy in copies(i + depth - 1):
                copy.start()
        for copy in copies(i):
            copy.wait()
        if i == 0 and has_total:
            total_copy.wait()
        for first in range(0, columns, chunk):
            span = slice(first, first + chunk)
            value = jnp.dot(x_buf[buf], w_buf[buf, :, span], preferred_element_type=F32)
            if has_inv:
                value = value * inv_ref[:, 0:1]
            if i > 0 or has_total:
                value = out_ref[:, span] + value
            out_ref[:, span] = value


def product(info, total, sources, weight, half, inv=None, place=0):
    columns = weight.shape[1]
    width = weight.shape[0] // info.shape[1]
    operands = [block for _, block, _ in sources] + [weight] + ([] if total is None else [total])
    in_specs = [pl.BlockSpec(memory_space=pl.ANY)] * len(operands)
    if inv is not None:
        operands.append(inv)
        in_specs.append(pl.BlockSpec((half, LANES), lambda j, info: (place, 0)))
    slots = [slot for slot, _, _ in sources]
    starts = [start for _, _, start in sources]
    return call(
        functools.partial(product_kernel, slots, starts, total is not None, inv is not None),
        shape_of((half, columns), F32),
        QUERY_WEIGHT,
        grid_spec=prefetch(
            1,
            (1,),
            in_specs,
            whole((half, columns)),
            [
                pltpu.VMEM((DEPTH, half, width), BF16),
                pltpu.VMEM((DEPTH, width, columns), BF16),
                pltpu.SemaphoreType.DMA((DEPTH, 2)),
                pltpu.SemaphoreType.DMA,
            ],
        ),
    )(info, *operands)


def rotate(values, cosines, sines):
    lane = lax.broadcasted_iota(jnp.int32, values.shape, 1)
    after = pltpu.roll(values, LANES - 1, 1)
    before = pltpu.roll(values, 1, 1)
    other = jnp.where(lane % 2 == 0, after, before)
    return values * cosines + other * sines


def attention_kernel(
    info_ref, lengths_ref, total_a_ref, total_b_ref, inv_ref, w_ref, cos_ref, sin_ref, own_ref,
    *refs,
):
    parts, sums = refs[:4], refs[4:10]
    out_ref, last_s, key_s, value_s, bias_s = refs[10:]
    mid = parts[0].shape[0]

    @pl.when(pl.program_id(0) == 0)
    def _():
        row = lax.broadcasted_iota(jnp.int32, (SLOT, SLOT), 0)
        col = lax.broadcasted_iota(jnp.int32, (SLOT, SLOT), 1)
        for i, part in enumerate(parts):
            last_s[i * mid : (i + 1) * mid, :] = part[...]
        for prompt in range(2):
            span = slice(prompt * SLOT, (prompt + 1) * SLOT)
            first, second, other = sums[3 * prompt : 3 * prompt + 3]
            pair = jnp.concatenate([first[...], second[...]], axis=0).astype(F32)
            pair = pair + other[...].astype(F32) + own_ref[span, :].astype(F32)
            pair = pair * inv_ref[span, 0:1]
            key = rotate(pair[:, :HEAD_WIDTH], cos_ref[...], sin_ref[...])
            key_s[prompt] = key.astype(BF16)
            value_s[prompt] = pair[:, HEAD_WIDTH:].astype(BF16)
            seen = (col <= row) & (col < lengths_ref[prompt])
            bias_s[prompt] = jnp.where(seen, 0.0, -1e30)

    product = jnp.dot(last_s[...], w_ref[...], preferred_element_type=F32)
    row_narrow = lax.broadcasted_iota(jnp.int32, (SLOT, HEAD_WIDTH), 0)
    factor = math.log2(math.e) / math.sqrt(HEAD_WIDTH)
    for prompt, total_ref in enumerate((total_a_ref, total_b_ref)):
        rows = slice(prompt * SLOT, (prompt + 1) * SLOT)
        queries = total_ref[...] + product[rows] * inv_ref[rows, 0:1]
        for head in range(w_ref.shape[1] // HEAD_WIDTH):
            span = slice(head * HEAD_WIDTH, (head + 1) * HEAD_WIDTH)
            query = rotate(queries[:, span], cos_ref[...], sin_ref[...]).astype(BF16)
            scores = lax.dot_general(
                query, key_s[prompt], (((1,), (1,)), ((), ())), preferred_element_type=F32
            )
            scores = scores * factor + bias_s[prompt]
            top = jnp.max(scores, axis=1, keepdims=True)
            weights = jnp.exp2(scores - top)
            totals = jnp.sum(weights, axis=1, keepdims=True)
            mixed = jnp.dot(weights.astype(BF16), value_s[prompt], preferred_element_type=F32)
            mixed = jnp.where(row_narrow < lengths_ref[prompt], mixed * (1.0 / totals), 0.0)
            out_ref[rows, span] = mixed.astype(BF16)


def attention(info, lengths, totals, inv, last_slot, weight, own, parts, tables):
    width = weight.shape[0] // info.shape[1]
    columns = weight.shape[1]
    tile = min(HEADS_AT_ONCE * HEAD_WIDTH, columns)
    pair = 2 * HEAD_WIDTH
    mid = SLOT // 2
    tokens = 2 * SLOT
    rows_of = [part for first, second, _ in parts for part in (first, second)]
    sums_of = [part for first, _, other in parts for part in (first, first, other)]
    lane = width // pair
    sums_specs = [
        pl.BlockSpec((mid, pair), lambda j, *_: (0, lane)),
        pl.BlockSpec((mid, pair), lambda j, *_: (0, lane + 1)),
        pl.BlockSpec((SLOT, pair), lambda j, *_: (0, lane)),
    ]
    return call(
        attention_kernel,
        shape_of((tokens, columns), BF16),
        grid_spec=prefetch(
            2,
            (columns // tile,),
            [
                pl.BlockSpec((SLOT, tile), lambda j, *_: (0, j)),
                pl.BlockSpec((SLOT, tile), lambda j, *_: (0, j)),
                whole((tokens, LANES)),
                pl.BlockSpec((width, tile), lambda j, info, _: (info[0, last_slot], j)),
                whole((SLOT, HEAD_WIDTH)),
                whole((SLOT, HEAD_WIDTH)),
                whole((tokens, pair)),
            ]
            + [pl.BlockSpec((mid, width), lambda j, *_: (0, 0))] * 4
            + sums_specs * 2,
            pl.BlockSpec((tokens, tile), lambda j, *_: (0, j)),
            [
                pltpu.VMEM((tokens, width), BF16),
                pltpu.VMEM((2, SLOT, HEAD_WIDTH), BF16),
                pltpu.VMEM((2, SLOT, HEAD_WIDTH), BF16),
                pltpu.VMEM((2, SLOT, SLOT), F32),
            ],
        ),
    )(info, lengths, *totals, inv, weight, *tables, own, *rows_of, *sums_of)


def rotation_tables():
    lane = jnp.arange(HEAD_WIDTH)
    inverse = jnp.power(F32(ROPE_BASE), -2.0 * (lane // 2).astype(F32) / HEAD_WIDTH)
    angles = jnp.arange(SLOT).astype(F32)[:, None] * inverse[None, :]
    sines = jnp.sin(angles)
    return jnp.cos(angles), jnp.where(lane[None, :] % 2 == 0, -sines, sines)


def ring_order(count):
    if count > 8:
        return list(range(count))
    return list(range(0, count, 2)) + list(range(1, count, 2))[::-1]


def after(value, *earlier):
    return lax.optimization_barrier((value, *earlier))[0]


def program(count, rows, lengths, info, x, scale, wq, wkv, wdown, wup, index, mix):
    order = ring_order(count)
    reach = count // 2
    cw = [(order[i], order[(i + 1) % count]) for i in range(count)]
    ccw = [(b, a) for a, b in cw]
    send_cw = functools.partial(lax.ppermute, axis_name="tensor", perm=cw)
    send_ccw = functools.partial(lax.ppermute, axis_name="tensor", perm=ccw)

    opposite = [(order[i], order[(i + reach) % count]) for i in range(count)]

    cw_first, ccw_first, packed = scale_rows(info, x, scale, wkv, reach)
    from_cw, from_ccw = [send_cw(cw_first), None], [send_ccw(ccw_first), None]
    low, side, cw_second, ccw_second, own = low_partials(
        info, x, packed, wdown, index, mix, wkv, reach
    )
    from_cw[1], from_ccw[1] = send_cw(cw_second), send_ccw(ccw_second)
    done = low
    totals = [None, None]
    inv = None
    last = []
    terms = None
    half = rows // 2

    for step in range(1, reach):
        final = step + 1 == reach
        for piece in range(2):
            got_cw, got_ccw, _ = lax.optimization_barrier((from_cw[piece], from_ccw[piece], done))
            aways = [reach - step - piece, count - reach + step + 1 - piece]
            ends = got_cw, got_ccw
            moved = list(ends)
            if final:
                sums_from, other = ends if piece == 0 else ends[::-1]
                first, second = last_messages(
                    info, sums_from, other, aways[piece], packed, wkv, terms, rows, piece
                )
                if piece == 0:
                    last.append((send_cw(first), send_ccw(second), got_ccw))
                else:
                    last.append((send_ccw(first), send_cw(second), got_cw))
                done = first
            else:
                if piece == 0:
                    moved = add_terms(info, moved, aways, packed, wkv, terms, rows)
                else:
                    moved = add_terms_low(
                        info, moved, aways, packed, wkv, terms, low, rows, step < reach - 2
                    )
                from_cw[piece], from_ccw[piece] = send_cw(moved[0]), send_ccw(moved[1])
                done = moved[piece]
            sources = [(count - step, moved[0], 0), (step, moved[1], 0)]
            if step == 1:
                sources = [(0, packed, piece * half)] + sources
            if step == 1 and piece == 1:
                opposite_low = lax.ppermute(moved[2], "tensor", opposite)
            if step == reach - 2 and piece == 1:
                late, _ = lax.optimization_barrier((opposite_low, done))
                *totals, inv = query_delta(
                    info, low, late, ends, (count - step, step), totals, wq, side, wup
                )
                done = inv
            else:
                totals[piece] = product(info, totals[piece], sources, wq, half, inv, piece)
                done = totals[piece]
            if step == 1 and piece == 0:
                late = late_terms(info, after(packed, done), wkv, count)
                done = late[0]
            if step == 1 and piece == 1:
                terms = late
    return attention(info, lengths, totals, inv, reach, wq, own, last, rotation_tables())


def shards(count, x, scale, wq, wkv, wdown, wup, index, mix, lengths):
    shard = lax.axis_index("tensor")
    order = ring_order(count)
    heads = wq.shape[1] // HEAD_WIDTH
    table = np.zeros((count, 2, count), np.int32)
    for place, device in enumerate(order):
        for i in range(count):
            other = order[(place + i) % count]
            table[device, 0, i] = other
            table[device, 1, i] = other * heads // (QUERY_HEADS // KV_HEADS)
    info = lax.dynamic_index_in_dim(jnp.asarray(table), shard, 0, keepdims=False)
    return program(count, x.shape[0], lengths, info, x, scale, wq, wkv, wdown, wup, index, mix)


def solution(mesh):
    placed = (
        P(("groups", "replica"), "tensor"),
        P(),
        P(None, "tensor"),
        P("tensor", None),
        P("tensor", None),
        P(None, "tensor"),
        P(("groups", "replica"), None),
        P(("groups", "replica"), None),
        P(("groups", "replica")),
    )
    return jax.shard_map(
        functools.partial(shards, mesh.shape["tensor"]),
        mesh=mesh,
        in_specs=placed,
        out_specs=P(("groups", "replica"), "tensor"),
        check_vma=False,
    )
```

time: 127 us -> 123 us (0.969)
  waiting for transfers between devices: 10.8 us -> 6.13 us
    ppermute x2, waiting for transfers between devices: 5.97 us -> 0.37 us  [program(): from_cw[1], from_ccw[1] = (send_cw(cw_second), send_ccw(ccw_second))]
    pallas_call x5, Pallas kernels: 32.2 us -> 30.9 us  [product(): call(functools.partial(product_kernel, slots, starts, total is not None,...]
    ppermute x11 -> x13, starting transfers between devices: 15.2 us -> 16.2 us  [the longest x8 8.1 us: program(): from_cw[piece], from_ccw[piece] = (send_cw(moved[0]), send_ccw(moved[1]))]
    ppermute x11 -> x13, waiting for transfers between devices: 4.33 us -> 4.15 us  [the longest x8 4.13 us: program(): from_cw[piece], from_ccw[piece] = (send_cw(moved[0]), send_ccw(moved[1]))]
  transfers between devices with their start and end apart: 15 -> 17, of which waited for: 6 -> 3; matrix products, arithmetic and copies ran while one was open for 1% -> 1% of each run, Pallas kernels for 65% -> 65%
where the time goes in v4:
time: 123 us; the launch traced here: 122 us
  Pallas kernels  92.4 us (75%)
  starting transfers between devices  21.3 us (17%)
  waiting for transfers between devices  6.13 us (5%)
  local copies, waits for them, and re-layouts  1.26 us (1%)
  other arithmetic  1.26 us (1%)
    pallas_call x5, Pallas kernels, product(): call(functools.partial(product_kernel, slots, starts, total is not None,...  30.9 us
    pallas_call x1, Pallas kernels, query_delta(): call(functools.partial(delta_kernel, weight.shape[0], slots), (shape_of((...  12.6 us
    pallas_call x1, Pallas kernels, low_partials(): call(functools.partial(low_kernel, (reach - 1, reach, 0)), (shape_of((LOW...  12 us
    pallas_call x1, Pallas kernels, attention(): call(attention_kernel, shape_of((tokens, columns), BF16), grid_spec=prefe...  9.14 us
    ppermute x8, starting transfers between devices, program(): from_cw[piece], from_ccw[piece] = (send_cw(moved[0]), send_ccw(moved[1]))  8.1 us
    pallas_call x2, Pallas kernels, add_terms_low(): call(functools.partial(add_low_kernel, half, terms is not None), out, ADD...  7.34 us
    pallas_call x2, Pallas kernels, add_terms(): call(functools.partial(add_kernel, terms is not None), (shape_of((half, f...  5.9 us
    pallas_call x2, Pallas kernels, last_messages(): call(functools.partial(last_kernel, half, terms is not None), out, ADD_WE...  5.81 us
  transfers between devices with their start and end apart: 17, of which 3 were waited for; matrix products, arithmetic and copies ran while one was open for 1% of the time, Pallas kernels for 65%

profile of v4, /device:TPU:0, one launch (start us, length us, event | category | flops | bytes accessed | tf_op | source)
XLA Modules:
  0.0 122.5 jit_solution(10583865147508842766)
XLA Ops:
  1.3 4.1 %shard_map.100 = (bf16[256,1280]{1,0:T(8,128)(2,1)}, bf16[256,1280]{1,0:T(8,128)(2,1)}, bf16[512,1024]{1,0:T(8,128)(2,1)}) custom-call(s32[2,8]{1,0:T(2,128)} %dynamic-slice_bitcast_fusion.info_ref, bf16[512,1024]{1,0:T(8,128)(2,1)} %x_ref.3, f32[1,8192]{1,0:T(1,128)} %bitcast.5, bf16[1024,2048]{1,0:T(8,128)(2,1)} %refs_4_.3, bf16[1024,2048]{1,0:T(8,128)(2,1)} %refs_4_.3), custom_call_target="tpu_custom_call" | custom-call | bytes 1000 | tf_op jit(solution)/shard_map/pallas_call | solution.py:90
  5.4 3.0 %collective-permute-start = (bf16[256,1280]{1,0:T(8,128)(2,1)}, bf16[256,1280]{1,0:T(8,128)(2,1)}, u32[]{:S(2)}, u32[]{:S(2)}) collective-permute-start(bf16[256,1280]{1,0:T(8,128)(2,1)} %get-tuple-element.45), channel_id=1, source_target_pairs={{0,2},{2,4},{4,6},{6,7},{7,5},{5,3},{3,1},{1,0},{8,10},{10,12},{12... | collective-permute-start | bytes 1966088 | tf_op jit(solution)/shard_map/ppermute | solution.py:737
  8.4 12.0 %shard_map.101 = (f32[40,512]{1,0:T(8,128)}, f32[512,128]{1,0:T(8,128)}, bf16[272,1280]{1,0:T(8,128)(2,1)}, bf16[272,1280]{1,0:T(8,128)(2,1)}, bf16[512,256]{1,0:T(8,128)(2,1)}) custom-call(s32[2,8]{1,0:T(2,128)} %dynamic-slice_bitcast_fusion.info_ref, bf16[512,1024]{1,0:T(8,128)(2,1)} %get-tuple-element.55.packed_ref.refs_2_.refs_0_.x_ref, ...), custom_call_target="tpu_custom_call" | custom-call | bytes 1000 | tf_op jit(solution)/shard_map/pallas_call | solution.py:396
  20.4 2.1 %collective-permute-start.4 = (bf16[272,1280]{1,0:T(8,128)(2,1)}, bf16[272,1280]{1,0:T(8,128)(2,1)}, u32[]{:S(2)}, u32[]{:S(2)}) collective-permute-start(bf16[272,1280]{1,0:T(8,128)(2,1)} %get-tuple-element.53), channel_id=1, source_target_pairs={{0,2},{2,4},{4,6},{6,7},{7,5},{5,3},{3,1},{1,0},{8,10},{10,12},{12... | collective-permute-start | bytes 2088968 | tf_op jit(solution)/shard_map/ppermute | solution.py:741
  25.4 3.3 %shard_map.102 = (bf16[256,1280]{1,0:T(8,128)(2,1)}, bf16[256,1280]{1,0:T(8,128)(2,1)}) custom-call(s32[2,8]{1,0:T(2,128)} %dynamic-slice_bitcast_fusion.info_ref, bf16[256,1280]{1,0:T(8,128)(2,1)} %collective-permute-done.refs_0_, bf16[256,1280]{1,0:T(8,128)(2,1)} %collective-permute-done.1.refs_1_, ...), custom_call_target="tpu_custom_call", output_to_operand_aliasing={{0}: (1, {}), {1}: (2, {})} | custom-call | flops 9200000000 | bytes 1000 | tf_op jit(solution)/shard_map/pallas_call | solution.py:217
  30.7 5.7 %shard_map.103.refs_3_ = f32[256,1024]{1,0:T(8,128)} custom-call(s32[2,8]{1,0:T(2,128)} %dynamic-slice_bitcast_fusion.info_ref, bf16[512,1024]{1,0:T(8,128)(2,1)} %get-tuple-element.55.packed_ref.refs_2_.refs_0_.x_ref, bf16[256,1280]{1,0:T(8,128)(2,1)} %get-tuple-element.51.refs_1_, bf16[256,1280]{1,0:T(8,128)(2,1)} %get-tuple-element.52.refs_2_, ...), custom_call_target="tpu_custom_call" | custom-call | flops 9200000000 | bytes 1000 | tf_op jit(solution)/shard_map/pallas_call | solution.py:591
  36.4 4.6 %shard_map.104 = (bf16[2,512,256]{2,1,0:T(8,128)(2,1)}, bf16[2,512,256]{2,1,0:T(8,128)(2,1)}) custom-call(s32[2,8]{1,0:T(2,128)} %dynamic-slice_bitcast_fusion.info_ref, bf16[512,1024]{1,0:T(8,128)(2,1)} %get-tuple-element.55.packed_ref.refs_2_.refs_0_.x_ref, bf16[1024,2048]{1,0:T(8,128)(2,1)} %refs_4_.3, bf16[1024,2048]{1,0:T(8,128)(2,1)} %refs_4_.3), custom_call_target="tpu_custom_call" | custom-call | bytes 1000 | tf_op jit(solution)/shard_map/pallas_call | solution.py:159
  41.3 4.1 %shard_map.105 = (bf16[272,1280]{1,0:T(8,128)(2,1)}, bf16[272,1280]{1,0:T(8,128)(2,1)}, f32[40,512]{1,0:T(8,128)}) custom-call(s32[2,8]{1,0:T(2,128)} %dynamic-slice_bitcast_fusion.info_ref, f32[40,512]{1,0:T(8,128)} %get-tuple-element.48.low_ref, bf16[272,1280]{1,0:T(8,128)(2,1)} %collective-permute-done.4.refs_0_, ...), custom_call_target="tpu_custom_call" | custom-call | flops 9200000000 | bytes 1000 | tf_op jit(solution)/shard_map/pallas_call | solution.py:252
  45.5 2.0 %collective-permute-start.9 = (bf16[272,1280]{1,0:T(8,128)(2,1)}, bf16[272,1280]{1,0:T(8,128)(2,1)}, u32[]{:S(2)}, u32[]{:S(2)}) collective-permute-start(bf16[272,1280]{1,0:T(8,128)(2,1)} %get-tuple-element.59.refs_1_), channel_id=1, source_target_pairs={{0,2},{2,4},{4,6},{6,7},{7,5},{5,3},{3,1},{1,0},{8,10},{10,12},{12... | collective-permute-start | bytes 2088968 | tf_op jit(solution)/shard_map/ppermute | solution.py:773
  47.5 3.4 %collective-permute-start.8 = (f32[40,512]{1,0:T(8,128)}, f32[40,512]{1,0:T(8,128)}, u32[]{:S(2)}, u32[]{:S(2)}) collective-permute-start(f32[40,512]{1,0:T(8,128)} %get-tuple-element.66), channel_id=1, source_target_pairs={{0,7},{2,5},{4,3},{6,1},{7,0},{5,2},{3,4},{1,6},{8,15},{10,13},{12... | collective-permute-start | bytes 245768 | tf_op jit(solution)/shard_map/ppermute | solution.py:779
  50.9 5.7 %shard_map.106.total_b_ref = f32[256,1024]{1,0:T(8,128)} custom-call(s32[2,8]{1,0:T(2,128)} %dynamic-slice_bitcast_fusion.info_ref, bf16[512,1024]{1,0:T(8,128)(2,1)} %get-tuple-element.55.packed_ref.refs_2_.refs_0_.x_ref, bf16[272,1280]{1,0:T(8,128)(2,1)} %get-tuple-element.59.refs_1_, bf16[272,1280]{1,0:T(8,128)(2,1)} %get-tuple-element.60.refs_2_, ...), custom_call_target="tpu_custom_call" | custom-call | flops 9200000000 | bytes 1000 | tf_op jit(solution)/shard_map/pallas_call | solution.py:591
  56.7 2.6 %shard_map.107 = (bf16[256,1280]{1,0:T(8,128)(2,1)}, bf16[256,1280]{1,0:T(8,128)(2,1)}) custom-call(s32[2,8]{1,0:T(2,128)} %dynamic-slice_bitcast_fusion.info_ref, bf16[256,1280]{1,0:T(8,128)(2,1)} %collective-permute-done.2.refs_0_, bf16[256,1280]{1,0:T(8,128)(2,1)} %collective-permute-done.3.refs_1_, ...), custom_call_target="tpu_custom_call", output_to_operand_aliasing={{0}: (1, {}), {1}: (2, {})} | custom-call | flops 9200000000 | bytes 1000 | tf_op jit(solution)/shard_map/pallas_call | solution.py:217
  59.5 1.7 %collective-permute-start.7 = (bf16[256,1280]{1,0:T(8,128)(2,1)}, bf16[256,1280]{1,0:T(8,128)(2,1)}, u32[]{:S(2)}, u32[]{:S(2)}) collective-permute-start(bf16[256,1280]{1,0:T(8,128)(2,1)} %get-tuple-element.65.refs_1_), channel_id=1, source_target_pairs={{2,0},{4,2},{6,4},{7,6},{5,7},{3,5},{1,3},{0,1},{10,8},{12,10},{14... | collective-permute-start | bytes 1966088 | tf_op jit(solution)/shard_map/ppermute | solution.py:773
  61.2 5.8 %shard_map.108.total_a_ref = f32[256,1024]{1,0:T(8,128)} custom-call(s32[2,8]{1,0:T(2,128)} %dynamic-slice_bitcast_fusion.info_ref, bf16[256,1280]{1,0:T(8,128)(2,1)} %get-tuple-element.64.refs_0_, bf16[256,1280]{1,0:T(8,128)(2,1)} %get-tuple-element.65.refs_1_, bf16[8192,1024]{1,0:T(8,128)(2,1)} %w_ref.5, f32[256,1024]{1,0:T(8,128)} %shard_map.103.refs_3_), custom_call_target="tpu_custom_call" | custom-call | flops 9200000000 | bytes 1000 | tf_op jit(solution)/shard_map/pallas_call | solution.py:591
  67.1 4.1 %collective-permute-done.10.refs_1_.ccw_ref = bf16[272,1280]{1,0:T(8,128)(2,1)} collective-permute-done((bf16[272,1280]{1,0:T(8,128)(2,1)}, bf16[272,1280]{1,0:T(8,128)(2,1)}, u32[]{:S(2)}, u32[]{:S(2)}) %collective-permute-start.10) | collective-permute-done | bytes 696352 | tf_op jit(solution)/shard_map/ppermute | solution.py:773
  71.2 3.2 %shard_map.109 = (bf16[256,1280]{1,0:T(8,128)(2,1)}, bf16[256,1280]{1,0:T(8,128)(2,1)}) custom-call(s32[2,8]{1,0:T(2,128)} %dynamic-slice_bitcast_fusion.info_ref, f32[40,512]{1,0:T(8,128)} %get-tuple-element.48.low_ref, bf16[272,1280]{1,0:T(8,128)(2,1)} %collective-permute-done.9.refs_0_.cw_ref, bf16[272,1280]{1,0:T(8,128)(2,1)} %collective-permute-done.10.refs_1_.ccw_ref, ...), custom_call_target="tpu_custom_call" | custom-call | flops 9200000000 | bytes 1000 | tf_op jit(solution)/shard_map/pallas_call | solution.py:252
  74.4 2.0 %collective-permute-start.11 = (bf16[256,1280]{1,0:T(8,128)(2,1)}, bf16[256,1280]{1,0:T(8,128)(2,1)}, u32[]{:S(2)}, u32[]{:S(2)}) collective-permute-start(bf16[256,1280]{1,0:T(8,128)(2,1)} %get-tuple-element.76), channel_id=1, source_target_pairs={{0,2},{2,4},{4,6},{6,7},{7,5},{5,3},{3,1},{1,0},{8,10},{10,12},{12... | collective-permute-start | bytes 1966088 | tf_op jit(solution)/shard_map/ppermute | solution.py:773
  76.4 12.6 %shard_map.110 = (f32[256,1024]{1,0:T(8,128)}, f32[256,1024]{1,0:T(8,128)}, f32[512,128]{1,0:T(8,128)}) custom-call(s32[2,8]{1,0:T(2,128)} %dynamic-slice_bitcast_fusion.info_ref, f32[40,512]{1,0:T(8,128)} %get-tuple-element.48.low_ref, f32[40,512]{1,0:T(8,128)} %collective-permute-done.8.opposite_ref, ...), custom_call_target="tpu_custom_call" | custom-call | flops 9200000000 | bytes 1000 | tf_op jit(solution)/shard_map/pallas_call | solution.py:512
  89.1 2.9 %shard_map.113 = (bf16[128,1536]{1,0:T(8,128)(2,1)}, bf16[128,1024]{1,0:T(8,128)(2,1)}) custom-call(s32[2,8]{1,0:T(2,128)} %dynamic-slice_bitcast_fusion.info_ref, bf16[256,1280]{1,0:T(8,128)(2,1)} %collective-permute-done.6.refs_0_.with_sums, bf16[256,1280]{1,0:T(8,128)(2,1)} %collective-permute-done.7.refs_1_.other.refs_6_, ...), custom_call_target="tpu_custom_call" | custom-call | flops 9200000000 | bytes 1000 | tf_op jit(solution)/shard_map/pallas_call | solution.py:286
  94.0 6.9 %shard_map.111.total_a_ref = f32[256,1024]{1,0:T(8,128)} custom-call(s32[2,8]{1,0:T(2,128)} %dynamic-slice_bitcast_fusion.info_ref, bf16[256,1280]{1,0:T(8,128)(2,1)} %collective-permute-done.6.refs_0_.with_sums, bf16[256,1280]{1,0:T(8,128)(2,1)} %collective-permute-done.7.refs_1_.other.refs_6_, bf16[8192,1024]{1,0:T(8,128)(2,1)} %w_ref.5, ...), custom_call_target="tpu_custom_call" | custom-call | flops 9200000000 | bytes 1000 | tf_op jit(solution)/shard_map/pallas_call | solution.py:591
  100.9 2.9 %shard_map.114 = (bf16[128,1536]{1,0:T(8,128)(2,1)}, bf16[128,1024]{1,0:T(8,128)(2,1)}) custom-call(s32[2,8]{1,0:T(2,128)} %dynamic-slice_bitcast_fusion.info_ref, bf16[256,1280]{1,0:T(8,128)(2,1)} %collective-permute-done.12.refs_1_.with_sums, bf16[256,1280]{1,0:T(8,128)(2,1)} %collective-permute-done.11.refs_0_.other.refs_9_, ...), custom_call_target="tpu_custom_call" | custom-call | flops 9200000000 | bytes 1000 | tf_op jit(solution)/shard_map/pallas_call | solution.py:286
  104.2 2.2 %collective-permute-start.16 = (bf16[128,1024]{1,0:T(8,128)(2,1)}, bf16[128,1024]{1,0:T(8,128)(2,1)}, u32[]{:S(2)}, u32[]{:S(2)}) collective-permute-start(bf16[128,1024]{1,0:T(8,128)(2,1)} %get-tuple-element.84), channel_id=1, source_target_pairs={{0,2},{2,4},{4,6},{6,7},{7,5},{5,3},{3,1},{1,0},{8,10},{10,12},{12... | collective-permute-start | bytes 786440 | tf_op jit(solution)/shard_map/ppermute | solution.py:764
  106.4 6.8 %shard_map.112.total_b_ref = f32[256,1024]{1,0:T(8,128)} custom-call(s32[2,8]{1,0:T(2,128)} %dynamic-slice_bitcast_fusion.info_ref, bf16[256,1280]{1,0:T(8,128)(2,1)} %collective-permute-done.11.refs_0_.other.refs_9_, bf16[256,1280]{1,0:T(8,128)(2,1)} %collective-permute-done.12.refs_1_.with_sums, bf16[8192,1024]{1,0:T(8,128)(2,1)} %w_ref.5, ...), custom_call_target="tpu_custom_call" | custom-call | flops 9200000000 | bytes 1000 | tf_op jit(solution)/shard_map/pallas_call | solution.py:591
  113.3 9.1 %shard_map.115 = bf16[512,1024]{1,0:T(8,128)(2,1)} custom-call(s32[2,8]{1,0:T(2,128)} %dynamic-slice_bitcast_fusion.info_ref, s32[2]{0:T(128)} %lengths_ref.1, f32[256,1024]{1,0:T(8,128)} %shard_map.111.total_a_ref, f32[256,1024]{1,0:T(8,128)} %shard_map.112.total_b_ref, f32[512,128]{1,0:T(8,128)} %get-tuple-element.72.refs_4_.inv_ref, ...), custom_call_target="tpu_custom_call" | custom-call | bytes 1000 | tf_op jit(solution)/shard_map/pallas_call | solution.py:680
  (31 shorter events, 9.3 us)
Async XLA Ops:
  5.4 18.4 %collective-permute-start = (bf16[256,1280]{1,0:T(8,128)(2,1)}, bf16[256,1280]{1,0:T(8,128)(2,1)}, u32[]{:S(2)}, u32[]{:S(2)}) collective-permute-start(bf16[256,1280]{1,0:T(8,128)(2,1)} %get-tuple-element.45), channel_id=1, source_target_pairs={{0,2},{2,4},{4,6},{6,7},{7,5},{5,3},{3,1},{1,0},{8,10},{10,12},{12... | collective-permute-start | bytes 1966088 | tf_op jit(solution)/shard_map/ppermute | solution.py:737
  8.4 17.0 %collective-permute-start.1 = (bf16[256,1280]{1,0:T(8,128)(2,1)}, bf16[256,1280]{1,0:T(8,128)(2,1)}, u32[]{:S(2)}, u32[]{:S(2)}) collective-permute-start(bf16[256,1280]{1,0:T(8,128)(2,1)} %get-tuple-element.46), channel_id=1, source_target_pairs={{2,0},{4,2},{6,4},{7,6},{5,7},{3,5},{1,3},{0,1},{10,8},{12,10},{14... | collective-permute-start | bytes 1966088 | tf_op jit(solution)/shard_map/ppermute | solution.py:737
  20.4 20.6 %collective-permute-start.4 = (bf16[272,1280]{1,0:T(8,128)(2,1)}, bf16[272,1280]{1,0:T(8,128)(2,1)}, u32[]{:S(2)}, u32[]{:S(2)}) collective-permute-start(bf16[272,1280]{1,0:T(8,128)(2,1)} %get-tuple-element.53), channel_id=1, source_target_pairs={{0,2},{2,4},{4,6},{6,7},{7,5},{5,3},{3,1},{1,0},{8,10},{10,12},{12... | collective-permute-start | bytes 2088968 | tf_op jit(solution)/shard_map/ppermute | solution.py:741
  22.5 18.9 %collective-permute-start.5 = (bf16[272,1280]{1,0:T(8,128)(2,1)}, bf16[272,1280]{1,0:T(8,128)(2,1)}, u32[]{:S(2)}, u32[]{:S(2)}) collective-permute-start(bf16[272,1280]{1,0:T(8,128)(2,1)} %get-tuple-element.54), channel_id=1, source_target_pairs={{2,0},{4,2},{6,4},{7,6},{5,7},{3,5},{1,3},{0,1},{10,8},{12,10},{14... | collective-permute-start | bytes 2088968 | tf_op jit(solution)/shard_map/ppermute | solution.py:741
  28.7 27.9 %collective-permute-start.2 = (bf16[256,1280]{1,0:T(8,128)(2,1)}, bf16[256,1280]{1,0:T(8,128)(2,1)}, u32[]{:S(2)}, u32[]{:S(2)}) collective-permute-start(bf16[256,1280]{1,0:T(8,128)(2,1)} %get-tuple-element.51.refs_1_), channel_id=1, source_target_pairs={{0,2},{2,4},{4,6},{6,7},{7,5},{5,3},{3,1},{1,0},{8,10},{10,12},{12... | collective-permute-start | bytes 1966088 | tf_op jit(solution)/shard_map/ppermute | solution.py:773
  30.3 26.4 %collective-permute-start.3 = (bf16[256,1280]{1,0:T(8,128)(2,1)}, bf16[256,1280]{1,0:T(8,128)(2,1)}, u32[]{:S(2)}, u32[]{:S(2)}) collective-permute-start(bf16[256,1280]{1,0:T(8,128)(2,1)} %get-tuple-element.52.refs_2_), channel_id=1, source_target_pairs={{2,0},{4,2},{6,4},{7,6},{5,7},{3,5},{1,3},{0,1},{10,8},{12,10},{14... | collective-permute-start | bytes 1966088 | tf_op jit(solution)/shard_map/ppermute | solution.py:773
  45.5 25.7 %collective-permute-start.10 = (bf16[272,1280]{1,0:T(8,128)(2,1)}, bf16[272,1280]{1,0:T(8,128)(2,1)}, u32[]{:S(2)}, u32[]{:S(2)}) collective-permute-start(bf16[272,1280]{1,0:T(8,128)(2,1)} %get-tuple-element.60.refs_2_), channel_id=1, source_target_pairs={{2,0},{4,2},{6,4},{7,6},{5,7},{3,5},{1,3},{0,1},{10,8},{12,10},{14... | collective-permute-start | bytes 2088968 | tf_op jit(solution)/shard_map/ppermute | solution.py:773
  45.5 25.7 %collective-permute-start.9 = (bf16[272,1280]{1,0:T(8,128)(2,1)}, bf16[272,1280]{1,0:T(8,128)(2,1)}, u32[]{:S(2)}, u32[]{:S(2)}) collective-permute-start(bf16[272,1280]{1,0:T(8,128)(2,1)} %get-tuple-element.59.refs_1_), channel_id=1, source_target_pairs={{0,2},{2,4},{4,6},{6,7},{7,5},{5,3},{3,1},{1,0},{8,10},{10,12},{12... | collective-permute-start | bytes 2088968 | tf_op jit(solution)/shard_map/ppermute | solution.py:773
  47.5 26.9 %collective-permute-start.8 = (f32[40,512]{1,0:T(8,128)}, f32[40,512]{1,0:T(8,128)}, u32[]{:S(2)}, u32[]{:S(2)}) collective-permute-start(f32[40,512]{1,0:T(8,128)} %get-tuple-element.66), channel_id=1, source_target_pairs={{0,7},{2,5},{4,3},{6,1},{7,0},{5,2},{3,4},{1,6},{8,15},{10,13},{12... | collective-permute-start | bytes 245768 | tf_op jit(solution)/shard_map/ppermute | solution.py:779
  59.2 29.8 %collective-permute-start.6 = (bf16[256,1280]{1,0:T(8,128)(2,1)}, bf16[256,1280]{1,0:T(8,128)(2,1)}, u32[]{:S(2)}, u32[]{:S(2)}) collective-permute-start(bf16[256,1280]{1,0:T(8,128)(2,1)} %get-tuple-element.64.refs_0_), channel_id=1, source_target_pairs={{0,2},{2,4},{4,6},{6,7},{7,5},{5,3},{3,1},{1,0},{8,10},{10,12},{12... | collective-permute-start | bytes 1966088 | tf_op jit(solution)/shard_map/ppermute | solution.py:773
  59.5 29.6 %collective-permute-start.7 = (bf16[256,1280]{1,0:T(8,128)(2,1)}, bf16[256,1280]{1,0:T(8,128)(2,1)}, u32[]{:S(2)}, u32[]{:S(2)}) collective-permute-start(bf16[256,1280]{1,0:T(8,128)(2,1)} %get-tuple-element.65.refs_1_), channel_id=1, source_target_pairs={{2,0},{4,2},{6,4},{7,6},{5,7},{3,5},{1,3},{0,1},{10,8},{12,10},{14... | collective-permute-start | bytes 1966088 | tf_op jit(solution)/shard_map/ppermute | solution.py:773
  74.4 26.4 %collective-permute-start.12 = (bf16[256,1280]{1,0:T(8,128)(2,1)}, bf16[256,1280]{1,0:T(8,128)(2,1)}, u32[]{:S(2)}, u32[]{:S(2)}) collective-permute-start(bf16[256,1280]{1,0:T(8,128)(2,1)} %get-tuple-element.69), channel_id=1, source_target_pairs={{2,0},{4,2},{6,4},{7,6},{5,7},{3,5},{1,3},{0,1},{10,8},{12,10},{14... | collective-permute-start | bytes 1966088 | tf_op jit(solution)/shard_map/ppermute | solution.py:773
  74.4 26.4 %collective-permute-start.11 = (bf16[256,1280]{1,0:T(8,128)(2,1)}, bf16[256,1280]{1,0:T(8,128)(2,1)}, u32[]{:S(2)}, u32[]{:S(2)}) collective-permute-start(bf16[256,1280]{1,0:T(8,128)(2,1)} %get-tuple-element.76), channel_id=1, source_target_pairs={{0,2},{2,4},{4,6},{6,7},{7,5},{5,3},{3,1},{1,0},{8,10},{10,12},{12... | collective-permute-start | bytes 1966088 | tf_op jit(solution)/shard_map/ppermute | solution.py:773
  91.9 21.4 %collective-permute-start.13 = (bf16[128,1536]{1,0:T(8,128)(2,1)}, bf16[128,1536]{1,0:T(8,128)(2,1)}, u32[]{:S(2)}, u32[]{:S(2)}) collective-permute-start(bf16[128,1536]{1,0:T(8,128)(2,1)} %get-tuple-element.81), channel_id=1, source_target_pairs={{0,2},{2,4},{4,6},{6,7},{7,5},{5,3},{3,1},{1,0},{8,10},{10,12},{12... | collective-permute-start | bytes 1179656 | tf_op jit(solution)/shard_map/ppermute | solution.py:762
  93.5 19.8 %collective-permute-start.14 = (bf16[128,1024]{1,0:T(8,128)(2,1)}, bf16[128,1024]{1,0:T(8,128)(2,1)}, u32[]{:S(2)}, u32[]{:S(2)}) collective-permute-start(bf16[128,1024]{1,0:T(8,128)(2,1)} %get-tuple-element.82), channel_id=1, source_target_pairs={{2,0},{4,2},{6,4},{7,6},{5,7},{3,5},{1,3},{0,1},{10,8},{12,10},{14... | collective-permute-start | bytes 786440 | tf_op jit(solution)/shard_map/ppermute | solution.py:762
  103.8 9.5 %collective-permute-start.15 = (bf16[128,1536]{1,0:T(8,128)(2,1)}, bf16[128,1536]{1,0:T(8,128)(2,1)}, u32[]{:S(2)}, u32[]{:S(2)}) collective-permute-start(bf16[128,1536]{1,0:T(8,128)(2,1)} %get-tuple-element.83), channel_id=1, source_target_pairs={{2,0},{4,2},{6,4},{7,6},{5,7},{3,5},{1,3},{0,1},{10,8},{12,10},{14... | collective-permute-start | bytes 1179656 | tf_op jit(solution)/shard_map/ppermute | solution.py:764
  104.2 9.1 %collective-permute-start.16 = (bf16[128,1024]{1,0:T(8,128)(2,1)}, bf16[128,1024]{1,0:T(8,128)(2,1)}, u32[]{:S(2)}, u32[]{:S(2)}) collective-permute-start(bf16[128,1024]{1,0:T(8,128)(2,1)} %get-tuple-element.84), channel_id=1, source_target_pairs={{0,2},{2,4},{4,6},{6,7},{7,5},{5,3},{3,1},{1,0},{8,10},{10,12},{12... | collective-permute-start | bytes 786440 | tf_op jit(solution)/shard_map/ppermute | solution.py:764

commit v5 on v4

--- a/solution.py
+++ b/solution.py
@@ -145,7 +145,14 @@
     message[half + row : half + row + ADAPTER_RANK, lanes] = block
 
 
-def terms_kernel(info_ref, x_ref, ahead_w_ref, behind_w_ref, ahead_ref, behind_ref):
+def terms_kernel(
+    info_ref, x_ref, ahead_w_ref, behind_w_ref, own_w_ref, ahead_ref, behind_ref, own_ref
+):
+    @pl.when(pl.program_id(0) == 0)
+    def _():
+        own = jnp.dot(x_ref[...], own_w_ref[...], preferred_element_type=F32)
+        own_ref[...] = own.astype(BF16)
+
     for w_ref, out_ref in ((ahead_w_ref, ahead_ref), (behind_w_ref, behind_ref)):
         out_ref[0] = jnp.dot(x_ref[...], w_ref[...], preferred_element_type=F32).astype(BF16)
 
@@ -158,7 +165,7 @@
     block = pl.BlockSpec((1, rows, pair), lambda i, info: (i, 0, 0))
     return call(
         terms_kernel,
-        (out, out),
+        (out, out, shape_of((rows, pair), BF16)),
         grid_spec=prefetch(
             1,
             (number,),
@@ -166,10 +173,11 @@
                 whole((rows, width)),
                 pl.BlockSpec((width, pair), lambda i, info: (0, info[1, 1 + i])),
                 pl.BlockSpec((width, pair), lambda i, info: (0, info[1, count - 1 - i])),
+                pl.BlockSpec((width, pair), lambda i, info: (0, info[1, 0])),
             ],
-            (block, block),
+            (block, block, whole((rows, pair))),
         ),
-    )(info, packed, weight, weight)
+    )(info, packed, weight, weight, weight)
 
 
 def own_term(block_ref, w_ref):
@@ -312,7 +320,7 @@
 
 def low_kernel(
     aways, info_ref, packed_ref, w_ref, index_ref, mix_ref, x_ref, kv_ref, out_ref, side_ref,
-    cw_ref, ccw_ref, own_ref, acc_ref, group_ref, squares_ref, x_s, columns_s, messages_s, sems,
+    cw_ref, ccw_ref, acc_ref, group_ref, squares_ref, x_s, columns_s, messages_s, sems,
     out_sems,
 ):
     step = pl.program_id(0)
@@ -355,9 +363,6 @@
         for i in range(2):
             write_message(messages_s.at[i], packed_ref[half:, :], columns_s.at[i])
             writes[2 * i].start()
-        own = jnp.dot(packed_ref[...], columns_s[2], preferred_element_type=F32)
-        own_ref[...] = own.astype(BF16)
-
     chunk = min(CHUNK, tile)
     for first in range(0, tile, chunk):
         product = jnp.dot(
@@ -394,10 +399,9 @@
     message = (tokens // 2 + low_places(tokens, width + pair)[0], width + pair)
     anywhere = pl.BlockSpec(memory_space=pl.ANY)
     return call(
-        functools.partial(low_kernel, (reach - 1, reach, 0)),
+        functools.partial(low_kernel, (reach - 1, reach)),
         (shape_of((LOW_ROWS, tokens), F32), shape_of((tokens, LANES), F32))
-        + (shape_of(message, BF16),) * 2
-        + (shape_of((tokens, pair), BF16),),
+        + (shape_of(message, BF16),) * 2,
         grid_spec=prefetch(
             1,
             (columns // tile,),
@@ -409,16 +413,15 @@
                 anywhere,
                 anywhere,
             ],
-            (whole((LOW_ROWS, tokens)), whole((tokens, LANES)), anywhere, anywhere)
-            + (whole((tokens, pair)),),
+            (whole((LOW_ROWS, tokens)), whole((tokens, LANES)), anywhere, anywhere),
             [
                 pltpu.VMEM((2, tokens, LANES), F32),
                 pltpu.VMEM((2, tokens, LANES), F32),
                 pltpu.VMEM((tokens, LANES), F32),
                 pltpu.VMEM((tokens, width), BF16),
-                pltpu.VMEM((3, width, pair), BF16),
+                pltpu.VMEM((2, width, pair), BF16),
                 pltpu.VMEM((2, *message), BF16),
-                pltpu.SemaphoreType.DMA((4,)),
+                pltpu.SemaphoreType.DMA((3,)),
                 pltpu.SemaphoreType.DMA((2, 2)),
             ],
         ),
@@ -609,9 +612,7 @@
 
 def rotate(values, cosines, sines):
     lane = lax.broadcasted_iota(jnp.int32, values.shape, 1)
-    after = pltpu.roll(values, LANES - 1, 1)
-    before = pltpu.roll(values, 1, 1)
-    other = jnp.where(lane % 2 == 0, after, before)
+    other = jnp.take_along_axis(values, lane ^ 1, axis=1, mode="promise_in_bounds")
     return values * cosines + other * sines
 
 
@@ -637,7 +638,8 @@
             pair = pair * inv_ref[span, 0:1]
             key = rotate(pair[:, :HEAD_WIDTH], cos_ref[...], sin_ref[...])
             key_s[prompt] = key.astype(BF16)
-            value_s[prompt] = pair[:, HEAD_WIDTH:].astype(BF16)
+            value_s[prompt, :, :HEAD_WIDTH] = pair[:, HEAD_WIDTH:].astype(BF16)
+            value_s[prompt, :, HEAD_WIDTH:] = jnp.ones((SLOT, HEAD_WIDTH), BF16)
             seen = (col <= row) & (col < lengths_ref[prompt])
             bias_s[prompt] = jnp.where(seen, 0.0, -1e30)
 
@@ -656,9 +658,9 @@
             scores = scores * factor + bias_s[prompt]
             top = jnp.max(scores, axis=1, keepdims=True)
             weights = jnp.exp2(scores - top)
-            totals = jnp.sum(weights, axis=1, keepdims=True)
             mixed = jnp.dot(weights.astype(BF16), value_s[prompt], preferred_element_type=F32)
-            mixed = jnp.where(row_narrow < lengths_ref[prompt], mixed * (1.0 / totals), 0.0)
+            mixed = mixed[:, :HEAD_WIDTH] / mixed[:, HEAD_WIDTH:]
+            mixed = jnp.where(row_narrow < lengths_ref[prompt], mixed, 0.0)
             out_ref[rows, span] = mixed.astype(BF16)
 
 
@@ -698,7 +700,7 @@
             [
                 pltpu.VMEM((tokens, width), BF16),
                 pltpu.VMEM((2, SLOT, HEAD_WIDTH), BF16),
-                pltpu.VMEM((2, SLOT, HEAD_WIDTH), BF16),
+                pltpu.VMEM((2, SLOT, 2 * HEAD_WIDTH), BF16),
                 pltpu.VMEM((2, SLOT, SLOT), F32),
             ],
         ),
@@ -735,7 +737,7 @@
 
     cw_first, ccw_first, packed = scale_rows(info, x, scale, wkv, reach)
     from_cw, from_ccw = [send_cw(cw_first), None], [send_ccw(ccw_first), None]
-    low, side, cw_second, ccw_second, own = low_partials(
+    low, side, cw_second, ccw_second = low_partials(
         info, x, packed, wdown, index, mix, wkv, reach
     )
     from_cw[1], from_ccw[1] = send_cw(cw_second), send_ccw(ccw_second)
@@ -787,7 +789,7 @@
                 totals[piece] = product(info, totals[piece], sources, wq, half, inv, piece)
                 done = totals[piece]
             if step == 1 and piece == 0:
-                late = late_terms(info, after(packed, done), wkv, count)
+                *late, own = late_terms(info, after(packed, done), wkv, count)
                 done = late[0]
             if step == 1 and piece == 1:
                 terms = late

time: 123 us -> 122 us (level)
  Pallas kernels: 92.4 us -> 90.8 us
    ppermute x8, waiting for transfers between devices: 4.13 us -> 2.01 us  [program(): from_cw[piece], from_ccw[piece] = (send_cw(moved[0]), send_ccw(moved[1]))]
    pallas_call x1, Pallas kernels: 9.14 us -> 7.48 us  [attention(): call(attention_kernel, shape_of((tokens, columns), BF16), grid_spec=prefe...]
  transfers between devices with their start and end apart: 17 -> 17, of which waited for: 3 -> 4; matrix products, arithmetic and copies ran while one was open for 1% -> 1% of each run, Pallas kernels for 65% -> 65%
where the time goes in v5:
time: 122 us; the launch traced here: 121 us
  Pallas kernels  90.8 us (74%)
  starting transfers between devices  22.2 us (18%)
  waiting for transfers between devices  5.3 us (4%)
  other arithmetic  1.28 us (1%)
  local copies, waits for them, and re-layouts  1.26 us (1%)
    pallas_call x5, Pallas kernels, product(): call(functools.partial(product_kernel, slots, starts, total is not None,...  30.9 us
    pallas_call x1, Pallas kernels, query_delta(): call(functools.partial(delta_kernel, weight.shape[0], slots), (shape_of((...  12.6 us
    pallas_call x1, Pallas kernels, low_partials(): call(functools.partial(low_kernel, (reach - 1, reach)), (shape_of((LOW_RO...  11.5 us
    ppermute x8, starting transfers between devices, program(): from_cw[piece], from_ccw[piece] = (send_cw(moved[0]), send_ccw(moved[1]))  8.73 us
    pallas_call x1, Pallas kernels, attention(): call(attention_kernel, shape_of((tokens, columns), BF16), grid_spec=prefe...  7.48 us
    pallas_call x2, Pallas kernels, add_terms_low(): call(functools.partial(add_low_kernel, half, terms is not None), out, ADD...  7.3 us
    pallas_call x2, Pallas kernels, add_terms(): call(functools.partial(add_kernel, terms is not None), (shape_of((half, f...  5.9 us
    pallas_call x2, Pallas kernels, last_messages(): call(functools.partial(last_kernel, half, terms is not None), out, ADD_WE...  5.81 us
  transfers between devices with their start and end apart: 17, of which 4 were waited for; matrix products, arithmetic and copies ran while one was open for 1% of the time, Pallas kernels for 65%

profile of v5, /device:TPU:0, one launch (start us, length us, event | category | flops | bytes accessed | tf_op | source)
XLA Modules:
  0.0 121.1 jit_solution(12908081015124710578)
XLA Ops:
  1.3 4.1 %shard_map.100 = (bf16[256,1280]{1,0:T(8,128)(2,1)}, bf16[256,1280]{1,0:T(8,128)(2,1)}, bf16[512,1024]{1,0:T(8,128)(2,1)}) custom-call(s32[2,8]{1,0:T(2,128)} %dynamic-slice_bitcast_fusion.info_ref, bf16[512,1024]{1,0:T(8,128)(2,1)} %x_ref.3, f32[1,8192]{1,0:T(1,128)} %bitcast.5, bf16[1024,2048]{1,0:T(8,128)(2,1)} %refs_4_.3, bf16[1024,2048]{1,0:T(8,128)(2,1)} %refs_4_.3), custom_call_target="tpu_custom_call" | custom-call | bytes 1000 | tf_op jit(solution)/shard_map/pallas_call | solution.py:90
  5.4 3.0 %collective-permute-start = (bf16[256,1280]{1,0:T(8,128)(2,1)}, bf16[256,1280]{1,0:T(8,128)(2,1)}, u32[]{:S(2)}, u32[]{:S(2)}) collective-permute-start(bf16[256,1280]{1,0:T(8,128)(2,1)} %get-tuple-element.45), channel_id=1, source_target_pairs={{0,2},{2,4},{4,6},{6,7},{7,5},{5,3},{3,1},{1,0},{8,10},{10,12},{12... | collective-permute-start | bytes 1966088 | tf_op jit(solution)/shard_map/ppermute | solution.py:739
  8.4 11.5 %shard_map.101 = (f32[40,512]{1,0:T(8,128)}, f32[512,128]{1,0:T(8,128)}, bf16[272,1280]{1,0:T(8,128)(2,1)}, bf16[272,1280]{1,0:T(8,128)(2,1)}) custom-call(s32[2,8]{1,0:T(2,128)} %dynamic-slice_bitcast_fusion.info_ref, bf16[512,1024]{1,0:T(8,128)(2,1)} %get-tuple-element.55.packed_ref.refs_2_.refs_0_.x_ref, bf16[1024,4096]{1,0:T(8,128)(2,1)} %w_ref.3, ...), custom_call_target="tpu_custom_call" | custom-call | bytes 1000 | tf_op jit(solution)/shard_map/pallas_call | solution.py:401
  19.9 2.1 %collective-permute-start.4 = (bf16[272,1280]{1,0:T(8,128)(2,1)}, bf16[272,1280]{1,0:T(8,128)(2,1)}, u32[]{:S(2)}, u32[]{:S(2)}) collective-permute-start(bf16[272,1280]{1,0:T(8,128)(2,1)} %get-tuple-element.53), channel_id=1, source_target_pairs={{0,2},{2,4},{4,6},{6,7},{7,5},{5,3},{3,1},{1,0},{8,10},{10,12},{12... | collective-permute-start | bytes 2088968 | tf_op jit(solution)/shard_map/ppermute | solution.py:743
  25.8 3.3 %shard_map.102 = (bf16[256,1280]{1,0:T(8,128)(2,1)}, bf16[256,1280]{1,0:T(8,128)(2,1)}) custom-call(s32[2,8]{1,0:T(2,128)} %dynamic-slice_bitcast_fusion.info_ref, bf16[256,1280]{1,0:T(8,128)(2,1)} %collective-permute-done.refs_0_, bf16[256,1280]{1,0:T(8,128)(2,1)} %collective-permute-done.1.refs_1_, ...), custom_call_target="tpu_custom_call", output_to_operand_aliasing={{0}: (1, {}), {1}: (2, {})} | custom-call | flops 9200000000 | bytes 1000 | tf_op jit(solution)/shard_map/pallas_call | solution.py:225
  31.2 5.7 %shard_map.103.refs_3_ = f32[256,1024]{1,0:T(8,128)} custom-call(s32[2,8]{1,0:T(2,128)} %dynamic-slice_bitcast_fusion.info_ref, bf16[512,1024]{1,0:T(8,128)(2,1)} %get-tuple-element.55.packed_ref.refs_2_.refs_0_.x_ref, bf16[256,1280]{1,0:T(8,128)(2,1)} %get-tuple-element.51.refs_1_, bf16[256,1280]{1,0:T(8,128)(2,1)} %get-tuple-element.52.refs_2_, ...), custom_call_target="tpu_custom_call" | custom-call | flops 9200000000 | bytes 1000 | tf_op jit(solution)/shard_map/pallas_call | solution.py:594
  36.9 5.2 %shard_map.104 = (bf16[2,512,256]{2,1,0:T(8,128)(2,1)}, bf16[2,512,256]{2,1,0:T(8,128)(2,1)}, bf16[512,256]{1,0:T(8,128)(2,1)}) custom-call(s32[2,8]{1,0:T(2,128)} %dynamic-slice_bitcast_fusion.info_ref, bf16[512,1024]{1,0:T(8,128)(2,1)} %get-tuple-element.55.packed_ref.refs_2_.refs_0_.x_ref, bf16[1024,2048]{1,0:T(8,128)(2,1)} %refs_4_.3, ...), custom_call_target="tpu_custom_call" | custom-call | bytes 1000 | tf_op jit(solution)/shard_map/pallas_call | solution.py:166
  42.1 4.1 %shard_map.105 = (bf16[272,1280]{1,0:T(8,128)(2,1)}, bf16[272,1280]{1,0:T(8,128)(2,1)}, f32[40,512]{1,0:T(8,128)}) custom-call(s32[2,8]{1,0:T(2,128)} %dynamic-slice_bitcast_fusion.info_ref, f32[40,512]{1,0:T(8,128)} %get-tuple-element.48.low_ref, bf16[272,1280]{1,0:T(8,128)(2,1)} %collective-permute-done.4.refs_0_, ...), custom_call_target="tpu_custom_call" | custom-call | flops 9200000000 | bytes 1000 | tf_op jit(solution)/shard_map/pallas_call | solution.py:260
  48.2 3.5 %collective-permute-start.8 = (f32[40,512]{1,0:T(8,128)}, f32[40,512]{1,0:T(8,128)}, u32[]{:S(2)}, u32[]{:S(2)}) collective-permute-start(f32[40,512]{1,0:T(8,128)} %get-tuple-element.66), channel_id=1, source_target_pairs={{0,7},{2,5},{4,3},{6,1},{7,0},{5,2},{3,4},{1,6},{8,15},{10,13},{12... | collective-permute-start | bytes 245768 | tf_op jit(solution)/shard_map/ppermute | solution.py:781
  51.7 5.7 %shard_map.106.total_b_ref = f32[256,1024]{1,0:T(8,128)} custom-call(s32[2,8]{1,0:T(2,128)} %dynamic-slice_bitcast_fusion.info_ref, bf16[512,1024]{1,0:T(8,128)(2,1)} %get-tuple-element.55.packed_ref.refs_2_.refs_0_.x_ref, bf16[272,1280]{1,0:T(8,128)(2,1)} %get-tuple-element.59.refs_1_, bf16[272,1280]{1,0:T(8,128)(2,1)} %get-tuple-element.60.refs_2_, ...), custom_call_target="tpu_custom_call" | custom-call | flops 9200000000 | bytes 1000 | tf_op jit(solution)/shard_map/pallas_call | solution.py:594
  57.5 2.6 %shard_map.107 = (bf16[256,1280]{1,0:T(8,128)(2,1)}, bf16[256,1280]{1,0:T(8,128)(2,1)}) custom-call(s32[2,8]{1,0:T(2,128)} %dynamic-slice_bitcast_fusion.info_ref, bf16[256,1280]{1,0:T(8,128)(2,1)} %collective-permute-done.2.refs_0_, bf16[256,1280]{1,0:T(8,128)(2,1)} %collective-permute-done.3.refs_1_, ...), custom_call_target="tpu_custom_call", output_to_operand_aliasing={{0}: (1, {}), {1}: (2, {})} | custom-call | flops 9200000000 | bytes 1000 | tf_op jit(solution)/shard_map/pallas_call | solution.py:225
  60.0 2.0 %collective-permute-start.7 = (bf16[256,1280]{1,0:T(8,128)(2,1)}, bf16[256,1280]{1,0:T(8,128)(2,1)}, u32[]{:S(2)}, u32[]{:S(2)}) collective-permute-start(bf16[256,1280]{1,0:T(8,128)(2,1)} %get-tuple-element.65.refs_1_), channel_id=1, source_target_pairs={{2,0},{4,2},{6,4},{7,6},{5,7},{3,5},{1,3},{0,1},{10,8},{12,10},{14... | collective-permute-start | bytes 1966088 | tf_op jit(solution)/shard_map/ppermute | solution.py:775
  62.1 5.8 %shard_map.108.total_a_ref = f32[256,1024]{1,0:T(8,128)} custom-call(s32[2,8]{1,0:T(2,128)} %dynamic-slice_bitcast_fusion.info_ref, bf16[256,1280]{1,0:T(8,128)(2,1)} %get-tuple-element.64.refs_0_, bf16[256,1280]{1,0:T(8,128)(2,1)} %get-tuple-element.65.refs_1_, bf16[8192,1024]{1,0:T(8,128)(2,1)} %w_ref.5, f32[256,1024]{1,0:T(8,128)} %shard_map.103.refs_3_), custom_call_target="tpu_custom_call" | custom-call | flops 9200000000 | bytes 1000 | tf_op jit(solution)/shard_map/pallas_call | solution.py:594
  67.9 2.0 %collective-permute-done.10.refs_1_.ccw_ref = bf16[272,1280]{1,0:T(8,128)(2,1)} collective-permute-done((bf16[272,1280]{1,0:T(8,128)(2,1)}, bf16[272,1280]{1,0:T(8,128)(2,1)}, u32[]{:S(2)}, u32[]{:S(2)}) %collective-permute-start.10) | collective-permute-done | bytes 696352 | tf_op jit(solution)/shard_map/ppermute | solution.py:775
  69.9 3.2 %shard_map.109 = (bf16[256,1280]{1,0:T(8,128)(2,1)}, bf16[256,1280]{1,0:T(8,128)(2,1)}) custom-call(s32[2,8]{1,0:T(2,128)} %dynamic-slice_bitcast_fusion.info_ref, f32[40,512]{1,0:T(8,128)} %get-tuple-element.48.low_ref, bf16[272,1280]{1,0:T(8,128)(2,1)} %collective-permute-done.9.refs_0_.cw_ref, bf16[272,1280]{1,0:T(8,128)(2,1)} %collective-permute-done.10.refs_1_.ccw_ref, ...), custom_call_target="tpu_custom_call" | custom-call | flops 9200000000 | bytes 1000 | tf_op jit(solution)/shard_map/pallas_call | solution.py:260
  73.2 2.5 %collective-permute-start.11 = (bf16[256,1280]{1,0:T(8,128)(2,1)}, bf16[256,1280]{1,0:T(8,128)(2,1)}, u32[]{:S(2)}, u32[]{:S(2)}) collective-permute-start(bf16[256,1280]{1,0:T(8,128)(2,1)} %get-tuple-element.76), channel_id=1, source_target_pairs={{0,2},{2,4},{4,6},{6,7},{7,5},{5,3},{3,1},{1,0},{8,10},{10,12},{12... | collective-permute-start | bytes 1966088 | tf_op jit(solution)/shard_map/ppermute | solution.py:775
  75.7 12.6 %shard_map.110 = (f32[256,1024]{1,0:T(8,128)}, f32[256,1024]{1,0:T(8,128)}, f32[512,128]{1,0:T(8,128)}) custom-call(s32[2,8]{1,0:T(2,128)} %dynamic-slice_bitcast_fusion.info_ref, f32[40,512]{1,0:T(8,128)} %get-tuple-element.48.low_ref, f32[40,512]{1,0:T(8,128)} %collective-permute-done.8.opposite_ref, ...), custom_call_target="tpu_custom_call" | custom-call | flops 9200000000 | bytes 1000 | tf_op jit(solution)/shard_map/pallas_call | solution.py:515
  88.4 2.9 %shard_map.113 = (bf16[128,1536]{1,0:T(8,128)(2,1)}, bf16[128,1024]{1,0:T(8,128)(2,1)}) custom-call(s32[2,8]{1,0:T(2,128)} %dynamic-slice_bitcast_fusion.info_ref, bf16[256,1280]{1,0:T(8,128)(2,1)} %collective-permute-done.6.refs_0_.with_sums, bf16[256,1280]{1,0:T(8,128)(2,1)} %collective-permute-done.7.refs_1_.other.refs_6_, ...), custom_call_target="tpu_custom_call" | custom-call | flops 9200000000 | bytes 1000 | tf_op jit(solution)/shard_map/pallas_call | solution.py:294
  91.2 1.8 %collective-permute-start.13 = (bf16[128,1536]{1,0:T(8,128)(2,1)}, bf16[128,1536]{1,0:T(8,128)(2,1)}, u32[]{:S(2)}, u32[]{:S(2)}) collective-permute-start(bf16[128,1536]{1,0:T(8,128)(2,1)} %get-tuple-element.81), channel_id=1, source_target_pairs={{0,2},{2,4},{4,6},{6,7},{7,5},{5,3},{3,1},{1,0},{8,10},{10,12},{12... | collective-permute-start | bytes 1179656 | tf_op jit(solution)/shard_map/ppermute | solution.py:764
  93.3 6.9 %shard_map.111.total_a_ref = f32[256,1024]{1,0:T(8,128)} custom-call(s32[2,8]{1,0:T(2,128)} %dynamic-slice_bitcast_fusion.info_ref, bf16[256,1280]{1,0:T(8,128)(2,1)} %collective-permute-done.6.refs_0_.with_sums, bf16[256,1280]{1,0:T(8,128)(2,1)} %collective-permute-done.7.refs_1_.other.refs_6_, bf16[8192,1024]{1,0:T(8,128)(2,1)} %w_ref.5, ...), custom_call_target="tpu_custom_call" | custom-call | flops 9200000000 | bytes 1000 | tf_op jit(solution)/shard_map/pallas_call | solution.py:594
  100.2 2.9 %shard_map.114 = (bf16[128,1536]{1,0:T(8,128)(2,1)}, bf16[128,1024]{1,0:T(8,128)(2,1)}) custom-call(s32[2,8]{1,0:T(2,128)} %dynamic-slice_bitcast_fusion.info_ref, bf16[256,1280]{1,0:T(8,128)(2,1)} %collective-permute-done.12.refs_1_.with_sums, bf16[256,1280]{1,0:T(8,128)(2,1)} %collective-permute-done.11.refs_0_.other.refs_9_, ...), custom_call_target="tpu_custom_call" | custom-call | flops 9200000000 | bytes 1000 | tf_op jit(solution)/shard_map/pallas_call | solution.py:294
  103.7 2.3 %collective-permute-start.16 = (bf16[128,1024]{1,0:T(8,128)(2,1)}, bf16[128,1024]{1,0:T(8,128)(2,1)}, u32[]{:S(2)}, u32[]{:S(2)}) collective-permute-start(bf16[128,1024]{1,0:T(8,128)(2,1)} %get-tuple-element.84), channel_id=1, source_target_pairs={{0,2},{2,4},{4,6},{6,7},{7,5},{5,3},{3,1},{1,0},{8,10},{10,12},{12... | collective-permute-start | bytes 786440 | tf_op jit(solution)/shard_map/ppermute | solution.py:766
  106.0 6.8 %shard_map.112.total_b_ref = f32[256,1024]{1,0:T(8,128)} custom-call(s32[2,8]{1,0:T(2,128)} %dynamic-slice_bitcast_fusion.info_ref, bf16[256,1280]{1,0:T(8,128)(2,1)} %collective-permute-done.11.refs_0_.other.refs_9_, bf16[256,1280]{1,0:T(8,128)(2,1)} %collective-permute-done.12.refs_1_.with_sums, bf16[8192,1024]{1,0:T(8,128)(2,1)} %w_ref.5, ...), custom_call_target="tpu_custom_call" | custom-call | flops 9200000000 | bytes 1000 | tf_op jit(solution)/shard_map/pallas_call | solution.py:594
  113.6 7.5 %shard_map.115 = bf16[512,1024]{1,0:T(8,128)(2,1)} custom-call(s32[2,8]{1,0:T(2,128)} %dynamic-slice_bitcast_fusion.info_ref, s32[2]{0:T(128)} %lengths_ref.1, f32[256,1024]{1,0:T(8,128)} %shard_map.111.total_a_ref, f32[256,1024]{1,0:T(8,128)} %shard_map.112.total_b_ref, f32[512,128]{1,0:T(8,128)} %get-tuple-element.72.refs_4_.inv_ref, ...), custom_call_target="tpu_custom_call" | custom-call | bytes 1000 | tf_op jit(solution)/shard_map/pallas_call | solution.py:682
  (31 shorter events, 10.9 us)
Async XLA Ops:
  5.4 18.8 %collective-permute-start = (bf16[256,1280]{1,0:T(8,128)(2,1)}, bf16[256,1280]{1,0:T(8,128)(2,1)}, u32[]{:S(2)}, u32[]{:S(2)}) collective-permute-start(bf16[256,1280]{1,0:T(8,128)(2,1)} %get-tuple-element.45), channel_id=1, source_target_pairs={{0,2},{2,4},{4,6},{6,7},{7,5},{5,3},{3,1},{1,0},{8,10},{10,12},{12... | collective-permute-start | bytes 1966088 | tf_op jit(solution)/shard_map/ppermute | solution.py:739
  8.4 17.4 %collective-permute-start.1 = (bf16[256,1280]{1,0:T(8,128)(2,1)}, bf16[256,1280]{1,0:T(8,128)(2,1)}, u32[]{:S(2)}, u32[]{:S(2)}) collective-permute-start(bf16[256,1280]{1,0:T(8,128)(2,1)} %get-tuple-element.46), channel_id=1, source_target_pairs={{2,0},{4,2},{6,4},{7,6},{5,7},{3,5},{1,3},{0,1},{10,8},{12,10},{14... | collective-permute-start | bytes 1966088 | tf_op jit(solution)/shard_map/ppermute | solution.py:739
  19.9 22.2 %collective-permute-start.4 = (bf16[272,1280]{1,0:T(8,128)(2,1)}, bf16[272,1280]{1,0:T(8,128)(2,1)}, u32[]{:S(2)}, u32[]{:S(2)}) collective-permute-start(bf16[272,1280]{1,0:T(8,128)(2,1)} %get-tuple-element.53), channel_id=1, source_target_pairs={{0,2},{2,4},{4,6},{6,7},{7,5},{5,3},{3,1},{1,0},{8,10},{10,12},{12... | collective-permute-start | bytes 2088968 | tf_op jit(solution)/shard_map/ppermute | solution.py:743
  22.0 20.1 %collective-permute-start.5 = (bf16[272,1280]{1,0:T(8,128)(2,1)}, bf16[272,1280]{1,0:T(8,128)(2,1)}, u32[]{:S(2)}, u32[]{:S(2)}) collective-permute-start(bf16[272,1280]{1,0:T(8,128)(2,1)} %get-tuple-element.54), channel_id=1, source_target_pairs={{2,0},{4,2},{6,4},{7,6},{5,7},{3,5},{1,3},{0,1},{10,8},{12,10},{14... | collective-permute-start | bytes 2088968 | tf_op jit(solution)/shard_map/ppermute | solution.py:743
  29.2 28.3 %collective-permute-start.2 = (bf16[256,1280]{1,0:T(8,128)(2,1)}, bf16[256,1280]{1,0:T(8,128)(2,1)}, u32[]{:S(2)}, u32[]{:S(2)}) collective-permute-start(bf16[256,1280]{1,0:T(8,128)(2,1)} %get-tuple-element.51.refs_1_), channel_id=1, source_target_pairs={{0,2},{2,4},{4,6},{6,7},{7,5},{5,3},{3,1},{1,0},{8,10},{10,12},{12... | collective-permute-start | bytes 1966088 | tf_op jit(solution)/shard_map/ppermute | solution.py:775
  30.8 26.7 %collective-permute-start.3 = (bf16[256,1280]{1,0:T(8,128)(2,1)}, bf16[256,1280]{1,0:T(8,128)(2,1)}, u32[]{:S(2)}, u32[]{:S(2)}) collective-permute-start(bf16[256,1280]{1,0:T(8,128)(2,1)} %get-tuple-element.52.refs_2_), channel_id=1, source_target_pairs={{2,0},{4,2},{6,4},{7,6},{5,7},{3,5},{1,3},{0,1},{10,8},{12,10},{14... | collective-permute-start | bytes 1966088 | tf_op jit(solution)/shard_map/ppermute | solution.py:775
  46.2 23.7 %collective-permute-start.10 = (bf16[272,1280]{1,0:T(8,128)(2,1)}, bf16[272,1280]{1,0:T(8,128)(2,1)}, u32[]{:S(2)}, u32[]{:S(2)}) collective-permute-start(bf16[272,1280]{1,0:T(8,128)(2,1)} %get-tuple-element.60.refs_2_), channel_id=1, source_target_pairs={{2,0},{4,2},{6,4},{7,6},{5,7},{3,5},{1,3},{0,1},{10,8},{12,10},{14... | collective-permute-start | bytes 2088968 | tf_op jit(solution)/shard_map/ppermute | solution.py:775
  46.5 23.4 %collective-permute-start.9 = (bf16[272,1280]{1,0:T(8,128)(2,1)}, bf16[272,1280]{1,0:T(8,128)(2,1)}, u32[]{:S(2)}, u32[]{:S(2)}) collective-permute-start(bf16[272,1280]{1,0:T(8,128)(2,1)} %get-tuple-element.59.refs_1_), channel_id=1, source_target_pairs={{0,2},{2,4},{4,6},{6,7},{7,5},{5,3},{3,1},{1,0},{8,10},{10,12},{12... | collective-permute-start | bytes 2088968 | tf_op jit(solution)/shard_map/ppermute | solution.py:775
  48.2 25.0 %collective-permute-start.8 = (f32[40,512]{1,0:T(8,128)}, f32[40,512]{1,0:T(8,128)}, u32[]{:S(2)}, u32[]{:S(2)}) collective-permute-start(f32[40,512]{1,0:T(8,128)} %get-tuple-element.66), channel_id=1, source_target_pairs={{0,7},{2,5},{4,3},{6,1},{7,0},{5,2},{3,4},{1,6},{8,15},{10,13},{12... | collective-permute-start | bytes 245768 | tf_op jit(solution)/shard_map/ppermute | solution.py:781
  60.0 28.3 %collective-permute-start.6 = (bf16[256,1280]{1,0:T(8,128)(2,1)}, bf16[256,1280]{1,0:T(8,128)(2,1)}, u32[]{:S(2)}, u32[]{:S(2)}) collective-permute-start(bf16[256,1280]{1,0:T(8,128)(2,1)} %get-tuple-element.64.refs_0_), channel_id=1, source_target_pairs={{0,2},{2,4},{4,6},{6,7},{7,5},{5,3},{3,1},{1,0},{8,10},{10,12},{12... | collective-permute-start | bytes 1966088 | tf_op jit(solution)/shard_map/ppermute | solution.py:775
  60.0 28.3 %collective-permute-start.7 = (bf16[256,1280]{1,0:T(8,128)(2,1)}, bf16[256,1280]{1,0:T(8,128)(2,1)}, u32[]{:S(2)}, u32[]{:S(2)}) collective-permute-start(bf16[256,1280]{1,0:T(8,128)(2,1)} %get-tuple-element.65.refs_1_), channel_id=1, source_target_pairs={{2,0},{4,2},{6,4},{7,6},{5,7},{3,5},{1,3},{0,1},{10,8},{12,10},{14... | collective-permute-start | bytes 1966088 | tf_op jit(solution)/shard_map/ppermute | solution.py:775
  73.1 27.1 %collective-permute-start.12 = (bf16[256,1280]{1,0:T(8,128)(2,1)}, bf16[256,1280]{1,0:T(8,128)(2,1)}, u32[]{:S(2)}, u32[]{:S(2)}) collective-permute-start(bf16[256,1280]{1,0:T(8,128)(2,1)} %get-tuple-element.69), channel_id=1, source_target_pairs={{2,0},{4,2},{6,4},{7,6},{5,7},{3,5},{1,3},{0,1},{10,8},{12,10},{14... | collective-permute-start | bytes 1966088 | tf_op jit(solution)/shard_map/ppermute | solution.py:775
  73.2 26.9 %collective-permute-start.11 = (bf16[256,1280]{1,0:T(8,128)(2,1)}, bf16[256,1280]{1,0:T(8,128)(2,1)}, u32[]{:S(2)}, u32[]{:S(2)}) collective-permute-start(bf16[256,1280]{1,0:T(8,128)(2,1)} %get-tuple-element.76), channel_id=1, source_target_pairs={{0,2},{2,4},{4,6},{6,7},{7,5},{5,3},{3,1},{1,0},{8,10},{10,12},{12... | collective-permute-start | bytes 1966088 | tf_op jit(solution)/shard_map/ppermute | solution.py:775
  91.2 21.6 %collective-permute-start.13 = (bf16[128,1536]{1,0:T(8,128)(2,1)}, bf16[128,1536]{1,0:T(8,128)(2,1)}, u32[]{:S(2)}, u32[]{:S(2)}) collective-permute-start(bf16[128,1536]{1,0:T(8,128)(2,1)} %get-tuple-element.81), channel_id=1, source_target_pairs={{0,2},{2,4},{4,6},{6,7},{7,5},{5,3},{3,1},{1,0},{8,10},{10,12},{12... | collective-permute-start | bytes 1179656 | tf_op jit(solution)/shard_map/ppermute | solution.py:764
  93.0 19.8 %collective-permute-start.14 = (bf16[128,1024]{1,0:T(8,128)(2,1)}, bf16[128,1024]{1,0:T(8,128)(2,1)}, u32[]{:S(2)}, u32[]{:S(2)}) collective-permute-start(bf16[128,1024]{1,0:T(8,128)(2,1)} %get-tuple-element.82), channel_id=1, source_target_pairs={{2,0},{4,2},{6,4},{7,6},{5,7},{3,5},{1,3},{0,1},{10,8},{12,10},{14... | collective-permute-start | bytes 786440 | tf_op jit(solution)/shard_map/ppermute | solution.py:764
  103.1 10.5 %collective-permute-start.15 = (bf16[128,1536]{1,0:T(8,128)(2,1)}, bf16[128,1536]{1,0:T(8,128)(2,1)}, u32[]{:S(2)}, u32[]{:S(2)}) collective-permute-start(bf16[128,1536]{1,0:T(8,128)(2,1)} %get-tuple-element.83), channel_id=1, source_target_pairs={{2,0},{4,2},{6,4},{7,6},{5,7},{3,5},{1,3},{0,1},{10,8},{12,10},{14... | collective-permute-start | bytes 1179656 | tf_op jit(solution)/shard_map/ppermute | solution.py:766
  103.7 9.1 %collective-permute-start.16 = (bf16[128,1024]{1,0:T(8,128)(2,1)}, bf16[128,1024]{1,0:T(8,128)(2,1)}, u32[]{:S(2)}, u32[]{:S(2)}) collective-permute-start(bf16[128,1024]{1,0:T(8,128)(2,1)} %get-tuple-element.84), channel_id=1, source_target_pairs={{0,2},{2,4},{4,6},{6,7},{7,5},{5,3},{3,1},{1,0},{8,10},{10,12},{12... | collective-permute-start | bytes 786440 | tf_op jit(solution)/shard_map/ppermute | solution.py:766

commit v6 on v5

--- a/solution.py
+++ b/solution.py
@@ -270,26 +270,34 @@
     )(info, low, *messages, *operands)
 
 
+def last_shares(half, width):
+    groups = width // (2 * HEAD_WIDTH)
+    below = half // groups
+    return groups, below, max(16, (half - below) // 2)
+
+
 def last_kernel(half, ready, info_ref, with_sums, other, *refs):
     refs = list(refs)
     block = None if ready else refs.pop(0)
     term, first_ref, second_ref = refs
     width = second_ref.shape[1]
-    mid = half // 2
-    pair = 2 * HEAD_WIDTH
+    pair = 2 * HEAD_WIDTH
+    groups, below, share = last_shares(half, width)
     own = own_term(block, term)
     sums = (with_sums[:half, width:].astype(F32) + own).astype(BF16)
-    first_ref[:, :width] = with_sums[:mid, :width]
-    first_ref[:, width : width + pair] = sums[:mid]
-    first_ref[:, width + pair :] = sums[mid:]
-    second_ref[...] = other[mid:half, :width]
+    first_ref[:share, :] = with_sums[:share, :width]
+    for i in range(groups):
+        lanes = slice(i * pair, (i + 1) * pair)
+        first_ref[share:, lanes] = sums[i * below : (i + 1) * below]
+    second_ref[...] = other[share:half, :width]
 
 
 def last_messages(info, with_sums, other, away, packed, weight, terms, rows, piece):
     half = rows // 2
     width = weight.shape[0]
     pair = 2 * HEAD_WIDTH
-    out = (shape_of((half // 2, width + 2 * pair), BF16), shape_of((half // 2, width), BF16))
+    _, below, share = last_shares(half, width)
+    out = (shape_of((share + below, width), BF16), shape_of((half - share, width), BF16))
     operands, specs = term_specs(info, [away], packed, weight, terms, piece)
     return call(
         functools.partial(last_kernel, half, terms is not None),
@@ -431,7 +439,7 @@
 def delta_kernel(
     model_width, slots, info_ref, low_ref, opposite_ref, cw_ref, ccw_ref, total_a_ref, total_b_ref,
     weight_ref, side_ref, w_ref, out_a_ref, out_b_ref, inv_ref, co_ref, group_ref, ends, x_buf,
-    w_buf, sems,
+    w_buf, total_buf, sems,
 ):
     step = pl.program_id(0)
     tile = w_ref.shape[0]
@@ -443,7 +451,7 @@
         for i, ref in enumerate(messages)
     ]
     total_copies = [
-        pltpu.make_async_copy(ref, outs[i], sems.at[2 + i])
+        pltpu.make_async_copy(ref, total_buf.at[i], sems.at[2 + i])
         for i, ref in enumerate((total_a_ref, total_b_ref))
     ]
     row_copies = [
@@ -460,7 +468,7 @@
 
     @pl.when(step == 0)
     def _():
-        for copy in end_copies + total_copies + row_copies + weight_copies:
+        for copy in end_copies:
             copy.start()
         for k in range(2):
             group_ref[k] = chosen_group(side_ref[:, SIDE_INDEX + k : SIDE_INDEX + k + 1])
@@ -480,8 +488,9 @@
             value = fold(jnp.where(lane // ADAPTER_RANK == k, low, 0.0))
             co_ref[k] = value * inverse * side_ref[:, SIDE_MIX + k : SIDE_MIX + k + 1]
         for i in range(2):
-            total_copies[i].wait()
-            outs[i][...] = outs[i][...] * inverse[i * half : (i + 1) * half]
+            outs[i][...] = jnp.zeros_like(outs[i])
+        for copy in total_copies + row_copies + weight_copies:
+            copy.start()
 
     pieces = []
     for s in range(tile // LANES):
@@ -496,11 +505,13 @@
 
     @pl.when(step == pl.num_programs(0) - 1)
     def _():
+        for copy in total_copies + row_copies + weight_copies:
+            copy.wait()
+        out_a_ref[...] += total_buf[0] * inv_ref[:half, 0:1]
+        total = total_buf[1]
         for i in range(2):
-            row_copies[i].wait()
-            weight_copies[i].wait()
-            product = jnp.dot(x_buf[i], w_buf[i], preferred_element_type=F32)
-            out_b_ref[...] += product * inv_ref[half:, 0:1]
+            total += jnp.dot(x_buf[i], w_buf[i], preferred_element_type=F32)
+        out_b_ref[...] += total * inv_ref[half:, 0:1]
 
 
 def query_delta(info, low, opposite, messages, slots, totals, weight, side, up):
@@ -529,20 +540,20 @@
                 pltpu.VMEM((2, extra, full), BF16),
                 pltpu.VMEM((2, half, width), BF16),
                 pltpu.VMEM((2, width, columns), BF16),
+                pltpu.VMEM((2, half, columns), F32),
                 pltpu.SemaphoreType.DMA((8,)),
             ],
         ),
     )(info, low, opposite, *messages, *totals, weight, side, up)
 
 
-def product_kernel(slots, starts, has_total, has_inv, info_ref, *refs):
+def product_kernel(slots, starts, has_total, has_inv, place, info_ref, *refs):
     refs = list(refs)
     count = len(slots)
     blocks = [refs.pop(0) for _ in range(count)]
     weight = refs.pop(0)
-    total_ref = refs.pop(0) if has_total else None
-    inv_ref = refs.pop(0) if has_inv else None
-    out_ref, x_buf, w_buf, sems, total_sem = refs
+    late = [refs.pop(0) for _ in range(has_total + has_inv)]
+    out_ref, x_buf, w_buf, sems, late_sems, *late_bufs = refs
     depth, half, width = x_buf.shape
     columns = w_buf.shape[2]
     chunk = min(CHUNK, columns)
@@ -559,9 +570,13 @@
     for i in range(min(depth - 1, count)):
         for copy in copies(i):
             copy.start()
-    if has_total:
-        total_copy = pltpu.make_async_copy(total_ref, out_ref, total_sem)
-        total_copy.start()
+    if has_inv:
+        late[-1] = late[-1].at[pl.ds(place * half, half)]
+    late_copies = [
+        pltpu.make_async_copy(ref, late_bufs[i], late_sems.at[i]) for i, ref in enumerate(late)
+    ]
+    for copy in late_copies:
+        copy.start()
     for i in range(count):
         buf = i % depth
         if i + depth - 1 < count:
@@ -569,30 +584,39 @@
                 copy.start()
         for copy in copies(i):
             copy.wait()
-        if i == 0 and has_total:
-            total_copy.wait()
+        if i == count - 1:
+            for copy in late_copies:
+                copy.wait()
         for first in range(0, columns, chunk):
             span = slice(first, first + chunk)
             value = jnp.dot(x_buf[buf], w_buf[buf, :, span], preferred_element_type=F32)
-            if has_inv:
-                value = value * inv_ref[:, 0:1]
-            if i > 0 or has_total:
+            if i > 0:
                 value = out_ref[:, span] + value
+            if i == count - 1 and has_inv:
+                value = value * late_bufs[-1][:, 0:1]
+            if i == count - 1 and has_total:
+                value = late_bufs[0][:, span] + value
             out_ref[:, span] = value
 
 
 def product(info, total, sources, weight, half, inv=None, place=0):
     columns = weight.shape[1]
     width = weight.shape[0] // info.shape[1]
-    operands = [block for _, block, _ in sources] + [weight] + ([] if total is None else [total])
-    in_specs = [pl.BlockSpec(memory_space=pl.ANY)] * len(operands)
+    operands = [block for _, block, _ in sources] + [weight]
+    late = []
+    if total is not None:
+        operands.append(total)
+        late.append(pltpu.VMEM((half, columns), F32))
     if inv is not None:
         operands.append(inv)
-        in_specs.append(pl.BlockSpec((half, LANES), lambda j, info: (place, 0)))
+        late.append(pltpu.VMEM((half, LANES), F32))
+    in_specs = [pl.BlockSpec(memory_space=pl.ANY)] * len(operands)
     slots = [slot for slot, _, _ in sources]
     starts = [start for _, _, start in sources]
     return call(
-        functools.partial(product_kernel, slots, starts, total is not None, inv is not None),
+        functools.partial(
+            product_kernel, slots, starts, total is not None, inv is not None, place
+        ),
         shape_of((half, columns), F32),
         QUERY_WEIGHT,
         grid_spec=prefetch(
@@ -604,7 +628,8 @@
                 pltpu.VMEM((DEPTH, half, width), BF16),
                 pltpu.VMEM((DEPTH, width, columns), BF16),
                 pltpu.SemaphoreType.DMA((DEPTH, 2)),
-                pltpu.SemaphoreType.DMA,
+                pltpu.SemaphoreType.DMA((2,)),
+                *late,
             ],
         ),
     )(info, *operands)
@@ -620,21 +645,23 @@
     info_ref, lengths_ref, total_a_ref, total_b_ref, inv_ref, w_ref, cos_ref, sin_ref, own_ref,
     *refs,
 ):
-    parts, sums = refs[:4], refs[4:10]
-    out_ref, last_s, key_s, value_s, bias_s = refs[10:]
-    mid = parts[0].shape[0]
+    parts, others = refs[:4], refs[4:6]
+    out_ref, last_s, key_s, value_s, bias_s = refs[6:]
+    groups, below, share = last_shares(SLOT, last_s.shape[1])
 
     @pl.when(pl.program_id(0) == 0)
     def _():
         row = lax.broadcasted_iota(jnp.int32, (SLOT, SLOT), 0)
         col = lax.broadcasted_iota(jnp.int32, (SLOT, SLOT), 1)
-        for i, part in enumerate(parts):
-            last_s[i * mid : (i + 1) * mid, :] = part[...]
         for prompt in range(2):
             span = slice(prompt * SLOT, (prompt + 1) * SLOT)
-            first, second, other = sums[3 * prompt : 3 * prompt + 3]
-            pair = jnp.concatenate([first[...], second[...]], axis=0).astype(F32)
-            pair = pair + other[...].astype(F32) + own_ref[span, :].astype(F32)
+            first, second = parts[2 * prompt : 2 * prompt + 2]
+            last_s[prompt * SLOT : prompt * SLOT + share, :] = first[:share, :]
+            last_s[prompt * SLOT + share : (prompt + 1) * SLOT, :] = second[...]
+            wide = 2 * HEAD_WIDTH
+            sums = [first[share:, i * wide : (i + 1) * wide] for i in range(groups)]
+            pair = jnp.concatenate(sums, axis=0).astype(F32)
+            pair = pair + others[prompt][...].astype(F32) + own_ref[span, :].astype(F32)
             pair = pair * inv_ref[span, 0:1]
             key = rotate(pair[:, :HEAD_WIDTH], cos_ref[...], sin_ref[...])
             key_s[prompt] = key.astype(BF16)
@@ -669,16 +696,9 @@
     columns = weight.shape[1]
     tile = min(HEADS_AT_ONCE * HEAD_WIDTH, columns)
     pair = 2 * HEAD_WIDTH
-    mid = SLOT // 2
     tokens = 2 * SLOT
     rows_of = [part for first, second, _ in parts for part in (first, second)]
-    sums_of = [part for first, _, other in parts for part in (first, first, other)]
-    lane = width // pair
-    sums_specs = [
-        pl.BlockSpec((mid, pair), lambda j, *_: (0, lane)),
-        pl.BlockSpec((mid, pair), lambda j, *_: (0, lane + 1)),
-        pl.BlockSpec((SLOT, pair), lambda j, *_: (0, lane)),
-    ]
+    others = [other for _, _, other in parts]
     return call(
         attention_kernel,
         shape_of((tokens, columns), BF16),
@@ -694,8 +714,8 @@
                 whole((SLOT, HEAD_WIDTH)),
                 whole((tokens, pair)),
             ]
-            + [pl.BlockSpec((mid, width), lambda j, *_: (0, 0))] * 4
-            + sums_specs * 2,
+            + [whole(part.shape) for part in rows_of]
+            + [pl.BlockSpec((SLOT, pair), lambda j, *_: (0, width // pair))] * 2,
             pl.BlockSpec((tokens, tile), lambda j, *_: (0, j)),
             [
                 pltpu.VMEM((tokens, width), BF16),
@@ -704,7 +724,7 @@
                 pltpu.VMEM((2, SLOT, SLOT), F32),
             ],
         ),
-    )(info, lengths, *totals, inv, weight, *tables, own, *rows_of, *sums_of)
+    )(info, lengths, *totals, inv, weight, *tables, own, *rows_of, *others)
 
 
 def rotation_tables():

time: 122 us -> 121 us (level)
  Pallas kernels: 90.8 us -> 87.1 us
  waiting for transfers between devices: 5.3 us -> 7.63 us
    pallas_call x5, Pallas kernels: 30.9 us -> 27.1 us  [product(): call(functools.partial(product_kernel, slots, starts, total is not None,...]
    ppermute x8, waiting for transfers between devices: 2.01 us -> 3.58 us  [program(): from_cw[piece], from_ccw[piece] = (send_cw(moved[0]), send_ccw(moved[1]))]
  transfers between devices with their start and end apart: 17 -> 17, of which waited for: 4 -> 5; matrix products, arithmetic and copies ran while one was open for 1% -> 1% of each run, Pallas kernels for 65% -> 63%
where the time goes in v6:
time: 121 us; the launch traced here: 120 us
  Pallas kernels  87.1 us (72%)
  starting transfers between devices  22.7 us (19%)
  waiting for transfers between devices  7.63 us (6%)
  other arithmetic  1.28 us (1%)
  local copies, waits for them, and re-layouts  1.26 us (1%)
    pallas_call x5, Pallas kernels, product(): call(functools.partial(product_kernel, slots, starts, total is not None,...  27.1 us
    pallas_call x1, Pallas kernels, query_delta(): call(functools.partial(delta_kernel, weight.shape[0], slots), (shape_of((...  12.7 us
    pallas_call x1, Pallas kernels, low_partials(): call(functools.partial(low_kernel, (reach - 1, reach)), (shape_of((LOW_RO...  11.5 us
    ppermute x8, starting transfers between devices, program(): from_cw[piece], from_ccw[piece] = (send_cw(moved[0]), send_ccw(moved[1]))  8.73 us
    pallas_call x1, Pallas kernels, attention(): call(attention_kernel, shape_of((tokens, columns), BF16), grid_spec=prefe...  7.48 us
    pallas_call x2, Pallas kernels, add_terms_low(): call(functools.partial(add_low_kernel, half, terms is not None), out, ADD...  7.3 us
    pallas_call x2, Pallas kernels, add_terms(): call(functools.partial(add_kernel, terms is not None), (shape_of((half, f...  5.9 us
    pallas_call x2, Pallas kernels, last_messages(): call(functools.partial(last_kernel, half, terms is not None), out, ADD_WE...  5.79 us
  transfers between devices with their start and end apart: 17, of which 5 were waited for; matrix products, arithmetic and copies ran while one was open for 1% of the time, Pallas kernels for 63%

profile of v6, /device:TPU:0, one launch (start us, length us, event | category | flops | bytes accessed | tf_op | source)
XLA Modules:
  0.0 120.2 jit_solution(656969144826296188)
XLA Ops:
  1.3 4.1 %shard_map.100 = (bf16[256,1280]{1,0:T(8,128)(2,1)}, bf16[256,1280]{1,0:T(8,128)(2,1)}, bf16[512,1024]{1,0:T(8,128)(2,1)}) custom-call(s32[2,8]{1,0:T(2,128)} %dynamic-slice_bitcast_fusion.info_ref, bf16[512,1024]{1,0:T(8,128)(2,1)} %x_ref.3, f32[1,8192]{1,0:T(1,128)} %bitcast.5, bf16[1024,2048]{1,0:T(8,128)(2,1)} %refs_4_.3, bf16[1024,2048]{1,0:T(8,128)(2,1)} %refs_4_.3), custom_call_target="tpu_custom_call" | custom-call | bytes 1000 | tf_op jit(solution)/shard_map/pallas_call | solution.py:90
  5.4 3.0 %collective-permute-start = (bf16[256,1280]{1,0:T(8,128)(2,1)}, bf16[256,1280]{1,0:T(8,128)(2,1)}, u32[]{:S(2)}, u32[]{:S(2)}) collective-permute-start(bf16[256,1280]{1,0:T(8,128)(2,1)} %get-tuple-element.45), channel_id=1, source_target_pairs={{0,2},{2,4},{4,6},{6,7},{7,5},{5,3},{3,1},{1,0},{8,10},{10,12},{12... | collective-permute-start | bytes 1966088 | tf_op jit(solution)/shard_map/ppermute | solution.py:759
  8.4 11.5 %shard_map.101 = (f32[40,512]{1,0:T(8,128)}, f32[512,128]{1,0:T(8,128)}, bf16[272,1280]{1,0:T(8,128)(2,1)}, bf16[272,1280]{1,0:T(8,128)(2,1)}) custom-call(s32[2,8]{1,0:T(2,128)} %dynamic-slice_bitcast_fusion.info_ref, bf16[512,1024]{1,0:T(8,128)(2,1)} %get-tuple-element.55.packed_ref.refs_2_.refs_0_.x_ref, bf16[1024,4096]{1,0:T(8,128)(2,1)} %w_ref.3, ...), custom_call_target="tpu_custom_call" | custom-call | bytes 1000 | tf_op jit(solution)/shard_map/pallas_call | solution.py:409
  19.9 2.1 %collective-permute-start.4 = (bf16[272,1280]{1,0:T(8,128)(2,1)}, bf16[272,1280]{1,0:T(8,128)(2,1)}, u32[]{:S(2)}, u32[]{:S(2)}) collective-permute-start(bf16[272,1280]{1,0:T(8,128)(2,1)} %get-tuple-element.53), channel_id=1, source_target_pairs={{0,2},{2,4},{4,6},{6,7},{7,5},{5,3},{3,1},{1,0},{8,10},{10,12},{12... | collective-permute-start | bytes 2088968 | tf_op jit(solution)/shard_map/ppermute | solution.py:763
  25.8 3.3 %shard_map.102 = (bf16[256,1280]{1,0:T(8,128)(2,1)}, bf16[256,1280]{1,0:T(8,128)(2,1)}) custom-call(s32[2,8]{1,0:T(2,128)} %dynamic-slice_bitcast_fusion.info_ref, bf16[256,1280]{1,0:T(8,128)(2,1)} %collective-permute-done.refs_0_, bf16[256,1280]{1,0:T(8,128)(2,1)} %collective-permute-done.1.refs_1_, ...), custom_call_target="tpu_custom_call", output_to_operand_aliasing={{0}: (1, {}), {1}: (2, {})} | custom-call | flops 9200000000 | bytes 1000 | tf_op jit(solution)/shard_map/pallas_call | solution.py:225
  31.2 5.7 %shard_map.103.refs_3_ = f32[256,1024]{1,0:T(8,128)} custom-call(s32[2,8]{1,0:T(2,128)} %dynamic-slice_bitcast_fusion.info_ref, bf16[512,1024]{1,0:T(8,128)(2,1)} %get-tuple-element.55.packed_ref.refs_2_.refs_0_.x_ref, bf16[256,1280]{1,0:T(8,128)(2,1)} %get-tuple-element.51.refs_1_, bf16[256,1280]{1,0:T(8,128)(2,1)} %get-tuple-element.52.refs_2_, ...), custom_call_target="tpu_custom_call" | custom-call | flops 9200000000 | bytes 1000 | tf_op jit(solution)/shard_map/pallas_call | solution.py:616
  36.9 5.2 %shard_map.104 = (bf16[2,512,256]{2,1,0:T(8,128)(2,1)}, bf16[2,512,256]{2,1,0:T(8,128)(2,1)}, bf16[512,256]{1,0:T(8,128)(2,1)}) custom-call(s32[2,8]{1,0:T(2,128)} %dynamic-slice_bitcast_fusion.info_ref, bf16[512,1024]{1,0:T(8,128)(2,1)} %get-tuple-element.55.packed_ref.refs_2_.refs_0_.x_ref, bf16[1024,2048]{1,0:T(8,128)(2,1)} %refs_4_.3, ...), custom_call_target="tpu_custom_call" | custom-call | bytes 1000 | tf_op jit(solution)/shard_map/pallas_call | solution.py:166
  42.1 4.1 %shard_map.105 = (bf16[272,1280]{1,0:T(8,128)(2,1)}, bf16[272,1280]{1,0:T(8,128)(2,1)}, f32[40,512]{1,0:T(8,128)}) custom-call(s32[2,8]{1,0:T(2,128)} %dynamic-slice_bitcast_fusion.info_ref, f32[40,512]{1,0:T(8,128)} %get-tuple-element.48.low_ref, bf16[272,1280]{1,0:T(8,128)(2,1)} %collective-permute-done.4.refs_0_, ...), custom_call_target="tpu_custom_call" | custom-call | flops 9200000000 | bytes 1000 | tf_op jit(solution)/shard_map/pallas_call | solution.py:260
  48.2 3.5 %collective-permute-start.8 = (f32[40,512]{1,0:T(8,128)}, f32[40,512]{1,0:T(8,128)}, u32[]{:S(2)}, u32[]{:S(2)}) collective-permute-start(f32[40,512]{1,0:T(8,128)} %get-tuple-element.66), channel_id=1, source_target_pairs={{0,7},{2,5},{4,3},{6,1},{7,0},{5,2},{3,4},{1,6},{8,15},{10,13},{12... | collective-permute-start | bytes 245768 | tf_op jit(solution)/shard_map/ppermute | solution.py:801
  51.7 5.7 %shard_map.106.total_b_ref = f32[256,1024]{1,0:T(8,128)} custom-call(s32[2,8]{1,0:T(2,128)} %dynamic-slice_bitcast_fusion.info_ref, bf16[512,1024]{1,0:T(8,128)(2,1)} %get-tuple-element.55.packed_ref.refs_2_.refs_0_.x_ref, bf16[272,1280]{1,0:T(8,128)(2,1)} %get-tuple-element.59.refs_1_, bf16[272,1280]{1,0:T(8,128)(2,1)} %get-tuple-element.60.refs_2_, ...), custom_call_target="tpu_custom_call" | custom-call | flops 9200000000 | bytes 1000 | tf_op jit(solution)/shard_map/pallas_call | solution.py:616
  57.5 2.6 %shard_map.107 = (bf16[256,1280]{1,0:T(8,128)(2,1)}, bf16[256,1280]{1,0:T(8,128)(2,1)}) custom-call(s32[2,8]{1,0:T(2,128)} %dynamic-slice_bitcast_fusion.info_ref, bf16[256,1280]{1,0:T(8,128)(2,1)} %collective-permute-done.2.refs_0_, bf16[256,1280]{1,0:T(8,128)(2,1)} %collective-permute-done.3.refs_1_, ...), custom_call_target="tpu_custom_call", output_to_operand_aliasing={{0}: (1, {}), {1}: (2, {})} | custom-call | flops 9200000000 | bytes 1000 | tf_op jit(solution)/shard_map/pallas_call | solution.py:225
  60.1 2.0 %collective-permute-start.7 = (bf16[256,1280]{1,0:T(8,128)(2,1)}, bf16[256,1280]{1,0:T(8,128)(2,1)}, u32[]{:S(2)}, u32[]{:S(2)}) collective-permute-start(bf16[256,1280]{1,0:T(8,128)(2,1)} %get-tuple-element.65.refs_1_), channel_id=1, source_target_pairs={{2,0},{4,2},{6,4},{7,6},{5,7},{3,5},{1,3},{0,1},{10,8},{12,10},{14... | collective-permute-start | bytes 1966088 | tf_op jit(solution)/shard_map/ppermute | solution.py:795
  62.1 5.2 %shard_map.108.total_a_ref = f32[256,1024]{1,0:T(8,128)} custom-call(s32[2,8]{1,0:T(2,128)} %dynamic-slice_bitcast_fusion.info_ref, bf16[256,1280]{1,0:T(8,128)(2,1)} %get-tuple-element.64.refs_0_, bf16[256,1280]{1,0:T(8,128)(2,1)} %get-tuple-element.65.refs_1_, bf16[8192,1024]{1,0:T(8,128)(2,1)} %w_ref.5, f32[256,1024]{1,0:T(8,128)} %shard_map.103.refs_3_), custom_call_target="tpu_custom_call" | custom-call | flops 9200000000 | bytes 1000 | tf_op jit(solution)/shard_map/pallas_call | solution.py:616
  67.3 2.6 %collective-permute-done.10.refs_1_.ccw_ref = bf16[272,1280]{1,0:T(8,128)(2,1)} collective-permute-done((bf16[272,1280]{1,0:T(8,128)(2,1)}, bf16[272,1280]{1,0:T(8,128)(2,1)}, u32[]{:S(2)}, u32[]{:S(2)}) %collective-permute-start.10) | collective-permute-done | bytes 696352 | tf_op jit(solution)/shard_map/ppermute | solution.py:795
  69.9 3.2 %shard_map.109 = (bf16[256,1280]{1,0:T(8,128)(2,1)}, bf16[256,1280]{1,0:T(8,128)(2,1)}) custom-call(s32[2,8]{1,0:T(2,128)} %dynamic-slice_bitcast_fusion.info_ref, f32[40,512]{1,0:T(8,128)} %get-tuple-element.48.low_ref, bf16[272,1280]{1,0:T(8,128)(2,1)} %collective-permute-done.9.refs_0_.cw_ref, bf16[272,1280]{1,0:T(8,128)(2,1)} %collective-permute-done.10.refs_1_.ccw_ref, ...), custom_call_target="tpu_custom_call" | custom-call | flops 9200000000 | bytes 1000 | tf_op jit(solution)/shard_map/pallas_call | solution.py:260
  73.2 2.5 %collective-permute-start.11 = (bf16[256,1280]{1,0:T(8,128)(2,1)}, bf16[256,1280]{1,0:T(8,128)(2,1)}, u32[]{:S(2)}, u32[]{:S(2)}) collective-permute-start(bf16[256,1280]{1,0:T(8,128)(2,1)} %get-tuple-element.76), channel_id=1, source_target_pairs={{0,2},{2,4},{4,6},{6,7},{7,5},{5,3},{3,1},{1,0},{8,10},{10,12},{12... | collective-permute-start | bytes 1966088 | tf_op jit(solution)/shard_map/ppermute | solution.py:795
  75.7 12.7 %shard_map.110 = (f32[256,1024]{1,0:T(8,128)}, f32[256,1024]{1,0:T(8,128)}, f32[512,128]{1,0:T(8,128)}) custom-call(s32[2,8]{1,0:T(2,128)} %dynamic-slice_bitcast_fusion.info_ref, f32[40,512]{1,0:T(8,128)} %get-tuple-element.48.low_ref, f32[40,512]{1,0:T(8,128)} %collective-permute-done.8.opposite_ref, ...), custom_call_target="tpu_custom_call" | custom-call | flops 9200000000 | bytes 1000 | tf_op jit(solution)/shard_map/pallas_call | solution.py:526
  88.5 2.9 %shard_map.113 = (bf16[160,1024]{1,0:T(8,128)(2,1)}, bf16[160,1024]{1,0:T(8,128)(2,1)}) custom-call(s32[2,8]{1,0:T(2,128)} %dynamic-slice_bitcast_fusion.info_ref, bf16[256,1280]{1,0:T(8,128)(2,1)} %collective-permute-done.6.refs_0_.with_sums, bf16[256,1280]{1,0:T(8,128)(2,1)} %collective-permute-done.7.refs_1_.other.refs_4_, ...), custom_call_target="tpu_custom_call" | custom-call | flops 9200000000 | bytes 1000 | tf_op jit(solution)/shard_map/pallas_call | solution.py:302
  91.4 1.8 %collective-permute-start.13 = (bf16[160,1024]{1,0:T(8,128)(2,1)}, bf16[160,1024]{1,0:T(8,128)(2,1)}, u32[]{:S(2)}, u32[]{:S(2)}) collective-permute-start(bf16[160,1024]{1,0:T(8,128)(2,1)} %get-tuple-element.81), channel_id=1, source_target_pairs={{0,2},{2,4},{4,6},{6,7},{7,5},{5,3},{3,1},{1,0},{8,10},{10,12},{12... | collective-permute-start | bytes 983048 | tf_op jit(solution)/shard_map/ppermute | solution.py:784
  93.4 5.2 %shard_map.111.total_a_ref = f32[256,1024]{1,0:T(8,128)} custom-call(s32[2,8]{1,0:T(2,128)} %dynamic-slice_bitcast_fusion.info_ref, bf16[256,1280]{1,0:T(8,128)(2,1)} %collective-permute-done.6.refs_0_.with_sums, bf16[256,1280]{1,0:T(8,128)(2,1)} %collective-permute-done.7.refs_1_.other.refs_4_, bf16[8192,1024]{1,0:T(8,128)(2,1)} %w_ref.5, ...), custom_call_target="tpu_custom_call" | custom-call | flops 9200000000 | bytes 1000 | tf_op jit(solution)/shard_map/pallas_call | solution.py:616
  99.7 2.9 %shard_map.114 = (bf16[160,1024]{1,0:T(8,128)(2,1)}, bf16[160,1024]{1,0:T(8,128)(2,1)}) custom-call(s32[2,8]{1,0:T(2,128)} %dynamic-slice_bitcast_fusion.info_ref, bf16[256,1280]{1,0:T(8,128)(2,1)} %collective-permute-done.12.refs_1_.with_sums, bf16[256,1280]{1,0:T(8,128)(2,1)} %collective-permute-done.11.refs_0_.other.refs_5_, ...), custom_call_target="tpu_custom_call" | custom-call | flops 9200000000 | bytes 1000 | tf_op jit(solution)/shard_map/pallas_call | solution.py:302
  102.8 3.2 %collective-permute-start.16 = (bf16[160,1024]{1,0:T(8,128)(2,1)}, bf16[160,1024]{1,0:T(8,128)(2,1)}, u32[]{:S(2)}, u32[]{:S(2)}) collective-permute-start(bf16[160,1024]{1,0:T(8,128)(2,1)} %get-tuple-element.84), channel_id=1, source_target_pairs={{0,2},{2,4},{4,6},{6,7},{7,5},{5,3},{3,1},{1,0},{8,10},{10,12},{12... | collective-permute-start | bytes 983048 | tf_op jit(solution)/shard_map/ppermute | solution.py:786
  105.9 5.2 %shard_map.112.total_b_ref = f32[256,1024]{1,0:T(8,128)} custom-call(s32[2,8]{1,0:T(2,128)} %dynamic-slice_bitcast_fusion.info_ref, bf16[256,1280]{1,0:T(8,128)(2,1)} %collective-permute-done.11.refs_0_.other.refs_5_, bf16[256,1280]{1,0:T(8,128)(2,1)} %collective-permute-done.12.refs_1_.with_sums, bf16[8192,1024]{1,0:T(8,128)(2,1)} %w_ref.5, ...), custom_call_target="tpu_custom_call" | custom-call | flops 9200000000 | bytes 1000 | tf_op jit(solution)/shard_map/pallas_call | solution.py:616
  112.7 7.5 %shard_map.115 = bf16[512,1024]{1,0:T(8,128)(2,1)} custom-call(s32[2,8]{1,0:T(2,128)} %dynamic-slice_bitcast_fusion.info_ref, s32[2]{0:T(128)} %lengths_ref.1, f32[256,1024]{1,0:T(8,128)} %shard_map.111.total_a_ref, f32[256,1024]{1,0:T(8,128)} %shard_map.112.total_b_ref, f32[512,128]{1,0:T(8,128)} %get-tuple-element.72.refs_4_.inv_ref, ...), custom_call_target="tpu_custom_call" | custom-call | bytes 1000 | tf_op jit(solution)/shard_map/pallas_call | solution.py:702
  (31 shorter events, 12.2 us)
Async XLA Ops:
  5.4 18.8 %collective-permute-start = (bf16[256,1280]{1,0:T(8,128)(2,1)}, bf16[256,1280]{1,0:T(8,128)(2,1)}, u32[]{:S(2)}, u32[]{:S(2)}) collective-permute-start(bf16[256,1280]{1,0:T(8,128)(2,1)} %get-tuple-element.45), channel_id=1, source_target_pairs={{0,2},{2,4},{4,6},{6,7},{7,5},{5,3},{3,1},{1,0},{8,10},{10,12},{12... | collective-permute-start | bytes 1966088 | tf_op jit(solution)/shard_map/ppermute | solution.py:759
  8.4 17.4 %collective-permute-start.1 = (bf16[256,1280]{1,0:T(8,128)(2,1)}, bf16[256,1280]{1,0:T(8,128)(2,1)}, u32[]{:S(2)}, u32[]{:S(2)}) collective-permute-start(bf16[256,1280]{1,0:T(8,128)(2,1)} %get-tuple-element.46), channel_id=1, source_target_pairs={{2,0},{4,2},{6,4},{7,6},{5,7},{3,5},{1,3},{0,1},{10,8},{12,10},{14... | collective-permute-start | bytes 1966088 | tf_op jit(solution)/shard_map/ppermute | solution.py:759
  19.9 22.2 %collective-permute-start.4 = (bf16[272,1280]{1,0:T(8,128)(2,1)}, bf16[272,1280]{1,0:T(8,128)(2,1)}, u32[]{:S(2)}, u32[]{:S(2)}) collective-permute-start(bf16[272,1280]{1,0:T(8,128)(2,1)} %get-tuple-element.53), channel_id=1, source_target_pairs={{0,2},{2,4},{4,6},{6,7},{7,5},{5,3},{3,1},{1,0},{8,10},{10,12},{12... | collective-permute-start | bytes 2088968 | tf_op jit(solution)/shard_map/ppermute | solution.py:763
  22.0 20.1 %collective-permute-start.5 = (bf16[272,1280]{1,0:T(8,128)(2,1)}, bf16[272,1280]{1,0:T(8,128)(2,1)}, u32[]{:S(2)}, u32[]{:S(2)}) collective-permute-start(bf16[272,1280]{1,0:T(8,128)(2,1)} %get-tuple-element.54), channel_id=1, source_target_pairs={{2,0},{4,2},{6,4},{7,6},{5,7},{3,5},{1,3},{0,1},{10,8},{12,10},{14... | collective-permute-start | bytes 2088968 | tf_op jit(solution)/shard_map/ppermute | solution.py:763
  29.2 28.3 %collective-permute-start.2 = (bf16[256,1280]{1,0:T(8,128)(2,1)}, bf16[256,1280]{1,0:T(8,128)(2,1)}, u32[]{:S(2)}, u32[]{:S(2)}) collective-permute-start(bf16[256,1280]{1,0:T(8,128)(2,1)} %get-tuple-element.51.refs_1_), channel_id=1, source_target_pairs={{0,2},{2,4},{4,6},{6,7},{7,5},{5,3},{3,1},{1,0},{8,10},{10,12},{12... | collective-permute-start | bytes 1966088 | tf_op jit(solution)/shard_map/ppermute | solution.py:795
  30.8 26.7 %collective-permute-start.3 = (bf16[256,1280]{1,0:T(8,128)(2,1)}, bf16[256,1280]{1,0:T(8,128)(2,1)}, u32[]{:S(2)}, u32[]{:S(2)}) collective-permute-start(bf16[256,1280]{1,0:T(8,128)(2,1)} %get-tuple-element.52.refs_2_), channel_id=1, source_target_pairs={{2,0},{4,2},{6,4},{7,6},{5,7},{3,5},{1,3},{0,1},{10,8},{12,10},{14... | collective-permute-start | bytes 1966088 | tf_op jit(solution)/shard_map/ppermute | solution.py:795
  46.2 23.7 %collective-permute-start.10 = (bf16[272,1280]{1,0:T(8,128)(2,1)}, bf16[272,1280]{1,0:T(8,128)(2,1)}, u32[]{:S(2)}, u32[]{:S(2)}) collective-permute-start(bf16[272,1280]{1,0:T(8,128)(2,1)} %get-tuple-element.60.refs_2_), channel_id=1, source_target_pairs={{2,0},{4,2},{6,4},{7,6},{5,7},{3,5},{1,3},{0,1},{10,8},{12,10},{14... | collective-permute-start | bytes 2088968 | tf_op jit(solution)/shard_map/ppermute | solution.py:795
  46.5 23.4 %collective-permute-start.9 = (bf16[272,1280]{1,0:T(8,128)(2,1)}, bf16[272,1280]{1,0:T(8,128)(2,1)}, u32[]{:S(2)}, u32[]{:S(2)}) collective-permute-start(bf16[272,1280]{1,0:T(8,128)(2,1)} %get-tuple-element.59.refs_1_), channel_id=1, source_target_pairs={{0,2},{2,4},{4,6},{6,7},{7,5},{5,3},{3,1},{1,0},{8,10},{10,12},{12... | collective-permute-start | bytes 2088968 | tf_op jit(solution)/shard_map/ppermute | solution.py:795
  48.2 25.0 %collective-permute-start.8 = (f32[40,512]{1,0:T(8,128)}, f32[40,512]{1,0:T(8,128)}, u32[]{:S(2)}, u32[]{:S(2)}) collective-permute-start(f32[40,512]{1,0:T(8,128)} %get-tuple-element.66), channel_id=1, source_target_pairs={{0,7},{2,5},{4,3},{6,1},{7,0},{5,2},{3,4},{1,6},{8,15},{10,13},{12... | collective-permute-start | bytes 245768 | tf_op jit(solution)/shard_map/ppermute | solution.py:801
  60.0 28.4 %collective-permute-start.6 = (bf16[256,1280]{1,0:T(8,128)(2,1)}, bf16[256,1280]{1,0:T(8,128)(2,1)}, u32[]{:S(2)}, u32[]{:S(2)}) collective-permute-start(bf16[256,1280]{1,0:T(8,128)(2,1)} %get-tuple-element.64.refs_0_), channel_id=1, source_target_pairs={{0,2},{2,4},{4,6},{6,7},{7,5},{5,3},{3,1},{1,0},{8,10},{10,12},{12... | collective-permute-start | bytes 1966088 | tf_op jit(solution)/shard_map/ppermute | solution.py:795
  60.1 28.5 %collective-permute-start.7 = (bf16[256,1280]{1,0:T(8,128)(2,1)}, bf16[256,1280]{1,0:T(8,128)(2,1)}, u32[]{:S(2)}, u32[]{:S(2)}) collective-permute-start(bf16[256,1280]{1,0:T(8,128)(2,1)} %get-tuple-element.65.refs_1_), channel_id=1, source_target_pairs={{2,0},{4,2},{6,4},{7,6},{5,7},{3,5},{1,3},{0,1},{10,8},{12,10},{14... | collective-permute-start | bytes 1966088 | tf_op jit(solution)/shard_map/ppermute | solution.py:795
  73.1 26.6 %collective-permute-start.12 = (bf16[256,1280]{1,0:T(8,128)(2,1)}, bf16[256,1280]{1,0:T(8,128)(2,1)}, u32[]{:S(2)}, u32[]{:S(2)}) collective-permute-start(bf16[256,1280]{1,0:T(8,128)(2,1)} %get-tuple-element.69), channel_id=1, source_target_pairs={{2,0},{4,2},{6,4},{7,6},{5,7},{3,5},{1,3},{0,1},{10,8},{12,10},{14... | collective-permute-start | bytes 1966088 | tf_op jit(solution)/shard_map/ppermute | solution.py:795
  73.2 25.4 %collective-permute-start.11 = (bf16[256,1280]{1,0:T(8,128)(2,1)}, bf16[256,1280]{1,0:T(8,128)(2,1)}, u32[]{:S(2)}, u32[]{:S(2)}) collective-permute-start(bf16[256,1280]{1,0:T(8,128)(2,1)} %get-tuple-element.76), channel_id=1, source_target_pairs={{0,2},{2,4},{4,6},{6,7},{7,5},{5,3},{3,1},{1,0},{8,10},{10,12},{12... | collective-permute-start | bytes 1966088 | tf_op jit(solution)/shard_map/ppermute | solution.py:795
  91.4 19.8 %collective-permute-start.13 = (bf16[160,1024]{1,0:T(8,128)(2,1)}, bf16[160,1024]{1,0:T(8,128)(2,1)}, u32[]{:S(2)}, u32[]{:S(2)}) collective-permute-start(bf16[160,1024]{1,0:T(8,128)(2,1)} %get-tuple-element.81), channel_id=1, source_target_pairs={{0,2},{2,4},{4,6},{6,7},{7,5},{5,3},{3,1},{1,0},{8,10},{10,12},{12... | collective-permute-start | bytes 983048 | tf_op jit(solution)/shard_map/ppermute | solution.py:784
  93.2 18.0 %collective-permute-start.14 = (bf16[160,1024]{1,0:T(8,128)(2,1)}, bf16[160,1024]{1,0:T(8,128)(2,1)}, u32[]{:S(2)}, u32[]{:S(2)}) collective-permute-start(bf16[160,1024]{1,0:T(8,128)(2,1)} %get-tuple-element.82), channel_id=1, source_target_pairs={{2,0},{4,2},{6,4},{7,6},{5,7},{3,5},{1,3},{0,1},{10,8},{12,10},{14... | collective-permute-start | bytes 983048 | tf_op jit(solution)/shard_map/ppermute | solution.py:784
  102.6 10.1 %collective-permute-start.15 = (bf16[160,1024]{1,0:T(8,128)(2,1)}, bf16[160,1024]{1,0:T(8,128)(2,1)}, u32[]{:S(2)}, u32[]{:S(2)}) collective-permute-start(bf16[160,1024]{1,0:T(8,128)(2,1)} %get-tuple-element.83), channel_id=1, source_target_pairs={{2,0},{4,2},{6,4},{7,6},{5,7},{3,5},{1,3},{0,1},{10,8},{12,10},{14... | collective-permute-start | bytes 983048 | tf_op jit(solution)/shard_map/ppermute | solution.py:786
  102.8 9.9 %collective-permute-start.16 = (bf16[160,1024]{1,0:T(8,128)(2,1)}, bf16[160,1024]{1,0:T(8,128)(2,1)}, u32[]{:S(2)}, u32[]{:S(2)}) collective-permute-start(bf16[160,1024]{1,0:T(8,128)(2,1)} %get-tuple-element.84), channel_id=1, source_target_pairs={{0,2},{2,4},{4,6},{6,7},{7,5},{5,3},{3,1},{1,0},{8,10},{10,12},{12... | collective-permute-start | bytes 983048 | tf_op jit(solution)/shard_map/ppermute | solution.py:786
